TPU v7x, 32 devices: a whole 2x2x4 slice. The times are simulated.
32 devices in a mesh: grp: 2 (over x), blk: 16 (over z, y, core).
Axes of the slice: x: 2, y: 2, z: 4, core: 2. Of those that a mesh axis runs over, the one named last changes fastest.
Arguments:
- probes: float32 [3, 192, 64, 256], P(None, ('grp', 'blk')), parts along dimension 1, may hold values from -6 to 6
- inverses: float32 [3, 192, 256, 256], P(None, ('grp', 'blk')), parts along dimension 1
- couplings: float32 [2, 192, 4, 256, 256], P(None, ('grp', 'blk')), parts along dimension 1, may hold values from -0.1875 to 0.1875
- neighbour_devices: int32 [2, 192, 4], P(None, 'grp'), parts along dimension 1, may hold values from 0 to 15, all different within a row; in each aligned block of 6 rows (0 to 5, 6 to 11, ..., all dimensions but the last counted through in order) at most 2 rows name the same one
- neighbour_slots: int32 [2, 192, 4], P(None, 'grp'), parts along dimension 1, may hold values from 0 to 5
Outputs:
- solved: float32 [3, 192, 64, 256], P(None, ('grp', 'blk')), parts along dimension 1
There are 2 independent parts, one for each index of `grp`. A program takes and returns all parts, laid end to end along the dimension named above; each array names one. Nothing has to cross between parts.
Inputs may be any that keep to these rules, and one draw needn't show every extreme that they name: `neighbour_devices`: each list names 4 different devices. In each level, the lists of one device's 6 blocks (aligned blocks of 6 rows) name no device more than 2 times, and some device exactly 2 times.
All inputs are finite; a program needn't handle non-finite values.
Results may differ from a plain program's by a relative error of at most 0.0001.
Values sent between devices are 32-bit elements; how exact they have to be, the bound alone decides.
No kernel may reach another device: no remote copies, remote signals or barrier semaphores. Data moves between devices by JAX's collectives and lax.ppermute only.
A program may use at most 128 MiB of HBM per device.

v0:
```python
import jax
import jax.numpy as jnp
from jax import lax
from jax.sharding import PartitionSpec as P

LEVELS = 3
CAP = 2


def solve_right(panel, inverse):
    return jnp.einsum("bpi,bji->bpj", panel, inverse, precision=lax.Precision.HIGHEST)


def solve_left(panel, inverse):
    return jnp.einsum("bpj,bji->bpi", panel, inverse, precision=lax.Precision.HIGHEST)


def tables(dev_rows, slot_rows, members, position):
    fanout = dev_rows.shape[1]
    blocks_dev = dev_rows.shape[0] // members
    width_all = blocks_dev * fanout
    readers = dev_rows.reshape(members, width_all)
    slot_lists = slot_rows.reshape(members, width_all)
    positions = jnp.arange(width_all)
    earlier = positions[None, :] < positions[:, None]
    matches = readers[:, :, None] == readers[:, None, :]
    order_rank = jnp.sum(jnp.logical_and(matches, earlier[None]), axis=2)
    own_dev = lax.dynamic_index_in_dim(readers, position, 0, keepdims=False)
    own_rank = lax.dynamic_index_in_dim(order_rank, position, 0, keepdims=False)
    own_slot = lax.dynamic_index_in_dim(slot_lists, position, 0, keepdims=False)
    to_me = readers == position
    selected = jnp.logical_and(
        to_me[:, None, :], order_rank[:, None, :] == jnp.arange(CAP)[None, :, None]
    )
    send_rows = jnp.sum(jnp.where(selected, slot_lists[:, None, :], 0), axis=2)
    filled = jnp.any(selected, axis=2)
    return (own_dev, own_rank, own_slot, send_rows, filled)


def local(probes, inverses, couplings, neighbour_devices, neighbour_slots):
    members = lax.axis_size("blk")
    position = lax.axis_index("blk")
    blocks_dev = probes.shape[1]
    probe_count = probes.shape[2]
    points = probes.shape[3]
    fanout = couplings.shape[2]
    forward = [solve_right(probes[0], inverses[0])]
    routing = []
    for height in range(1, LEVELS):
        own_dev, own_rank, own_slot, send_rows, filled = tables(
            neighbour_devices[height - 1], neighbour_slots[height - 1], members, position
        )
        routing.append((own_dev, own_rank, own_slot, send_rows, filled))
        outgoing = forward[-1][send_rows]
        incoming = lax.all_to_all(outgoing, "blk", split_axis=0, concat_axis=0, tiled=True)
        fetched = incoming.reshape(members * CAP, probe_count, points)[own_dev * CAP + own_rank]
        fetched = fetched.reshape(blocks_dev, fanout, probe_count, points)
        coupled = jnp.einsum(
            "bkpi,bkji->bpj", fetched, couplings[height - 1], precision=lax.Precision.HIGHEST
        )
        forward.append(solve_right(probes[height] - coupled, inverses[height]))
    solved = [None] * LEVELS
    solved[LEVELS - 1] = solve_left(forward[LEVELS - 1], inverses[LEVELS - 1])
    for height in range(LEVELS - 2, -1, -1):
        own_dev, own_rank, own_slot, send_rows, filled = routing[height]
        partials = jnp.einsum(
            "bpj,bkji->bkpi", solved[height + 1], couplings[height], precision=lax.Precision.HIGHEST
        )
        partials = partials.reshape(blocks_dev * fanout, probe_count * points)
        target = own_dev * blocks_dev + own_slot
        row_ids = jnp.arange(blocks_dev * lax.axis_size("blk"))
        selector = (row_ids[:, None] == target[None, :]).astype(jnp.float32)
        summed = jnp.dot(selector, partials, precision=lax.Precision.HIGHEST)
        incoming_sum = lax.psum_scatter(
            summed.reshape(blocks_dev * lax.axis_size("blk"), probe_count, points),
            "blk",
            scatter_dimension=0,
            tiled=True,
        )
        solved[height] = solve_left(forward[height] - incoming_sum, inverses[height])
    return jnp.stack(solved)


def solution(mesh):
    return jax.shard_map(
        local,
        mesh=mesh,
        in_specs=(
            P(None, ("grp", "blk"), None, None),
            P(None, ("grp", "blk"), None, None),
            P(None, ("grp", "blk"), None, None, None),
            P(None, "grp", None),
            P(None, "grp", None),
        ),
        out_specs=P(None, ("grp", "blk"), None, None),
        check_vma=False,
    )
```

profile of v0, /device:TPU:0, one launch (start us, length us, event | category | flops | bytes accessed | tf_op | source)
XLA Modules:
  0.0 370.2 jit_solution(8559819483927968182)
XLA Ops:
  6.5 0.7 fusion.76
  7.2 0.7 fusion.75
  7.9 0.1 copy.26
  8.1 0.1 copy.22
  8.7 0.7 convert_reduce_fusion
  9.5 0.2 select_reduce_fusion
  9.8 3.1 fusion.28
  12.9 2.0 gather_fusion
  15.0 7.4 %all-to-all-start = ((f32[16,2,64,256]{3,2,1,0:T(8,128)}), f32[16,2,64,256]{3,2,1,0:T(8,128)S(1)}, u32[]{:S(2)}, u32[]{:S(2)}) async-start(f32[16,2,64,256]{3,2,1,0:T(8,128)} %bitcast.6), calls=%async_computation | async-start | bytes 4194304 | tf_op jit(solution)/shard_map/all_to_all | solution.py:55
  22.6 40.9 %all-to-all-done = f32[16,2,64,256]{3,2,1,0:T(8,128)S(1)} async-done(((f32[16,2,64,256]{3,2,1,0:T(8,128)}), f32[16,2,64,256]{3,2,1,0:T(8,128)S(1)}, u32[]{:S(2)}, u32[]{:S(2)}) %all-to-all-start) | async-done | bytes 2097184 | tf_op jit(solution)/shard_map/all_to_all | solution.py:55
  63.5 1.8 gather_fusion.1
  65.3 9.4 %fusion.48 = f32[6,64,256]{2,1,0:T(8,128)S(1)} fusion(f32[6,4,64,256]{3,2,1,0:T(8,128)} %bitcast.139, f32[2,6,4,256,256]{4,3,2,1,0:T(8,128)} %param.7, f32[3,6,64,256]{3,2,1,0:T(8,128)} %param.5), kind=kOutput, calls=%fused_computation.44 | convolution fusion | flops 1208057856 | bytes 8650752 | tf_op jit(solution)/shard_map/bkpi,bkji->bpj/dot_general | solution.py:58
  74.7 3.0 fusion.24
  77.7 2.0 gather_fusion.2
  79.7 11.2 %all-to-all-start.1 = ((f32[16,2,64,256]{3,2,1,0:T(8,128)}), f32[16,2,64,256]{3,2,1,0:T(8,128)S(1)}, u32[]{:S(2)}, u32[]{:S(2)}) async-start(f32[16,2,64,256]{3,2,1,0:T(8,128)} %bitcast.19), calls=%async_computation.1 | async-start | bytes 4194304 | tf_op jit(solution)/shard_map/all_to_all | solution.py:55
  91.0 0.2 reduce-scatter.3.cloned.1.call-start
  91.3 40.8 %all-to-all-done.1 = f32[16,2,64,256]{3,2,1,0:T(8,128)S(1)} async-done(((f32[16,2,64,256]{3,2,1,0:T(8,128)}), f32[16,2,64,256]{3,2,1,0:T(8,128)S(1)}, u32[]{:S(2)}, u32[]{:S(2)}) %all-to-all-start.1) | async-done | bytes 2097184 | tf_op jit(solution)/shard_map/all_to_all | solution.py:55
  132.1 1.8 gather_fusion.3
  133.9 9.4 %fusion.45 = f32[6,64,256]{2,1,0:T(8,128)S(1)} fusion(f32[6,4,64,256]{3,2,1,0:T(8,128)} %bitcast.140, f32[2,6,4,256,256]{4,3,2,1,0:T(8,128)} %param.7, f32[3,6,64,256]{3,2,1,0:T(8,128)} %param.5), kind=kOutput, calls=%fused_computation.43 | convolution fusion | flops 1208057856 | bytes 8650752 | tf_op jit(solution)/shard_map/bkpi,bkji->bpj/dot_general | solution.py:58
  143.3 3.0 fusion.20
  146.3 2.5 fusion.18
  148.8 6.1 %fusion = f32[6,64,4,256]{3,1,2,0:T(8,128)S(1)} fusion(f32[2,6,4,256,256]{4,3,2,1,0:T(8,128)} %param.7, f32[6,64,256]{2,1,0:T(8,128)S(1)} %fusion.18), kind=kOutput, calls=%fused_computation.4 | convolution fusion | flops 1207959552 | bytes 8257536 | tf_op jit(solution)/shard_map/bpj,bkji->bkpi/dot_general | solution.py:66
  154.9 3.4 fusion.15
  158.3 6.3 %copy.29 = f32[96,64,256]{2,1,0:T(8,128)} copy(f32[96,64,256]{2,0,1:T(8,128)S(1)} %fusion.15) | data formatting | bytes 12582912 | tf_op jit(solution)/shard_map/dot_general | solution.py:73
  164.7 91.8 %reduce-scatter.3.cloned.1.call-done = f32[6,64,256]{2,1,0:T(8,128)} async-done(((f32[96,64,256]{2,1,0:T(8,128)}), f32[6,64,256]{2,1,0:T(8,128)}) %reduce-scatter.3.cloned.1.call-update) | async-done | bytes 393232 | tf_op jit(solution)/shard_map/reduce_scatter | solution.py:74
  256.5 2.6 fusion.22
  259.1 6.2 %fusion.4 = f32[6,64,4,256]{3,1,2,0:T(8,128)S(1)} fusion(f32[2,6,4,256,256]{4,3,2,1,0:T(8,128)} %param.7, f32[6,64,256]{2,1,0:T(8,128)S(1)} %fusion.22), kind=kOutput, calls=%fused_computation.8 | convolution fusion | flops 1207959552 | bytes 8257536 | tf_op jit(solution)/shard_map/bpj,bkji->bkpi/dot_general | solution.py:66
  265.3 3.4 fusion.12
  268.7 6.3 %copy.31 = f32[96,64,256]{2,1,0:T(8,128)} copy(f32[96,64,256]{2,0,1:T(8,128)S(1)} %fusion.12) | data formatting | bytes 12582912 | tf_op jit(solution)/shard_map/dot_general | solution.py:73
  275.0 84.5 %reduce-scatter.5.cloned.1.call-done = f32[6,64,256]{2,1,0:T(8,128)} async-done(((f32[96,64,256]{2,1,0:T(8,128)}), f32[6,64,256]{2,1,0:T(8,128)}) %reduce-scatter.5.cloned.1.call-update) | async-done | bytes 393232 | tf_op jit(solution)/shard_map/reduce_scatter | solution.py:74
  359.6 2.6 fusion.36
  362.2 1.1 pad_maximum_fusion
  (25 shorter events, 1.0 us)
Async XLA Ops:
  15.0 48.5 %all-to-all-start = ((f32[16,2,64,256]{3,2,1,0:T(8,128)}), f32[16,2,64,256]{3,2,1,0:T(8,128)S(1)}, u32[]{:S(2)}, u32[]{:S(2)}) async-start(f32[16,2,64,256]{3,2,1,0:T(8,128)} %bitcast.6), calls=%async_computation | async-start | bytes 4194304 | tf_op jit(solution)/shard_map/all_to_all | solution.py:55
  79.7 52.3 %all-to-all-start.1 = ((f32[16,2,64,256]{3,2,1,0:T(8,128)}), f32[16,2,64,256]{3,2,1,0:T(8,128)S(1)}, u32[]{:S(2)}, u32[]{:S(2)}) async-start(f32[16,2,64,256]{3,2,1,0:T(8,128)} %bitcast.19), calls=%async_computation.1 | async-start | bytes 4194304 | tf_op jit(solution)/shard_map/all_to_all | solution.py:55
  91.0 165.5 %reduce-scatter.3.cloned.1.call-start = ((), (), s32[]{:S(2)}) async-start(), calls=%async_computation.4 | async-start | bytes 6684672 | tf_op jit(solution)/shard_map/reduce_scatter | solution.py:74
  164.6 194.9 %reduce-scatter.5.cloned.1.call-start = ((), (), s32[]{:S(2)}) async-start(), calls=%async_computation.5 | async-start | bytes 6684672 | tf_op jit(solution)/shard_map/reduce_scatter | solution.py:74
Sparse Core Ops, SparseCore 0:
  164.7 91.7 reduce-scatter.2
  275.1 84.3 reduce-scatter.4
where the time goes:
time: 371 us; the launch traced here: 370 us
  waiting for transfers between devices  258 us (70%)
  matrix products  54.7 us (15%)
  local copies, waits for them, and re-layouts  22.7 us (6%)
  starting transfers between devices  18.9 us (5%)
  between operations  13.6 us (4%)
    reduce_scatter x2, waiting for transfers between devices, local(): lax.psum_scatter(summed.reshape(blocks_dev * lax.axis_size('blk'), probe_...  176 us
    all_to_all x2, waiting for transfers between devices, local(): lax.all_to_all(outgoing, 'blk', split_axis=0, concat_axis=0, tiled=True)  81.7 us
    dot_general x2, matrix products, local(): jnp.einsum('bkpi,bkji->bpj', fetched, couplings[height - 1], precision=la...  18.8 us
    all_to_all x2, starting transfers between devices, local(): lax.all_to_all(outgoing, 'blk', split_axis=0, concat_axis=0, tiled=True)  18.6 us
    dot_general x2, local copies, waits for them, and re-layouts, local(): summed = jnp.dot(selector, partials, precision=lax.Precision.HIGHEST)  12.6 us
    dot_general x2, matrix products, local(): jnp.einsum('bpj,bkji->bkpi', solved[height + 1], couplings[height], preci...  12.3 us
    dot_general x3, matrix products, solve_right(): jnp.einsum('bpi,bji->bpj', panel, inverse, precision=lax.Precision.HIGHEST)  9.14 us
    dot_general x3, matrix products, solve_left(): jnp.einsum('bpj,bji->bpi', panel, inverse, precision=lax.Precision.HIGHEST)  7.78 us
  transfers between devices with their start and end apart: 4, of which 4 were waited for; matrix products, arithmetic and copies ran while one was open for 0% of the time, Pallas kernels for 0%

commit v1 on v0

v1 whole, which is shorter than its diff:
```python
import functools

import jax
import jax.numpy as jnp
from jax import lax
from jax.experimental import pallas as pl
from jax.experimental.pallas import tpu as pltpu
from jax.sharding import PartitionSpec as P

LEVELS = 3
CAP = 2
PLANE = 4
CHUNKS = 2
F32 = jnp.float32
BF16 = jnp.bfloat16
NT = (((1,), (1,)), ((), ()))
NN = (((1,), (0,)), ((), ()))
PARAMS = pltpu.CompilerParams(vmem_limit_bytes=32 * 1024 * 1024)


def low_bit(offset):
    return offset & -offset


def near(offset):
    return offset & (offset - 1) == 0


def split(value):
    high = value.astype(BF16)
    return high, (value - high.astype(F32)).astype(BF16)


def product(panel, matrix, dims):
    rows = panel.shape[0]
    panel_high, panel_low = split(panel)
    matrix_high, matrix_low = split(matrix)
    both = lax.dot_general(
        jnp.concatenate([panel_high, panel_low], axis=0), matrix_high, dims, preferred_element_type=F32
    )
    cross = lax.dot_general(panel_high, matrix_low, dims, preferred_element_type=F32)
    return both[:rows] + (both[rows:] + cross)


def tables(dev_rows, slot_rows, members, position):
    levels, rows, fanout = dev_rows.shape
    blocks_dev = rows // members
    width = blocks_dev * fanout
    depth = members // PLANE
    height, place = position // PLANE, position % PLANE
    start = height * PLANE
    flips = jnp.arange(PLANE)
    offsets = jnp.arange(depth)

    def plane_rows(table):
        table = table.reshape(levels, members, width)
        return lax.dynamic_slice_in_dim(table, start, PLANE, axis=1)

    lists, slots = plane_rows(dev_rows), plane_rows(slot_rows)
    positions = jnp.arange(width)
    earlier = positions[None, :] < positions[:, None]
    matches = lists[:, :, :, None] == lists[:, :, None, :]
    rank = jnp.sum(jnp.logical_and(matches, earlier), axis=3, dtype=jnp.int32)
    code = lists * CAP + rank
    owners = (height ^ offsets) * PLANE + place
    wanted = (owners[:, None] * CAP + jnp.arange(CAP)[None, :]).reshape(depth * CAP)
    found = code[:, :, None, :] == wanted[None, None, :, None]
    by_place = jnp.sum(jnp.where(found, slots[:, :, None, :] + 1, 0), axis=3) - 1
    pick = (flips[:, None] ^ place) == flips[None, :]
    packed = jnp.sum(jnp.where(pick[None, :, :, None], by_place[:, None], 0), axis=2)
    mine = (flips == place)[None, :, None]
    own_dev = jnp.sum(jnp.where(mine, lists, 0), axis=1)
    own_slot = jnp.sum(jnp.where(mine, slots, 0), axis=1)
    own_rank = jnp.sum(jnp.where(mine, rank, 0), axis=1)
    flip = (own_dev % PLANE) ^ place
    offset = (own_dev // PLANE) ^ height
    fetch = jnp.where(
        flip == 0,
        offset * blocks_dev + own_slot,
        depth * blocks_dev + ((flip - 1) * depth + offset) * CAP + own_rank,
    )
    put = (flip * depth + offset) * CAP + own_rank
    return packed.reshape(levels, PLANE * depth * CAP), fetch, put


def whole_spec(array):
    return pl.BlockSpec(array.shape, lambda *_: (0,) * array.ndim)


def solve_kernel(*refs, has_fetch, has_probe, has_left, has_parts, order, depth, blocks, fanout):
    refs = list(refs)
    fetch_ref = refs.pop(0)
    put_ref = refs.pop(0)
    probe_ref = refs.pop(0)
    inverse_ref = refs.pop(0)
    coupling_ref = refs.pop(0) if has_fetch or has_parts else None
    step = pl.program_id(0)
    sums = []
    if has_fetch:
        local_refs = [refs.pop(0) for _ in range(depth)]
        moved_refs = [refs.pop(0) for _ in range(2 * (PLANE - 1))]
    elif not has_probe:
        sums = [refs.pop(0) for _ in range(1 + depth.bit_length() - 1)]
    forward_ref = refs.pop(0) if not has_left else None
    solved_ref = refs.pop(0) if has_left else None
    part_refs = [refs.pop(0) for _ in range(2 * PLANE)] if has_parts else []
    pan_ref = refs.pop(0) if has_fetch else None
    hold_ref = refs.pop(0) if has_parts else None
    if has_fetch:

        @pl.when(step == 0)
        def _():
            for offset in range(depth):
                pan_ref[pl.ds(offset * blocks, blocks)] = local_refs[offset][...]
            for flip in range(PLANE - 1):
                for group in range(2):
                    for place, offset in enumerate(order[group]):
                        base = depth * blocks + (flip * depth + offset) * CAP
                        pan_ref[pl.ds(base, CAP)] = moved_refs[group * (PLANE - 1) + flip][place]

    value = probe_ref[...]
    if has_fetch:
        for k in range(fanout):
            value = value - product(pan_ref[fetch_ref[step * fanout + k]], coupling_ref[k], NT)
    for ref in sums:
        value = value - ref[step]
    if has_probe:
        value = product(value, inverse_ref[...], NT)
    if has_left:
        value = product(value, inverse_ref[...], NN)
        solved_ref[...] = value
    else:
        forward_ref[...] = value
    if has_parts:
        for k in range(fanout):
            hold_ref[put_ref[step * fanout + k]] = product(value, coupling_ref[k], NN)

        @pl.when(step == blocks - 1)
        def _():
            for flip in range(PLANE):
                for group in range(2):
                    for place, offset in enumerate(order[group]):
                        part_refs[group * PLANE + flip][place] = hold_ref[pl.ds((flip * depth + offset) * CAP, CAP)]


def solve(
    fetch, put, panel, panel_level, inverses, couplings, level, chunk, order, depth,
    local=None, moved=None, sums=None, left=False, coupling_level=None,
):
    blocks, points = inverses.shape[1], inverses.shape[3]
    fanout = couplings.shape[2]
    has_probe = panel_level is not None
    rows = panel.shape[2] // CHUNKS if has_probe else panel.shape[1]
    has_fetch = local is not None
    has_parts = left and coupling_level is not None
    block_spec = pl.BlockSpec((None, rows, points), lambda g, *_: (g, 0, 0))
    operands, specs = [panel], []
    if has_probe:
        specs.append(pl.BlockSpec((None, None, rows, points), lambda g, *_: (panel_level, g, chunk, 0)))
    else:
        specs.append(block_spec)
    operands.append(inverses)
    specs.append(pl.BlockSpec((None, None, points, points), lambda g, *_: (level, g, 0, 0)))
    if has_fetch or has_parts:
        operands.append(couplings)
        specs.append(
            pl.BlockSpec((None, None, fanout, points, points), lambda g, *_: (coupling_level, g, 0, 0, 0))
        )
    if has_fetch:
        extra = list(local) + list(moved)
    else:
        extra = list(sums) if sums is not None else []
    operands += extra
    specs += [whole_spec(array) for array in extra]
    out_shapes = [jax.ShapeDtypeStruct((blocks, rows, points), F32)]
    out_specs = [block_spec]
    scratch = []
    if has_fetch:
        scratch.append(pltpu.VMEM((depth * (blocks + (PLANE - 1) * CAP), rows, points), F32))
    if has_parts:
        for group in range(2):
            for _ in range(PLANE):
                shape = jax.ShapeDtypeStruct((len(order[group]), CAP, rows, points), F32)
                out_shapes.append(shape)
                out_specs.append(whole_spec(shape))
        scratch.append(pltpu.VMEM((PLANE * depth * CAP, rows, points), F32))
    kernel = functools.partial(
        solve_kernel, has_fetch=has_fetch, has_probe=has_probe, has_left=left, has_parts=has_parts,
        order=order, depth=depth, blocks=blocks, fanout=fanout,
    )
    return pl.pallas_call(
        kernel,
        out_shape=out_shapes,
        grid_spec=pltpu.PrefetchScalarGridSpec(
            num_scalar_prefetch=2, grid=(blocks,), in_specs=specs, out_specs=out_specs, scratch_shapes=scratch
        ),
        compiler_params=PARAMS,
    )(fetch, put, *operands)


def pack_kernel(packed_ref, *refs, offsets, depth):
    sources = refs[: len(offsets)]
    targets = refs[len(offsets) : len(offsets) + PLANE - 1]
    sems = refs[-1]
    copies = []
    for flip in range(1, PLANE):
        for place, offset in enumerate(offsets):
            for rank in range(CAP):
                slot = jnp.maximum(packed_ref[(flip * depth + offset) * CAP + rank], 0)
                copies.append(
                    pltpu.make_async_copy(
                        sources[place].at[slot], targets[flip - 1].at[place, rank], sems.at[len(copies)]
                    )
                )
                copies[-1].start()
    for copy in copies:
        copy.wait()


def pack(packed, sources, offsets, depth):
    rows, points = sources[0].shape[1:]
    count = (PLANE - 1) * len(offsets) * CAP
    anywhere = pl.BlockSpec(memory_space=pl.ANY)
    return pl.pallas_call(
        functools.partial(pack_kernel, offsets=offsets, depth=depth),
        out_shape=[jax.ShapeDtypeStruct((len(offsets), CAP, rows, points), F32)] * (PLANE - 1),
        grid_spec=pltpu.PrefetchScalarGridSpec(
            num_scalar_prefetch=1,
            grid=(),
            in_specs=[anywhere] * len(offsets),
            out_specs=[anywhere] * (PLANE - 1),
            scratch_shapes=[pltpu.SemaphoreType.DMA((count,))],
        ),
        compiler_params=PARAMS,
    )(packed, *sources)


def gather_kernel(packed_ref, *refs, offsets, depth, extra):
    sources = refs[:PLANE]
    extras = refs[PLANE : PLANE + len(extra)]
    targets = refs[PLANE + len(extra) :]
    for place, offset in enumerate(offsets):
        start = jnp.zeros(targets[place].shape, F32)
        for ref, to in zip(extras, extra):
            if to == offset:
                start = start + ref[...]
        targets[place][...] = start
    for flip in range(PLANE):
        for place, offset in enumerate(offsets):
            for rank in range(CAP):
                slot = packed_ref[(flip * depth + offset) * CAP + rank]

                @pl.when(slot >= 0)
                def _(place=place, flip=flip, rank=rank, slot=slot):
                    targets[place][slot] = targets[place][slot] + sources[flip][place, rank]


def gather_sums(packed, sources, offsets, depth, blocks, extra):
    rows, points = sources[0].shape[2:]
    operands = list(sources) + [array for _, array in extra]
    shape = jax.ShapeDtypeStruct((blocks, rows, points), F32)
    return pl.pallas_call(
        functools.partial(gather_kernel, offsets=offsets, depth=depth, extra=[to for to, _ in extra]),
        out_shape=[shape] * len(offsets),
        grid_spec=pltpu.PrefetchScalarGridSpec(
            num_scalar_prefetch=1,
            grid=(1,),
            in_specs=[whole_spec(array) for array in operands],
            out_specs=[whole_spec(shape)] * len(offsets),
        ),
        compiler_params=PARAMS,
    )(packed, *operands)


def flip_move(array, bits):
    members = lax.axis_size("blk")
    return lax.ppermute(array, "blk", [(source, source ^ bits) for source in range(members)])


def local(probes, inverses, couplings, neighbour_devices, neighbour_slots):
    members = lax.axis_size("blk")
    position = lax.axis_index("blk")
    blocks = probes.shape[1]
    depth = members // PLANE
    packed, fetch, put = tables(neighbour_devices, neighbour_slots, members, position)
    order = (
        tuple(offset for offset in range(depth) if near(offset)),
        tuple(offset for offset in range(depth) if not near(offset)),
    )
    far_first = sorted(order[1], key=lambda offset: -offset.bit_count())
    call = functools.partial(solve, inverses=inverses, couplings=couplings, order=order, depth=depth)

    def spread(panels, level):
        held = {0: panels}
        for offset in sorted(order[0][1:], reverse=True):
            held[offset] = flip_move(panels, offset * PLANE)
        for offset in sorted(order[1], key=lambda offset: offset.bit_count()):
            held[offset] = flip_move(held[offset ^ low_bit(offset)], low_bit(offset) * PLANE)
        moved = []
        for group in order:
            packs = pack(packed[level], [held[offset] for offset in group], group, depth)
            moved += [flip_move(array, flip + 1) for flip, array in enumerate(packs)]
        return [held[offset] for offset in range(depth)], moved

    def collect(parts, level):
        arrived = []
        sums = {}
        for group in (1, 0):
            own = parts[group * PLANE]
            others = [flip_move(parts[group * PLANE + flip], flip) for flip in range(1, PLANE)]
            extra = [entry for entry in arrived if entry[0] in order[0][1:]] if group == 0 else []
            results = gather_sums(packed[level], [own] + others, order[group], depth, blocks, extra)
            sums.update(zip(order[group], results))
            if group == 1:
                for offset in far_first:
                    total = sums[offset]
                    for to, array in arrived:
                        if to == offset:
                            total = total + array
                    bit = low_bit(offset)
                    arrived.append((offset ^ bit, flip_move(total, bit * PLANE)))
        addends = [sums[0]]
        for offset in sorted(order[0][1:], reverse=True):
            addends.append(flip_move(sums[offset], offset * PLANE))
        return addends

    columns = []
    for chunk in range(CHUNKS):
        forward = []
        solved = [None] * LEVELS
        (panels,) = call(fetch[0], put[0], probes, 0, level=0, chunk=chunk)
        forward.append(panels)
        for level in range(1, LEVELS):
            held, moved = spread(forward[-1], level - 1)
            top = level == LEVELS - 1
            results = call(
                fetch[level - 1], put[level - 1], probes, level, level=level, chunk=chunk,
                local=held, moved=moved, left=top, coupling_level=level - 1,
            )
            if top:
                solved[level], parts = results[0], results[1:]
            else:
                forward.append(results[0])
        for level in range(LEVELS - 2, -1, -1):
            addends = collect(parts, level)
            lower = level - 1 if level else None
            results = call(
                fetch[max(level - 1, 0)], put[max(level - 1, 0)], forward[level], None, level=level, chunk=chunk,
                sums=addends, left=True, coupling_level=lower,
            )
            solved[level], parts = results[0], results[1:]
        columns.append(jnp.stack(solved))
    return jnp.concatenate(columns, axis=2)


def solution(mesh):
    return jax.shard_map(
        local,
        mesh=mesh,
        in_specs=(
            P(None, ("grp", "blk"), None, None),
            P(None, ("grp", "blk"), None, None),
            P(None, ("grp", "blk"), None, None, None),
            P(None, "grp", None),
            P(None, "grp", None),
        ),
        out_specs=P(None, ("grp", "blk"), None, None),
        check_vma=False,
    )
```

time: 371 us -> 246 us (0.66)
  waiting for transfers between devices: 258 us -> 80.1 us
  Pallas kernels: 0 us -> 61 us
  matrix products: 54.7 us -> 0 us
  starting transfers between devices: 18.9 us -> 62.5 us
  local copies, waits for them, and re-layouts: 22.7 us -> 38.6 us
  between operations: 13.6 us -> 0.53 us
    reduce_scatter x2 -> x0, waiting for transfers between devices: 176 us -> none  [local(): lax.psum_scatter(summed.reshape(blocks_dev * lax.axis_size('blk'), probe_...]
    all_to_all x2 -> x0, waiting for transfers between devices: 81.7 us -> none  [local(): lax.all_to_all(outgoing, 'blk', split_axis=0, concat_axis=0, tiled=True)]
    ppermute x0 -> x72, waiting for transfers between devices: none -> 80.1 us  [flip_move(): lax.ppermute(array, 'blk', [(source, source ^ bits) for source in range(m...]
    ppermute x0 -> x72, starting transfers between devices: none -> 62.5 us  [flip_move(): lax.ppermute(array, 'blk', [(source, source ^ bits) for source in range(m...]
    pallas_call x0 -> x26, Pallas kernels: none -> 61 us  [the longest x10 39 us: solve(): pl.pallas_call(kernel, out_shape=out_shapes, grid_spec=pltpu.PrefetchScal...]
    dot_general x12 -> x0, matrix products: 54.7 us -> none  [the longest x2 18.8 us: local(): jnp.einsum('bkpi,bkji->bpj', fetched, couplings[height - 1], precision=la...]
    unnamed x0 -> x72, local copies, waits for them, and re-layouts: none -> 38.2 us
    all_to_all x2 -> x0, starting transfers between devices: 18.6 us -> none  [local(): lax.all_to_all(outgoing, 'blk', split_axis=0, concat_axis=0, tiled=True)]
  transfers between devices with their start and end apart: 4 -> 72, of which waited for: 4 -> 27; matrix products, arithmetic and copies ran while one was open for 0% -> 0% of each run, Pallas kernels for 0% -> 24%
where the time goes in v1:
time: 246 us; the launch traced here: 245 us
  waiting for transfers between devices  80.1 us (33%)
  starting transfers between devices  62.5 us (25%)
  Pallas kernels  61 us (25%)
  local copies, waits for them, and re-layouts  38.6 us (16%)
    ppermute x72, waiting for transfers between devices, flip_move(): lax.ppermute(array, 'blk', [(source, source ^ bits) for source in range(m...  80.1 us
    ppermute x72, starting transfers between devices, flip_move(): lax.ppermute(array, 'blk', [(source, source ^ bits) for source in range(m...  62.5 us
    pallas_call x10, Pallas kernels, solve(): pl.pallas_call(kernel, out_shape=out_shapes, grid_spec=pltpu.PrefetchScal...  39 us
    unnamed x72, local copies, waits for them, and re-layouts  38.2 us
    pallas_call x8, Pallas kernels, pack(): pl.pallas_call(functools.partial(pack_kernel, offsets=offsets, depth=dept...  16.3 us
    pallas_call x8, Pallas kernels, gather_sums(): pl.pallas_call(functools.partial(gather_kernel, offsets=offsets, depth=de...  5.61 us
  transfers between devices with their start and end apart: 72, of which 27 were waited for; matrix products, arithmetic and copies ran while one was open for 0% of the time, Pallas kernels for 24%

profile of v1, /device:TPU:0, one launch (start us, length us, event | category | flops | bytes accessed | tf_op | source)
XLA Modules:
  0.0 244.8 jit_solution(5500686160451952976)
XLA Ops:
  2.3 2.3 copy-done
  7.7 3.1 %collective-permute-start = (f32[6,32,256]{2,1,0:T(8,128)S(1)}, f32[6,32,256]{2,1,0:T(8,128)S(1)}, u32[]{:S(2)}, u32[]{:S(2)}) collective-permute-start(f32[6,32,256]{2,1,0:T(8,128)S(1)} %shard_map.55.refs_0_.refs_5_.refs_2_), channel_id=1, source_target_pairs={{0,4},{1,5},{2,6},{3,7},{4,0},{5,1},{6,2},{7,3},{8,12},{9,13},{10,... | collective-permute-start | bytes 589832 | tf_op jit(solution)/shard_map/ppermute | solution.py:277
  10.8 2.6 %collective-permute-start.1 = (f32[6,32,256]{2,1,0:T(8,128)S(1)}, f32[6,32,256]{2,1,0:T(8,128)S(1)}, u32[]{:S(2)}, u32[]{:S(2)}) collective-permute-start(f32[6,32,256]{2,1,0:T(8,128)S(1)} %shard_map.55.refs_0_.refs_5_.refs_2_), channel_id=1, source_target_pairs={{0,8},{1,9},{2,10},{3,11},{4,12},{5,13},{6,14},{7,15},{8,0},{9,1},... | collective-permute-start | bytes 589832 | tf_op jit(solution)/shard_map/ppermute | solution.py:277
  16.4 10.5 %collective-permute-done.1.refs_2_.refs_7_ = f32[6,32,256]{2,1,0:T(8,128)S(1)} collective-permute-done((f32[6,32,256]{2,1,0:T(8,128)S(1)}, f32[6,32,256]{2,1,0:T(8,128)S(1)}, u32[]{:S(2)}, u32[]{:S(2)}) %collective-permute-start.1) | collective-permute-done | bytes 196640 | tf_op jit(solution)/shard_map/ppermute | solution.py:277
  38.2 7.8 %shard_map.69 = (f32[3,2,32,256]{3,2,1,0:T(8,128)}, f32[3,2,32,256]{3,2,1,0:T(8,128)}, f32[3,2,32,256]{3,2,1,0:T(8,128)}) custom-call(s32[32]{0:T(128)S(1)} %squeeze.14.packed_ref, f32[6,32,256]{2,1,0:T(8,128)S(1)} %shard_map.68.refs_0_.refs_5_.refs_2_, f32[6,32,256]{2,1,0:T(8,128)S(1)} %collective-permute-done.36.refs_1_.refs_6_, ...), custom_call_target="tpu_custom_call" | custom-call | tf_op jit(solution)/shard_map/pallas_call | solution.py:224
  51.9 8.2 %collective-permute-done.8.refs_14_ = f32[1,2,32,256]{3,2,1,0:T(8,128)S(1)} collective-permute-done((f32[1,2,32,256]{3,2,1,0:T(8,128)S(1)}, f32[1,2,32,256]{3,2,1,0:T(8,128)S(1)}, u32[]{:S(2)}, u32[]{:S(2)}) %collective-permute-start.8) | collective-permute-done | bytes 65568 | tf_op jit(solution)/shard_map/ppermute | solution.py:277
  60.7 2.3 copy-done.1
  63.0 4.6 %copy-done.3 = f32[2,6,4,256,256]{4,3,2,1,0:T(8,128)S(1)} copy-done((f32[2,6,4,256,256]{4,3,2,1,0:T(8,128)S(1)}, f32[2,6,4,256,256]{4,3,2,1,0:T(8,128)}, u32[]{:S(2)}) %copy-start.3) | copy-done | bytes 12582936
  77.0 4.7 %shard_map.58.refs_0_.refs_5_.refs_2_ = f32[6,32,256]{2,1,0:T(8,128)S(1)} custom-call(s32[24]{0:T(128)S(1)} %get-tuple-element.165.refs_0_, s32[24]{0:T(128)S(1)} %get-tuple-element.158.refs_1_, f32[3,6,64,256]{3,2,1,0:T(8,128)S(1)} %copy-done.8, f32[3,6,256,256]{3,2,1,0:T(8,128)S(1)} %copy-done.1, f32[2,6,4,256,256]{4,3,2,1,0:T(8,128)S(1)} %copy-done.3, ...), custom_call_target="tpu_custom_call" | custom-call | tf_op jit(solution)/shard_map/pallas_call | solution.py:191
  81.7 2.6 %collective-permute-start.10 = (f32[6,32,256]{2,1,0:T(8,128)S(1)}, f32[6,32,256]{2,1,0:T(8,128)}, u32[]{:S(2)}, u32[]{:S(2)}) collective-permute-start(f32[6,32,256]{2,1,0:T(8,128)S(1)} %shard_map.58.refs_0_.refs_5_.refs_2_), channel_id=1, source_target_pairs={{0,8},{1,9},{2,10},{3,11},{4,12},{5,13},{6,14},{7,15},{8,0},{9,1},... | collective-permute-start | bytes 589832 | tf_op jit(solution)/shard_map/ppermute | solution.py:277
  87.6 2.6 %collective-permute-done.43.refs_13_ = f32[1,2,32,256]{3,2,1,0:T(8,128)S(1)} collective-permute-done((f32[1,2,32,256]{3,2,1,0:T(8,128)S(1)}, f32[1,2,32,256]{3,2,1,0:T(8,128)S(1)}, u32[]{:S(2)}, u32[]{:S(2)}) %collective-permute-start.43) | collective-permute-done | bytes 65568 | tf_op jit(solution)/shard_map/ppermute | solution.py:277
  92.7 6.0 %shard_map.71.refs_0_.refs_5_.refs_2_ = f32[6,32,256]{2,1,0:T(8,128)S(1)} custom-call(s32[24]{0:T(128)S(1)} %get-tuple-element.165.refs_0_, s32[24]{0:T(128)S(1)} %get-tuple-element.158.refs_1_, f32[3,6,64,256]{3,2,1,0:T(8,128)S(1)} %copy-done.9, f32[3,6,256,256]{3,2,1,0:T(8,128)S(1)} %copy-done.1, f32[2,6,4,256,256]{4,3,2,1,0:T(8,128)S(1)} %copy-done.4, ...), custom_call_target="tpu_custom_call" | custom-call | tf_op jit(solution)/shard_map/pallas_call | solution.py:191
  104.6 6.7 %collective-permute-done.46.refs_2_.refs_7_ = f32[6,32,256]{2,1,0:T(8,128)S(1)} collective-permute-done((f32[6,32,256]{2,1,0:T(8,128)S(1)}, f32[6,32,256]{2,1,0:T(8,128)S(1)}, u32[]{:S(2)}, u32[]{:S(2)}) %collective-permute-start.46) | collective-permute-done | bytes 196640 | tf_op jit(solution)/shard_map/ppermute | solution.py:277
  122.8 5.5 %collective-permute-done.16.refs_13_ = f32[1,2,32,256]{3,2,1,0:T(8,128)S(1)} collective-permute-done((f32[1,2,32,256]{3,2,1,0:T(8,128)S(1)}, f32[1,2,32,256]{3,2,1,0:T(8,128)S(1)}, u32[]{:S(2)}, u32[]{:S(2)}) %collective-permute-start.16) | collective-permute-done | bytes 65568 | tf_op jit(solution)/shard_map/ppermute | solution.py:277
  130.8 2.3 copy-done.2
  133.1 4.6 %copy-done.5 = f32[2,6,4,256,256]{4,3,2,1,0:T(8,128)S(1)} copy-done((f32[2,6,4,256,256]{4,3,2,1,0:T(8,128)S(1)}, f32[2,6,4,256,256]{4,3,2,1,0:T(8,128)}, u32[]{:S(2)}) %copy-start.5) | copy-done | bytes 12582936
  137.7 8.1 %shard_map.61 = (f32[6,32,256]{2,1,0:T(8,128)S(1)}, f32[3,2,32,256]{3,2,1,0:T(8,128)S(1)}, f32[3,2,32,256]{3,2,1,0:T(8,128)S(1)}, f32[3,2,32,256]{3,2,1,0:T(8,12...) custom-call(s32[24]{0:T(128)S(1)} %get-tuple-element.164.refs_0_, ...), custom_call_target="tpu_custom_call" | custom-call | tf_op jit(solution)/shard_map/pallas_call | solution.py:191
  150.2 7.1 %shard_map.74 = (f32[6,32,256]{2,1,0:T(8,128)S(1)}, f32[3,2,32,256]{3,2,1,0:T(8,128)S(1)}, f32[3,2,32,256]{3,2,1,0:T(8,128)S(1)}, f32[3,2,32,256]{3,2,1,0:T(8,12...) custom-call(s32[24]{0:T(128)S(1)} %get-tuple-element.164.refs_0_, ...), custom_call_target="tpu_custom_call" | custom-call | tf_op jit(solution)/shard_map/pallas_call | solution.py:191
  157.6 2.4 collective-permute-done.23.refs_3_
  162.3 2.4 collective-permute-done.58.refs_2_
  171.4 1.9 collective-permute-start.25
  176.8 2.1 collective-permute-done.60.refs_4_
  182.4 4.6 %collective-permute-done.26.refs_7_ = f32[6,32,256]{2,1,0:T(8,128)S(1)} collective-permute-done((f32[6,32,256]{2,1,0:T(8,128)S(1)}, f32[6,32,256]{2,1,0:T(8,128)S(1)}, u32[]{:S(2)}, u32[]{:S(2)}) %collective-permute-start.26) | collective-permute-done | bytes 196640 | tf_op jit(solution)/shard_map/ppermute | solution.py:277
  187.0 4.6 %copy-done.6 = f32[2,6,4,256,256]{4,3,2,1,0:T(8,128)S(1)} copy-done((f32[2,6,4,256,256]{4,3,2,1,0:T(8,128)S(1)}, f32[2,6,4,256,256]{4,3,2,1,0:T(8,128)}, u32[]{:S(2)}) %copy-start.6) | copy-done | bytes 12582936
  191.6 3.2 %shard_map.64 = (f32[6,32,256]{2,1,0:T(8,128)S(1)}, f32[3,2,32,256]{3,2,1,0:T(8,128)S(1)}, f32[3,2,32,256]{3,2,1,0:T(8,128)S(1)}, f32[3,2,32,256]{3,2,1,0:T(8,12...) custom-call(s32[24]{0:T(128)S(1)} %get-tuple-element.165.refs_0_, ...), custom_call_target="tpu_custom_call" | custom-call | tf_op jit(solution)/shard_map/pallas_call | solution.py:191
  197.3 3.2 %shard_map.77 = (f32[6,32,256]{2,1,0:T(8,128)S(1)}, f32[3,2,32,256]{3,2,1,0:T(8,128)S(1)}, f32[3,2,32,256]{3,2,1,0:T(8,128)S(1)}, f32[3,2,32,256]{3,2,1,0:T(8,12...) custom-call(s32[24]{0:T(128)S(1)} %get-tuple-element.165.refs_0_, ...), custom_call_target="tpu_custom_call" | custom-call | tf_op jit(solution)/shard_map/pallas_call | solution.py:191
  202.2 6.5 %collective-permute-done.32.refs_3_ = f32[1,2,32,256]{3,2,1,0:T(8,128)S(1)} collective-permute-done((f32[1,2,32,256]{3,2,1,0:T(8,128)S(1)}, f32[1,2,32,256]{3,2,1,0:T(8,128)S(1)}, u32[]{:S(2)}, u32[]{:S(2)}) %collective-permute-start.32) | collective-permute-done | bytes 65568 | tf_op jit(solution)/shard_map/ppermute | solution.py:277
  211.0 2.7 %collective-permute-done.67.refs_2_ = f32[1,2,32,256]{3,2,1,0:T(8,128)S(1)} collective-permute-done((f32[1,2,32,256]{3,2,1,0:T(8,128)S(1)}, f32[1,2,32,256]{3,2,1,0:T(8,128)S(1)}, u32[]{:S(2)}, u32[]{:S(2)}) %collective-permute-start.67) | collective-permute-done | bytes 65568 | tf_op jit(solution)/shard_map/ppermute | solution.py:277
  218.0 3.4 %collective-permute-done.33.refs_4_ = f32[6,32,256]{2,1,0:T(8,128)S(1)} collective-permute-done((f32[6,32,256]{2,1,0:T(8,128)S(1)}, f32[6,32,256]{2,1,0:T(8,128)S(1)}, u32[]{:S(2)}, u32[]{:S(2)}) %collective-permute-start.33) | collective-permute-done | bytes 196640 | tf_op jit(solution)/shard_map/ppermute | solution.py:277
  222.5 2.1 collective-permute-start.35
  229.3 8.2 %collective-permute-done.34.refs_5_ = f32[6,32,256]{2,1,0:T(8,128)S(1)} collective-permute-done((f32[6,32,256]{2,1,0:T(8,128)S(1)}, f32[6,32,256]{2,1,0:T(8,128)S(1)}, u32[]{:S(2)}, u32[]{:S(2)}) %collective-permute-start.34) | collective-permute-done | bytes 196640 | tf_op jit(solution)/shard_map/ppermute | solution.py:277
  239.0 3.0 %collective-permute-done.70.refs_5_ = f32[6,32,256]{2,1,0:T(8,128)S(1)} collective-permute-done((f32[6,32,256]{2,1,0:T(8,128)S(1)}, f32[6,32,256]{2,1,0:T(8,128)S(1)}, u32[]{:S(2)}, u32[]{:S(2)}) %collective-permute-start.70) | collective-permute-done | bytes 196640 | tf_op jit(solution)/shard_map/ppermute | solution.py:277
  (232 shorter events, 102.4 us)
Async XLA Ops:
  7.7 20.1 %collective-permute-start = (f32[6,32,256]{2,1,0:T(8,128)S(1)}, f32[6,32,256]{2,1,0:T(8,128)S(1)}, u32[]{:S(2)}, u32[]{:S(2)}) collective-permute-start(f32[6,32,256]{2,1,0:T(8,128)S(1)} %shard_map.55.refs_0_.refs_5_.refs_2_), channel_id=1, source_target_pairs={{0,4},{1,5},{2,6},{3,7},{4,0},{5,1},{6,2},{7,3},{8,12},{9,13},{10,... | collective-permute-start | bytes 589832 | tf_op jit(solution)/shard_map/ppermute | solution.py:277
  10.8 16.1 %collective-permute-start.1 = (f32[6,32,256]{2,1,0:T(8,128)S(1)}, f32[6,32,256]{2,1,0:T(8,128)S(1)}, u32[]{:S(2)}, u32[]{:S(2)}) collective-permute-start(f32[6,32,256]{2,1,0:T(8,128)S(1)} %shard_map.55.refs_0_.refs_5_.refs_2_), channel_id=1, source_target_pairs={{0,8},{1,9},{2,10},{3,11},{4,12},{5,13},{6,14},{7,15},{8,0},{9,1},... | collective-permute-start | bytes 589832 | tf_op jit(solution)/shard_map/ppermute | solution.py:277
  15.2 18.6 %collective-permute-start.37 = (f32[6,32,256]{2,1,0:T(8,128)S(1)}, f32[6,32,256]{2,1,0:T(8,128)}, u32[]{:S(2)}, u32[]{:S(2)}) collective-permute-start(f32[6,32,256]{2,1,0:T(8,128)S(1)} %shard_map.68.refs_0_.refs_5_.refs_2_), channel_id=1, source_target_pairs={{0,8},{1,9},{2,10},{3,11},{4,12},{5,13},{6,14},{7,15},{8,0},{9,1},... | collective-permute-start | bytes 589832 | tf_op jit(solution)/shard_map/ppermute | solution.py:277
  15.6 19.9 %collective-permute-start.36 = (f32[6,32,256]{2,1,0:T(8,128)S(1)}, f32[6,32,256]{2,1,0:T(8,128)S(1)}, u32[]{:S(2)}, u32[]{:S(2)}) collective-permute-start(f32[6,32,256]{2,1,0:T(8,128)S(1)} %shard_map.68.refs_0_.refs_5_.refs_2_), channel_id=1, source_target_pairs={{0,4},{1,5},{2,6},{3,7},{4,0},{5,1},{6,2},{7,3},{8,12},{9,13},{10,... | collective-permute-start | bytes 589832 | tf_op jit(solution)/shard_map/ppermute | solution.py:277
  29.5 16.5 %collective-permute-start.4 = (f32[3,2,32,256]{3,2,1,0:T(8,128)S(1)}, f32[3,2,32,256]{3,2,1,0:T(8,128)S(1)}, u32[]{:S(2)}, u32[]{:S(2)}) collective-permute-start(f32[3,2,32,256]{3,2,1,0:T(8,128)S(1)} %get-tuple-element.78), channel_id=1, source_target_pairs={{0,2},{1,3},{2,0},{3,1},{4,6},{5,7},{6,4},{7,5},{8,10},{9,11},{10,... | collective-permute-start | bytes 589832 | tf_op jit(solution)/shard_map/ppermute | solution.py:277
  32.9 13.7 %collective-permute-start.5 = (f32[3,2,32,256]{3,2,1,0:T(8,128)S(1)}, f32[3,2,32,256]{3,2,1,0:T(8,128)S(1)}, u32[]{:S(2)}, u32[]{:S(2)}) collective-permute-start(f32[3,2,32,256]{3,2,1,0:T(8,128)S(1)} %get-tuple-element.79), channel_id=1, source_target_pairs={{0,3},{1,2},{2,1},{3,0},{4,7},{5,6},{6,5},{7,4},{8,11},{9,10},{10,... | collective-permute-start | bytes 589832 | tf_op jit(solution)/shard_map/ppermute | solution.py:277
  33.8 15.0 %collective-permute-start.6 = (f32[1,2,32,256]{3,2,1,0:T(8,128)S(1)}, f32[1,2,32,256]{3,2,1,0:T(8,128)S(1)}, u32[]{:S(2)}, u32[]{:S(2)}) collective-permute-start(f32[1,2,32,256]{3,2,1,0:T(8,128)S(1)} %get-tuple-element.80), channel_id=1, source_target_pairs={{0,1},{1,0},{2,3},{3,2},{4,5},{5,4},{6,7},{7,6},{8,9},{9,8},{10,11... | collective-permute-start | bytes 196616 | tf_op jit(solution)/shard_map/ppermute | solution.py:277
  35.5 14.3 %collective-permute-start.7 = (f32[1,2,32,256]{3,2,1,0:T(8,128)S(1)}, f32[1,2,32,256]{3,2,1,0:T(8,128)S(1)}, u32[]{:S(2)}, u32[]{:S(2)}) collective-permute-start(f32[1,2,32,256]{3,2,1,0:T(8,128)S(1)} %get-tuple-element.81), channel_id=1, source_target_pairs={{0,2},{1,3},{2,0},{3,1},{4,6},{5,7},{6,4},{7,5},{8,10},{9,11},{10,... | collective-permute-start | bytes 196616 | tf_op jit(solution)/shard_map/ppermute | solution.py:277
  36.7 47.6 %collective-permute-start.38 = (f32[6,32,256]{2,1,0:T(8,128)}, f32[6,32,256]{2,1,0:T(8,128)S(1)}, u32[]{:S(2)}, u32[]{:S(2)}) collective-permute-start(f32[6,32,256]{2,1,0:T(8,128)} %collective-permute-done.37.refs_2_.refs_7_), channel_id=1, source_target_pairs={{0,4},{1,5},{2,6},{3,7},{4,0},{5,1},{6,2},{7,3},{8,12},{9,13},{10,... | collective-permute-start | bytes 589832 | tf_op jit(solution)/shard_map/ppermute | solution.py:277
  46.6 39.0 %collective-permute-start.39 = (f32[3,2,32,256]{3,2,1,0:T(8,128)}, f32[3,2,32,256]{3,2,1,0:T(8,128)}, u32[]{:S(2)}, u32[]{:S(2)}) collective-permute-start(f32[3,2,32,256]{3,2,1,0:T(8,128)} %get-tuple-element.113), channel_id=1, source_target_pairs={{0,1},{1,0},{2,3},{3,2},{4,5},{5,4},{6,7},{7,6},{8,9},{9,8},{10,11... | collective-permute-start | bytes 589832 | tf_op jit(solution)/shard_map/ppermute | solution.py:277
  47.3 38.4 %collective-permute-start.40 = (f32[3,2,32,256]{3,2,1,0:T(8,128)}, f32[3,2,32,256]{3,2,1,0:T(8,128)}, u32[]{:S(2)}, u32[]{:S(2)}) collective-permute-start(f32[3,2,32,256]{3,2,1,0:T(8,128)} %get-tuple-element.114), channel_id=1, source_target_pairs={{0,2},{1,3},{2,0},{3,1},{4,6},{5,7},{6,4},{7,5},{8,10},{9,11},{10,... | collective-permute-start | bytes 589832 | tf_op jit(solution)/shard_map/ppermute | solution.py:277
  49.5 37.9 %collective-permute-start.41 = (f32[3,2,32,256]{3,2,1,0:T(8,128)}, f32[3,2,32,256]{3,2,1,0:T(8,128)}, u32[]{:S(2)}, u32[]{:S(2)}) collective-permute-start(f32[3,2,32,256]{3,2,1,0:T(8,128)} %get-tuple-element.115), channel_id=1, source_target_pairs={{0,3},{1,2},{2,1},{3,0},{4,7},{5,6},{6,5},{7,4},{8,11},{9,10},{10,... | collective-permute-start | bytes 589832 | tf_op jit(solution)/shard_map/ppermute | solution.py:277
  81.7 18.9 %collective-permute-start.10 = (f32[6,32,256]{2,1,0:T(8,128)S(1)}, f32[6,32,256]{2,1,0:T(8,128)}, u32[]{:S(2)}, u32[]{:S(2)}) collective-permute-start(f32[6,32,256]{2,1,0:T(8,128)S(1)} %shard_map.58.refs_0_.refs_5_.refs_2_), channel_id=1, source_target_pairs={{0,8},{1,9},{2,10},{3,11},{4,12},{5,13},{6,14},{7,15},{8,0},{9,1},... | collective-permute-start | bytes 589832 | tf_op jit(solution)/shard_map/ppermute | solution.py:277
  84.3 17.0 %collective-permute-start.9 = (f32[6,32,256]{2,1,0:T(8,128)S(1)}, f32[6,32,256]{2,1,0:T(8,128)}, u32[]{:S(2)}, u32[]{:S(2)}) collective-permute-start(f32[6,32,256]{2,1,0:T(8,128)S(1)} %shard_map.58.refs_0_.refs_5_.refs_2_), channel_id=1, source_target_pairs={{0,4},{1,5},{2,6},{3,7},{4,0},{5,1},{6,2},{7,3},{8,12},{9,13},{10,... | collective-permute-start | bytes 589832 | tf_op jit(solution)/shard_map/ppermute | solution.py:277
  100.6 14.0 %collective-permute-start.11 = (f32[6,32,256]{2,1,0:T(8,128)}, f32[6,32,256]{2,1,0:T(8,128)S(1)}, u32[]{:S(2)}, u32[]{:S(2)}) collective-permute-start(f32[6,32,256]{2,1,0:T(8,128)} %collective-permute-done.10.refs_2_.refs_7_), channel_id=1, source_target_pairs={{0,4},{1,5},{2,6},{3,7},{4,0},{5,1},{6,2},{7,3},{8,12},{9,13},{10,... | collective-permute-start | bytes 589832 | tf_op jit(solution)/shard_map/ppermute | solution.py:277
  114.7 31.2 %collective-permute-start.49 = (f32[3,2,32,256]{3,2,1,0:T(8,128)S(1)}, f32[3,2,32,256]{3,2,1,0:T(8,128)S(1)}, u32[]{:S(2)}, u32[]{:S(2)}) collective-permute-start(f32[3,2,32,256]{3,2,1,0:T(8,128)S(1)} %get-tuple-element.120), channel_id=1, source_target_pairs={{0,2},{1,3},{2,0},{3,1},{4,6},{5,7},{6,4},{7,5},{8,10},{9,11},{10,... | collective-permute-start | bytes 589832 | tf_op jit(solution)/shard_map/ppermute | solution.py:277
  116.1 30.2 %collective-permute-start.50 = (f32[3,2,32,256]{3,2,1,0:T(8,128)S(1)}, f32[3,2,32,256]{3,2,1,0:T(8,128)S(1)}, u32[]{:S(2)}, u32[]{:S(2)}) collective-permute-start(f32[3,2,32,256]{3,2,1,0:T(8,128)S(1)} %get-tuple-element.121), channel_id=1, source_target_pairs={{0,3},{1,2},{2,1},{3,0},{4,7},{5,6},{6,5},{7,4},{8,11},{9,10},{10,... | collective-permute-start | bytes 589832 | tf_op jit(solution)/shard_map/ppermute | solution.py:277
  121.8 25.2 %collective-permute-start.51 = (f32[1,2,32,256]{3,2,1,0:T(8,128)S(1)}, f32[1,2,32,256]{3,2,1,0:T(8,128)S(1)}, u32[]{:S(2)}, u32[]{:S(2)}) collective-permute-start(f32[1,2,32,256]{3,2,1,0:T(8,128)S(1)} %get-tuple-element.122), channel_id=1, source_target_pairs={{0,1},{1,0},{2,3},{3,2},{4,5},{5,4},{6,7},{7,6},{8,9},{9,8},{10,11... | collective-permute-start | bytes 196616 | tf_op jit(solution)/shard_map/ppermute | solution.py:277
  128.3 18.7 %collective-permute-start.52 = (f32[1,2,32,256]{3,2,1,0:T(8,128)S(1)}, f32[1,2,32,256]{3,2,1,0:T(8,128)S(1)}, u32[]{:S(2)}, u32[]{:S(2)}) collective-permute-start(f32[1,2,32,256]{3,2,1,0:T(8,128)S(1)} %get-tuple-element.123), channel_id=1, source_target_pairs={{0,2},{1,3},{2,0},{3,1},{4,6},{5,7},{6,4},{7,5},{8,10},{9,11},{10,... | collective-permute-start | bytes 196616 | tf_op jit(solution)/shard_map/ppermute | solution.py:277
  129.7 18.7 %collective-permute-start.53 = (f32[1,2,32,256]{3,2,1,0:T(8,128)S(1)}, f32[1,2,32,256]{3,2,1,0:T(8,128)S(1)}, u32[]{:S(2)}, u32[]{:S(2)}) collective-permute-start(f32[1,2,32,256]{3,2,1,0:T(8,128)S(1)} %get-tuple-element.124), channel_id=1, source_target_pairs={{0,3},{1,2},{2,1},{3,0},{4,7},{5,6},{6,5},{7,4},{8,11},{9,10},{10,... | collective-permute-start | bytes 196616 | tf_op jit(solution)/shard_map/ppermute | solution.py:277
  147.0 19.1 %collective-permute-start.18 = (f32[3,2,32,256]{3,2,1,0:T(8,128)S(1)}, f32[3,2,32,256]{3,2,1,0:T(8,128)S(1)}, u32[]{:S(2)}, u32[]{:S(2)}) collective-permute-start(f32[3,2,32,256]{3,2,1,0:T(8,128)S(1)} %get-tuple-element.90), channel_id=1, source_target_pairs={{0,1},{1,0},{2,3},{3,2},{4,5},{5,4},{6,7},{7,6},{8,9},{9,8},{10,11... | collective-permute-start | bytes 589832 | tf_op jit(solution)/shard_map/ppermute | solution.py:277
  147.0 20.1 %collective-permute-start.19 = (f32[3,2,32,256]{3,2,1,0:T(8,128)S(1)}, f32[3,2,32,256]{3,2,1,0:T(8,128)S(1)}, u32[]{:S(2)}, u32[]{:S(2)}) collective-permute-start(f32[3,2,32,256]{3,2,1,0:T(8,128)S(1)} %get-tuple-element.91), channel_id=1, source_target_pairs={{0,2},{1,3},{2,0},{3,1},{4,6},{5,7},{6,4},{7,5},{8,10},{9,11},{10,... | collective-permute-start | bytes 589832 | tf_op jit(solution)/shard_map/ppermute | solution.py:277
  148.5 19.4 %collective-permute-start.20 = (f32[3,2,32,256]{3,2,1,0:T(8,128)S(1)}, f32[3,2,32,256]{3,2,1,0:T(8,128)S(1)}, u32[]{:S(2)}, u32[]{:S(2)}) collective-permute-start(f32[3,2,32,256]{3,2,1,0:T(8,128)S(1)} %get-tuple-element.92), channel_id=1, source_target_pairs={{0,3},{1,2},{2,1},{3,0},{4,7},{5,6},{6,5},{7,4},{8,11},{9,10},{10,... | collective-permute-start | bytes 589832 | tf_op jit(solution)/shard_map/ppermute | solution.py:277
  179.7 15.9 %collective-permute-start.61 = (f32[6,32,256]{2,1,0:T(8,128)S(1)}, f32[6,32,256]{2,1,0:T(8,128)S(1)}, u32[]{:S(2)}, u32[]{:S(2)}) collective-permute-start(f32[6,32,256]{2,1,0:T(8,128)S(1)} %get-tuple-element.134), channel_id=1, source_target_pairs={{0,8},{1,9},{2,10},{3,11},{4,12},{5,13},{6,14},{7,15},{8,0},{9,1},... | collective-permute-start | bytes 589832 | tf_op jit(solution)/shard_map/ppermute | solution.py:277
  180.7 16.4 %collective-permute-start.62 = (f32[6,32,256]{2,1,0:T(8,128)S(1)}, f32[6,32,256]{2,1,0:T(8,128)S(1)}, u32[]{:S(2)}, u32[]{:S(2)}) collective-permute-start(f32[6,32,256]{2,1,0:T(8,128)S(1)} %get-tuple-element.135), channel_id=1, source_target_pairs={{0,4},{1,5},{2,6},{3,7},{4,0},{5,1},{6,2},{7,3},{8,12},{9,13},{10,... | collective-permute-start | bytes 589832 | tf_op jit(solution)/shard_map/ppermute | solution.py:277
  195.5 18.9 %collective-permute-start.27 = (f32[3,2,32,256]{3,2,1,0:T(8,128)S(1)}, f32[3,2,32,256]{3,2,1,0:T(8,128)S(1)}, u32[]{:S(2)}, u32[]{:S(2)}) collective-permute-start(f32[3,2,32,256]{3,2,1,0:T(8,128)S(1)} %get-tuple-element.101), channel_id=1, source_target_pairs={{0,1},{1,0},{2,3},{3,2},{4,5},{5,4},{6,7},{7,6},{8,9},{9,8},{10,11... | collective-permute-start | bytes 589832 | tf_op jit(solution)/shard_map/ppermute | solution.py:277
  195.6 20.1 %collective-permute-start.28 = (f32[3,2,32,256]{3,2,1,0:T(8,128)S(1)}, f32[3,2,32,256]{3,2,1,0:T(8,128)S(1)}, u32[]{:S(2)}, u32[]{:S(2)}) collective-permute-start(f32[3,2,32,256]{3,2,1,0:T(8,128)S(1)} %get-tuple-element.102), channel_id=1, source_target_pairs={{0,2},{1,3},{2,0},{3,1},{4,6},{5,7},{6,4},{7,5},{8,10},{9,11},{10,... | collective-permute-start | bytes 589832 | tf_op jit(solution)/shard_map/ppermute | solution.py:277
  197.1 19.2 %collective-permute-start.29 = (f32[3,2,32,256]{3,2,1,0:T(8,128)S(1)}, f32[3,2,32,256]{3,2,1,0:T(8,128)S(1)}, u32[]{:S(2)}, u32[]{:S(2)}) collective-permute-start(f32[3,2,32,256]{3,2,1,0:T(8,128)S(1)} %get-tuple-element.103), channel_id=1, source_target_pairs={{0,3},{1,2},{2,1},{3,0},{4,7},{5,6},{6,5},{7,4},{8,11},{9,10},{10,... | collective-permute-start | bytes 589832 | tf_op jit(solution)/shard_map/ppermute | solution.py:277
  222.3 15.2 %collective-permute-start.34 = (f32[6,32,256]{2,1,0:T(8,128)S(1)}, f32[6,32,256]{2,1,0:T(8,128)S(1)}, u32[]{:S(2)}, u32[]{:S(2)}) collective-permute-start(f32[6,32,256]{2,1,0:T(8,128)S(1)} %get-tuple-element.109), channel_id=1, source_target_pairs={{0,8},{1,9},{2,10},{3,11},{4,12},{5,13},{6,14},{7,15},{8,0},{9,1},... | collective-permute-start | bytes 589832 | tf_op jit(solution)/shard_map/ppermute | solution.py:277
  222.5 14.9 %collective-permute-start.35 = (f32[6,32,256]{2,1,0:T(8,128)S(1)}, f32[6,32,256]{2,1,0:T(8,128)S(1)}, u32[]{:S(2)}, u32[]{:S(2)}) collective-permute-start(f32[6,32,256]{2,1,0:T(8,128)S(1)} %get-tuple-element.110), channel_id=1, source_target_pairs={{0,4},{1,5},{2,6},{3,7},{4,0},{5,1},{6,2},{7,3},{8,12},{9,13},{10,... | collective-permute-start | bytes 589832 | tf_op jit(solution)/shard_map/ppermute | solution.py:277
  226.8 15.2 %collective-permute-start.70 = (f32[6,32,256]{2,1,0:T(8,128)S(1)}, f32[6,32,256]{2,1,0:T(8,128)S(1)}, u32[]{:S(2)}, u32[]{:S(2)}) collective-permute-start(f32[6,32,256]{2,1,0:T(8,128)S(1)} %get-tuple-element.145), channel_id=1, source_target_pairs={{0,8},{1,9},{2,10},{3,11},{4,12},{5,13},{6,14},{7,15},{8,0},{9,1},... | collective-permute-start | bytes 589832 | tf_op jit(solution)/shard_map/ppermute | solution.py:277
  228.2 14.0 %collective-permute-start.71 = (f32[6,32,256]{2,1,0:T(8,128)S(1)}, f32[6,32,256]{2,1,0:T(8,128)S(1)}, u32[]{:S(2)}, u32[]{:S(2)}) collective-permute-start(f32[6,32,256]{2,1,0:T(8,128)S(1)} %get-tuple-element.146), channel_id=1, source_target_pairs={{0,4},{1,5},{2,6},{3,7},{4,0},{5,1},{6,2},{7,3},{8,12},{9,13},{10,... | collective-permute-start | bytes 589832 | tf_op jit(solution)/shard_map/ppermute | solution.py:277
  (75 other events, 649.0 us)

commit v2 on v0

v2 whole, which is shorter than its diff:
```python
import functools

import jax
import jax.numpy as jnp
from jax import lax
from jax.experimental import pallas as pl
from jax.experimental.pallas import tpu as pltpu
from jax.sharding import PartitionSpec as P

LEVELS = 3
CAP = 2
PLANE = 4
CHUNKS = 2
F32 = jnp.float32
BF16 = jnp.bfloat16
NT = (((1,), (1,)), ((), ()))
NN = (((1,), (0,)), ((), ()))
PARAMS = pltpu.CompilerParams(vmem_limit_bytes=16 * 1024 * 1024)


def low_bit(offset):
    return offset & -offset


def split(value):
    high = value.astype(BF16)
    return high, (value - high.astype(F32)).astype(BF16)


def product(panel, high, low, dims):
    rows = panel.shape[0]
    panel_high, panel_low = split(panel)
    both = lax.dot_general(
        jnp.concatenate([panel_high, panel_low], axis=0), high, dims, preferred_element_type=F32
    )
    cross = lax.dot_general(panel_high, low, dims, preferred_element_type=F32)
    return both[:rows] + (both[rows:] + cross)


def line_offsets(depth):
    whole = tuple(offset for offset in range(depth) if offset % 2 == 0 or offset == 1)
    return whole, tuple(offset for offset in range(depth) if offset not in whole)


def lookup(values, index):
    hits = index[..., None] == jnp.arange(len(values))
    return jnp.sum(jnp.where(hits, jnp.array(values, jnp.int32), 0), axis=-1)


def tables(dev_rows, slot_rows, members, position):
    levels, rows, fanout = dev_rows.shape
    blocks_dev = rows // members
    width = blocks_dev * fanout
    depth = members // PLANE
    whole, listed = line_offsets(depth)
    height, place = position // PLANE, position % PLANE
    flips = jnp.arange(PLANE)

    def plane_rows(table, at):
        table = table.reshape(levels, members, width)
        return lax.dynamic_slice_in_dim(table, at * PLANE, PLANE, axis=1)

    lists = jnp.stack([plane_rows(dev_rows, height), plane_rows(dev_rows, height ^ 1)])
    slots = jnp.stack([plane_rows(slot_rows, height), plane_rows(slot_rows, height ^ 1)])
    positions = jnp.arange(width)
    earlier = positions[None, :] < positions[:, None]
    matches = lists[..., :, None] == lists[..., None, :]
    rank = jnp.sum(jnp.logical_and(matches, earlier), axis=-1, dtype=jnp.int32)
    code = lists * CAP + rank
    pick = (flips[:, None] ^ place) == flips[None, :]

    def asked(readers, offsets):
        owners = (height ^ jnp.array(offsets, jnp.int32)) * PLANE + place
        wanted = (owners[:, None] * CAP + jnp.arange(CAP)[None, :]).reshape(len(offsets) * CAP)
        found = code[readers][:, :, None, :] == wanted[None, None, :, None]
        by_place = jnp.sum(jnp.where(found, slots[readers][:, :, None, :] + 1, 0), axis=3) - 1
        by_flip = jnp.sum(jnp.where(pick[None, :, :, None], by_place[:, None], 0), axis=2)
        return by_flip.reshape(levels, PLANE * len(offsets) * CAP)

    plane = asked(0, whole)
    beyond = asked(1, tuple(offset ^ 1 for offset in listed))
    mine = (flips == place)[None, :, None]
    own_dev = jnp.sum(jnp.where(mine, lists[0], 0), axis=1)
    own_slot = jnp.sum(jnp.where(mine, slots[0], 0), axis=1)
    own_rank = jnp.sum(jnp.where(mine, rank[0], 0), axis=1)
    flip = (own_dev % PLANE) ^ place
    offset = (own_dev // PLANE) ^ height
    spot = lookup([whole.index(o) if o in whole else listed.index(o) for o in range(depth)], offset)
    is_whole = lookup([int(o in whole) for o in range(depth)], offset) == 1
    moved = len(whole) * blocks_dev
    far = moved + (PLANE - 1) * len(whole) * CAP
    fetch = jnp.where(
        is_whole,
        jnp.where(
            flip == 0,
            spot * blocks_dev + own_slot,
            moved + ((flip - 1) * len(whole) + spot) * CAP + own_rank,
        ),
        far + (flip * len(listed) + spot) * CAP + own_rank,
    )
    put = (flip * depth + offset) * CAP + own_rank
    return plane, beyond, fetch, put


VMEM_SPEC = pl.BlockSpec(memory_space=pltpu.VMEM)


def halves_kernel(*refs, streams, count):
    step = pl.program_id(0)
    for stream in range(streams):
        high, low = split(refs[stream][...])
        refs[streams][pl.ds((stream * count + step) * high.shape[0], high.shape[0])] = high
        refs[streams + 1][pl.ds((stream * count + step) * high.shape[0], high.shape[0])] = low


def halves(matrices, level, streams, width):
    points = matrices.shape[-1]
    matrices = matrices.reshape(matrices.shape[0], -1, points, points)
    total = matrices.shape[1]
    count = total // (streams * width)
    shape = pltpu.VMEM((total, points, points), BF16)
    specs = [
        pl.BlockSpec((None, width, points, points), lambda step, stream=stream: (level, stream * count + step, 0, 0))
        for stream in range(streams)
    ]
    return pl.pallas_call(
        functools.partial(halves_kernel, streams=streams, count=count),
        out_shape=[shape, shape],
        grid=(count,),
        in_specs=specs,
        out_specs=[VMEM_SPEC, VMEM_SPEC],
        compiler_params=PARAMS,
    )(*[pltpu.with_memory_space_constraint(matrices, pltpu.HBM)] * streams)


def first_kernel(probe_ref, inverse_ref, forward_ref):
    forward_ref[...] = product(probe_ref[...], *split(inverse_ref[...]), NT)


def first(probes, inverses, chunk):
    blocks, rows, points = probes.shape[1], probes.shape[2] // CHUNKS, probes.shape[3]
    return pl.pallas_call(
        first_kernel,
        out_shape=jax.ShapeDtypeStruct((blocks, rows, points), F32),
        grid=(blocks,),
        in_specs=[
            pl.BlockSpec((None, None, rows, points), lambda g: (0, g, chunk, 0)),
            pl.BlockSpec((None, None, points, points), lambda g: (0, g, 0, 0)),
        ],
        out_specs=pl.BlockSpec((None, rows, points), lambda g: (g, 0, 0)),
        compiler_params=PARAMS,
    )(*[pltpu.with_memory_space_constraint(array, pltpu.HBM) for array in (probes, inverses)])


def solve_kernel(*refs, has_fetch, has_left, has_parts, whole, listed, blocks, fanout, adds):
    refs = list(refs)

    def take(count):
        taken, refs[:count] = refs[:count], []
        return taken

    fetch_ref, put_ref, panel_ref = take(3)
    inverse_refs = take(2)
    in_refs = take(2) if has_fetch else None
    back_refs = (in_refs if has_fetch else take(2)) if has_parts else None
    sums = []
    if has_fetch:
        local_refs = take(len(whole))
        moved_refs = take(PLANE - 1)
        far_refs = take(PLANE)
    else:
        sums = take(adds)
    (out_ref,) = take(1)
    if has_parts:
        near_parts, far_parts = take(PLANE), take(PLANE)
    pan_ref = take(1)[0] if has_fetch else None
    hold_ref = take(1)[0] if has_parts else None
    if has_fetch:
        start = 0
        for ref in local_refs:
            pan_ref[pl.ds(start, blocks)] = ref[...]
            start += blocks
        for ref, offsets in [(ref, whole) for ref in moved_refs] + [(ref, listed) for ref in far_refs]:
            for place in range(len(offsets)):
                pan_ref[pl.ds(start, CAP)] = ref[place]
                start += CAP

    for g in range(blocks):
        inverse = [ref[g] for ref in inverse_refs]
        if has_fetch:
            value = panel_ref[g]
            for k in range(fanout):
                coupling = [ref[g * fanout + k] for ref in in_refs]
                value = value - product(pan_ref[fetch_ref[g * fanout + k]], *coupling, NT)
            value = product(value, *inverse, NT)
        else:
            value = panel_ref[g]
            for ref in sums:
                value = value - ref[g]
        if has_left:
            value = product(value, *inverse, NN)
        out_ref[g] = value
        if has_parts:
            for k in range(fanout):
                coupling = [ref[g * fanout + k] for ref in back_refs]
                hold_ref[put_ref[g * fanout + k]] = product(value, *coupling, NN)

    if has_parts:
        depth = len(whole) + len(listed)
        for flip in range(PLANE):
            for part_refs, offsets in ((near_parts, whole), (far_parts, listed)):
                for place, offset in enumerate(offsets):
                    part_refs[flip][place] = hold_ref[pl.ds((flip * depth + offset) * CAP, CAP)]


def solve(fetch, put, panel, inverse, coupling, whole, listed, held=None, moved=None, far=None, sums=None, left=False):
    blocks, rows, points = panel.shape
    has_fetch = held is not None
    has_parts = left and coupling is not None
    fanout = coupling[0].shape[0] // blocks if coupling is not None else 0
    operands = [panel, *inverse, *(coupling if coupling is not None else [])]
    operands = [operands[0]] + [pltpu.with_memory_space_constraint(array, pltpu.VMEM) for array in operands[1:]]
    operands += [*held, *moved, *far] if has_fetch else sums
    out_shapes = [jax.ShapeDtypeStruct((blocks, rows, points), F32)]
    scratch = []
    if has_fetch:
        slots = len(whole) * blocks + ((PLANE - 1) * len(whole) + PLANE * len(listed)) * CAP
        scratch.append(pltpu.VMEM((slots, rows, points), F32))
    if has_parts:
        for offsets in (whole, listed):
            out_shapes += [jax.ShapeDtypeStruct((len(offsets), CAP, rows, points), F32)] * PLANE
        scratch.append(pltpu.VMEM((PLANE * (len(whole) + len(listed)) * CAP, rows, points), F32))
    kernel = functools.partial(
        solve_kernel, has_fetch=has_fetch, has_left=left, has_parts=has_parts, whole=whole, listed=listed,
        blocks=blocks, fanout=fanout, adds=0 if has_fetch else len(sums),
    )
    results = pl.pallas_call(
        kernel,
        out_shape=out_shapes,
        grid_spec=pltpu.PrefetchScalarGridSpec(
            num_scalar_prefetch=2, grid=(), in_specs=[VMEM_SPEC] * len(operands),
            out_specs=[VMEM_SPEC] * len(out_shapes), scratch_shapes=scratch,
        ),
        compiler_params=PARAMS,
    )(fetch, put, *operands)
    return results[0], results[1 : 1 + PLANE], results[1 + PLANE :]


def pack_kernel(plane_ref, beyond_ref, *refs, whole, listed):
    sources = dict(zip(whole, refs))
    moved, far = refs[len(whole) : len(whole) + PLANE - 1], refs[len(whole) + PLANE - 1 :]

    def copy(table_ref, row, target, place, rank, source):
        slot = jnp.maximum(table_ref[row * CAP + rank], 0)
        target[place, rank] = source[slot]

    for flip in range(PLANE):
        for rank in range(CAP):
            for place, offset in enumerate(whole):
                if flip:
                    copy(plane_ref, flip * len(whole) + place, moved[flip - 1], place, rank, sources[offset])
            for place, offset in enumerate(listed):
                copy(beyond_ref, flip * len(listed) + place, far[flip], place, rank, sources[offset ^ 1])


def pack(plane, beyond, held, whole, listed):
    rows, points = held[0].shape[1:]
    near_shape = jax.ShapeDtypeStruct((len(whole), CAP, rows, points), F32)
    far_shape = jax.ShapeDtypeStruct((len(listed), CAP, rows, points), F32)
    results = pl.pallas_call(
        functools.partial(pack_kernel, whole=whole, listed=listed),
        out_shape=[near_shape] * (PLANE - 1) + [far_shape] * PLANE,
        grid_spec=pltpu.PrefetchScalarGridSpec(
            num_scalar_prefetch=2, grid=(), in_specs=[VMEM_SPEC] * len(whole), out_specs=[VMEM_SPEC] * (2 * PLANE - 1)
        ),
        compiler_params=PARAMS,
    )(plane, beyond, *held)
    return results[: PLANE - 1], results[PLANE - 1 :]


def gather_kernel(plane_ref, beyond_ref, *refs, whole, listed):
    near_parts, far_parts = refs[:PLANE], refs[PLANE : 2 * PLANE]
    targets = dict(zip(whole, refs[2 * PLANE :]))
    for target in targets.values():
        target[...] = jnp.zeros(target.shape, F32)

    def add(slot, target, source, place, rank):
        @pl.when(slot >= 0)
        def _():
            target[slot] = target[slot] + source[place, rank]

    for flip in range(PLANE):
        for rank in range(CAP):
            for place, offset in enumerate(whole):
                slot = plane_ref[(flip * len(whole) + place) * CAP + rank]
                add(slot, targets[offset], near_parts[flip], place, rank)
            for place, offset in enumerate(listed):
                slot = beyond_ref[(flip * len(listed) + place) * CAP + rank]
                add(slot, targets[offset ^ 1], far_parts[flip], place, rank)


def gather_sums(plane, beyond, near_parts, far_parts, whole, listed, blocks):
    rows, points = near_parts[0].shape[2:]
    operands = [*near_parts, *far_parts]
    return pl.pallas_call(
        functools.partial(gather_kernel, whole=whole, listed=listed),
        out_shape=[jax.ShapeDtypeStruct((blocks, rows, points), F32)] * len(whole),
        grid_spec=pltpu.PrefetchScalarGridSpec(
            num_scalar_prefetch=2, grid=(), in_specs=[VMEM_SPEC] * len(operands), out_specs=[VMEM_SPEC] * len(whole)
        ),
        compiler_params=PARAMS,
    )(plane, beyond, *operands)


def flip_move(array, bits):
    members = lax.axis_size("blk")
    return lax.ppermute(array, "blk", [(source, source ^ bits) for source in range(members)])


def local(probes, inverses, couplings, neighbour_devices, neighbour_slots):
    members = lax.axis_size("blk")
    position = lax.axis_index("blk")
    blocks = probes.shape[1]
    depth = members // PLANE
    whole, listed = line_offsets(depth)
    plane, beyond, fetch, put = tables(neighbour_devices, neighbour_slots, members, position)
    travel = sorted(whole[1:], key=lambda offset: (offset.bit_count(), -offset))

    def spread(panels, level):
        held = {0: panels}
        for offset in travel:
            bit = low_bit(offset)
            held[offset] = flip_move(held[offset ^ bit], bit * PLANE)
        held = [held[offset] for offset in whole]
        moved, far = pack(plane[level], beyond[level], held, whole, listed)
        moved = [flip_move(array, flip) for flip, array in enumerate(moved, 1)]
        far = [flip_move(array, PLANE | flip) for flip, array in enumerate(far)]
        return dict(held=held, moved=moved, far=far)

    def collect(near_parts, far_parts, level):
        near_parts = [near_parts[0]] + [flip_move(near_parts[flip], flip) for flip in range(1, PLANE)]
        far_parts = [flip_move(array, PLANE | flip) for flip, array in enumerate(far_parts)]
        sums = gather_sums(plane[level], beyond[level], near_parts, far_parts, whole, listed, blocks)
        sums = {offset: [array] for offset, array in zip(whole, sums)}
        for offset in travel[::-1]:
            bit = low_bit(offset)
            sums[offset ^ bit].append(flip_move(sum(sums[offset][1:], sums[offset][0]), bit * PLANE))
        return sums[0]

    chunks = range(CHUNKS)
    rows = probes.shape[2] // CHUNKS
    panels = [first(probes, inverses, chunk) for chunk in chunks]
    coupling = [halves(couplings, level, 4, 2) for level in range(LEVELS - 1)]
    inverse = [halves(inverses, level, 2, 1) for level in range(LEVELS)]
    call = functools.partial(solve, whole=whole, listed=listed)
    columns = []
    for chunk in chunks:
        forward = [panels[chunk]]
        solved = [None] * LEVELS
        for level in range(1, LEVELS):
            result, *parts = call(
                fetch[level - 1], put[level - 1], probes[level, :, chunk * rows : (chunk + 1) * rows],
                inverse[level], coupling[level - 1], **spread(forward[-1], level - 1), left=level == LEVELS - 1,
            )
            forward.append(result)
        solved[LEVELS - 1] = forward.pop()
        for level in range(LEVELS - 2, -1, -1):
            below = max(level - 1, 0)
            solved[level], *parts = call(
                fetch[below], put[below], forward[level], inverse[level], coupling[below] if level else None,
                sums=collect(*parts, level), left=True,
            )
        columns.append(jnp.stack(solved))
    return jnp.concatenate(columns, axis=2)


def solution(mesh):
    return jax.shard_map(
        local,
        mesh=mesh,
        in_specs=(
            P(None, ("grp", "blk"), None, None),
            P(None, ("grp", "blk"), None, None),
            P(None, ("grp", "blk"), None, None, None),
            P(None, "grp", None),
            P(None, "grp", None),
        ),
        out_specs=P(None, ("grp", "blk"), None, None),
        check_vma=False,
    )
```

time: 371 us -> 202 us (0.54)
  waiting for transfers between devices: 258 us -> 54.7 us
  Pallas kernels: 0 us -> 63.2 us
  matrix products: 54.7 us -> 0 us
  starting transfers between devices: 18.9 us -> 69.5 us
  between operations: 13.6 us -> 0.77 us
  local copies, waits for them, and re-layouts: 22.7 us -> 10.2 us
    reduce_scatter x2 -> x0, waiting for transfers between devices: 176 us -> none  [local(): lax.psum_scatter(summed.reshape(blocks_dev * lax.axis_size('blk'), probe_...]
    all_to_all x2 -> x0, waiting for transfers between devices: 81.7 us -> none  [local(): lax.all_to_all(outgoing, 'blk', split_axis=0, concat_axis=0, tiled=True)]
    ppermute x0 -> x72, starting transfers between devices: none -> 69.5 us  [flip_move(): lax.ppermute(array, 'blk', [(source, source ^ bits) for source in range(m...]
    pallas_call x0 -> x23, Pallas kernels: none -> 63.2 us  [the longest x8 32.1 us: solve(): pl.pallas_call(kernel, out_shape=out_shapes, grid_spec=pltpu.PrefetchScal...]
    dot_general x12 -> x0, matrix products: 54.7 us -> none  [the longest x2 18.8 us: local(): jnp.einsum('bkpi,bkji->bpj', fetched, couplings[height - 1], precision=la...]
    ppermute x0 -> x72, waiting for transfers between devices: none -> 54.7 us  [flip_move(): lax.ppermute(array, 'blk', [(source, source ^ bits) for source in range(m...]
    all_to_all x2 -> x0, starting transfers between devices: 18.6 us -> none  [local(): lax.all_to_all(outgoing, 'blk', split_axis=0, concat_axis=0, tiled=True)]
    dot_general x2 -> x0, local copies, waits for them, and re-layouts: 12.6 us -> none  [local(): summed = jnp.dot(selector, partials, precision=lax.Precision.HIGHEST)]
  transfers between devices with their start and end apart: 4 -> 72, of which waited for: 4 -> 29; matrix products, arithmetic and copies ran while one was open for 0% -> 5% of each run, Pallas kernels for 0% -> 29%
where the time goes in v2:
time: 202 us; the launch traced here: 201 us
  starting transfers between devices  69.5 us (34%)
  Pallas kernels  63.2 us (31%)
  waiting for transfers between devices  54.7 us (27%)
  local copies, waits for them, and re-layouts  10.2 us (5%)
  other arithmetic  2.79 us (1%)
    ppermute x72, starting transfers between devices, flip_move(): lax.ppermute(array, 'blk', [(source, source ^ bits) for source in range(m...  69.5 us
    ppermute x72, waiting for transfers between devices, flip_move(): lax.ppermute(array, 'blk', [(source, source ^ bits) for source in range(m...  54.7 us
    pallas_call x8, Pallas kernels, solve(): pl.pallas_call(kernel, out_shape=out_shapes, grid_spec=pltpu.PrefetchScal...  32.1 us
    pallas_call x5, Pallas kernels, halves(): pl.pallas_call(functools.partial(halves_kernel, streams=streams, count=co...  15.5 us
    pallas_call x2, Pallas kernels, first(): pl.pallas_call(first_kernel, out_shape=jax.ShapeDtypeStruct((blocks, rows...  7.58 us
    pallas_call x4, Pallas kernels, pack(): pl.pallas_call(functools.partial(pack_kernel, whole=whole, listed=listed)...  4.63 us
  transfers between devices with their start and end apart: 72, of which 29 were waited for; matrix products, arithmetic and copies ran while one was open for 5% of the time, Pallas kernels for 29%

profile of v2, /device:TPU:0, one launch (start us, length us, event | category | flops | bytes accessed | tf_op | source)
XLA Modules:
  0.0 201.1 jit_solution(9918953772094833088)
XLA Ops:
  0.0 3.8 %shard_map.91.refs_0_.refs_7_.refs_2_ = f32[6,32,256]{2,1,0:T(8,128)S(1)} custom-call(f32[3,6,64,256]{3,2,1,0:T(8,128)} %probe_ref.3, f32[3,6,256,256]{3,2,1,0:T(8,128)} %inverse_ref.3), custom_call_target="tpu_custom_call" | custom-call | tf_op jit(solution)/shard_map/pallas_call | solution.py:142
  3.8 3.1 %collective-permute-start = (f32[6,32,256]{2,1,0:T(8,128)S(1)}, f32[6,32,256]{2,1,0:T(8,128)S(1)}, u32[]{:S(2)}, u32[]{:S(2)}) collective-permute-start(f32[6,32,256]{2,1,0:T(8,128)S(1)} %shard_map.91.refs_0_.refs_7_.refs_2_), channel_id=1, source_target_pairs={{0,4},{1,5},{2,6},{3,7},{4,0},{5,1},{6,2},{7,3},{8,12},{9,13},{10,... | collective-permute-start | bytes 589832 | tf_op jit(solution)/shard_map/ppermute | solution.py:317
  6.9 2.6 %collective-permute-start.1 = (f32[6,32,256]{2,1,0:T(8,128)S(1)}, f32[6,32,256]{2,1,0:T(8,128)S(1)}, u32[]{:S(2)}, u32[]{:S(2)}) collective-permute-start(f32[6,32,256]{2,1,0:T(8,128)S(1)} %shard_map.91.refs_0_.refs_7_.refs_2_), channel_id=1, source_target_pairs={{0,8},{1,9},{2,10},{3,11},{4,12},{5,13},{6,14},{7,15},{8,0},{9,1},... | collective-permute-start | bytes 589832 | tf_op jit(solution)/shard_map/ppermute | solution.py:317
  9.5 3.8 %shard_map.105.refs_0_.refs_7_.refs_2_ = f32[6,32,256]{2,1,0:T(8,128)S(1)} custom-call(f32[3,6,64,256]{3,2,1,0:T(8,128)} %probe_ref.3, f32[3,6,256,256]{3,2,1,0:T(8,128)} %inverse_ref.3), custom_call_target="tpu_custom_call" | custom-call | tf_op jit(solution)/shard_map/pallas_call | solution.py:142
  19.2 2.0 collective-permute-start.5
  22.6 2.9 %collective-permute-done.36.refs_1_.refs_8_ = f32[6,32,256]{2,1,0:T(8,128)S(1)} collective-permute-done((f32[6,32,256]{2,1,0:T(8,128)S(1)}, f32[6,32,256]{2,1,0:T(8,128)S(1)}, u32[]{:S(2)}, u32[]{:S(2)}) %collective-permute-start.36) | collective-permute-done | bytes 196640 | tf_op jit(solution)/shard_map/ppermute | solution.py:317
  30.2 1.9 collective-permute-start.41
  32.3 2.1 %collective-permute-done.41.refs_13_ = f32[1,2,32,256]{3,2,1,0:T(8,128)S(1)} collective-permute-done((f32[1,2,32,256]{3,2,1,0:T(8,128)S(1)}, f32[1,2,32,256]{3,2,1,0:T(8,128)S(1)}, u32[]{:S(2)}, u32[]{:S(2)}) %collective-permute-start.41) | collective-permute-done | bytes 65568 | tf_op jit(solution)/shard_map/ppermute | solution.py:317
  37.0 2.1 %collective-permute-start.43 = (f32[1,2,32,256]{3,2,1,0:T(8,128)S(1)}, f32[1,2,32,256]{3,2,1,0:T(8,128)S(1)}, u32[]{:S(2)}, u32[]{:S(2)}) collective-permute-start(f32[1,2,32,256]{3,2,1,0:T(8,128)S(1)} %get-tuple-element.144), channel_id=1, source_target_pairs={{0,6},{1,7},{2,4},{3,5},{4,2},{5,3},{6,0},{7,1},{8,14},{9,15},{10,... | collective-permute-start | bytes 196616 | tf_op jit(solution)/shard_map/ppermute | solution.py:317
  42.0 2.3 %shard_map.93 = (bf16[6,256,256]{2,1,0:T(8,128)(2,1)S(1)}, bf16[6,256,256]{2,1,0:T(8,128)(2,1)S(1)}) custom-call(f32[3,6,256,256]{3,2,1,0:T(8,128)} %inverse_ref.3, f32[3,6,256,256]{3,2,1,0:T(8,128)} %inverse_ref.3), custom_call_target="tpu_custom_call" | custom-call | tf_op jit(solution)/shard_map/pallas_call | solution.py:126
  44.4 4.5 %shard_map.94 = (bf16[24,256,256]{2,1,0:T(8,128)(2,1)S(1)}, bf16[24,256,256]{2,1,0:T(8,128)(2,1)S(1)}) custom-call(f32[2,24,256,256]{3,2,1,0:T(8,128)} %bitcast.43, f32[2,24,256,256]{3,2,1,0:T(8,128)} %bitcast.44, f32[2,24,256,256]{3,2,1,0:T(8,128)} %bitcast.45, f32[2,24,256,256]{3,2,1,0:T(8,128)} %bitcast.46), custom_call_target="tpu_custom_call" | custom-call | tf_op jit(solution)/shard_map/pallas_call | solution.py:126
  49.0 4.2 %shard_map.96.refs_0_.refs_7_.refs_2_ = f32[6,32,256]{2,1,0:T(8,128)} custom-call(s32[24]{0:T(128)S(1)} %get-tuple-element.206.refs_0_, s32[24]{0:T(128)S(1)} %get-tuple-element.201.refs_1_, f32[6,32,256]{2,1,0:T(8,128)S(1)} %copy-done.9, bf16[6,256,256]{2,1,0:T(8,128)(2,1)S(1)} %get-tuple-element.93.refs_3_, ...), custom_call_target="tpu_custom_call" | custom-call | tf_op jit(solution)/shard_map/pallas_call | solution.py:237
  53.2 2.3 %collective-permute-start.10 = (f32[6,32,256]{2,1,0:T(8,128)}, f32[6,32,256]{2,1,0:T(8,128)}, u32[]{:S(2)}, u32[]{:S(2)}) collective-permute-start(f32[6,32,256]{2,1,0:T(8,128)} %shard_map.96.refs_0_.refs_7_.refs_2_), channel_id=1, source_target_pairs={{0,8},{1,9},{2,10},{3,11},{4,12},{5,13},{6,14},{7,15},{8,0},{9,1},... | collective-permute-start | bytes 589832 | tf_op jit(solution)/shard_map/ppermute | solution.py:317
  56.6 4.2 %shard_map.107.refs_0_.refs_7_.refs_2_ = f32[6,32,256]{2,1,0:T(8,128)} custom-call(s32[24]{0:T(128)S(1)} %get-tuple-element.206.refs_0_, s32[24]{0:T(128)S(1)} %get-tuple-element.201.refs_1_, f32[6,32,256]{2,1,0:T(8,128)S(1)} %copy-done.8, bf16[6,256,256]{2,1,0:T(8,128)(2,1)S(1)} %get-tuple-element.93.refs_3_, ...), custom_call_target="tpu_custom_call" | custom-call | tf_op jit(solution)/shard_map/pallas_call | solution.py:237
  66.3 5.4 %collective-permute-done.9.refs_1_.refs_8_ = f32[6,32,256]{2,1,0:T(8,128)} collective-permute-done((f32[6,32,256]{2,1,0:T(8,128)}, f32[6,32,256]{2,1,0:T(8,128)}, u32[]{:S(2)}, u32[]{:S(2)}) %collective-permute-start.9) | collective-permute-done | bytes 196640 | tf_op jit(solution)/shard_map/ppermute | solution.py:317
  85.8 3.2 %collective-permute-done.50.refs_13_ = f32[1,2,32,256]{3,2,1,0:T(8,128)S(1)} collective-permute-done((f32[1,2,32,256]{3,2,1,0:T(8,128)S(1)}, f32[1,2,32,256]{3,2,1,0:T(8,128)S(1)}, u32[]{:S(2)}, u32[]{:S(2)}) %collective-permute-start.50) | collective-permute-done | bytes 65568 | tf_op jit(solution)/shard_map/ppermute | solution.py:317
  94.5 3.9 %shard_map.98 = (bf16[24,256,256]{2,1,0:T(8,128)(2,1)S(1)}, bf16[24,256,256]{2,1,0:T(8,128)(2,1)S(1)}) custom-call(f32[2,24,256,256]{3,2,1,0:T(8,128)} %bitcast.47, f32[2,24,256,256]{3,2,1,0:T(8,128)} %bitcast.48, f32[2,24,256,256]{3,2,1,0:T(8,128)} %bitcast.49, f32[2,24,256,256]{3,2,1,0:T(8,128)} %bitcast.50), custom_call_target="tpu_custom_call" | custom-call | tf_op jit(solution)/shard_map/pallas_call | solution.py:126
  98.4 2.5 %shard_map.97 = (bf16[6,256,256]{2,1,0:T(8,128)(2,1)S(1)}, bf16[6,256,256]{2,1,0:T(8,128)(2,1)S(1)}) custom-call(f32[3,6,256,256]{3,2,1,0:T(8,128)} %inverse_ref.3, f32[3,6,256,256]{3,2,1,0:T(8,128)} %inverse_ref.3), custom_call_target="tpu_custom_call" | custom-call | tf_op jit(solution)/shard_map/pallas_call | solution.py:126
  101.0 7.3 %shard_map.100 = (f32[6,32,256]{2,1,0:T(8,128)S(1)}, f32[3,2,32,256]{3,2,1,0:T(8,128)S(1)}, f32[3,2,32,256]{3,2,1,0:T(8,128)S(1)}, f32[3,2,32,256]{3,2,1,0:T(8,1...) custom-call(s32[24]{0:T(128)S(1)} %copy-done.25, ...), custom_call_target="tpu_custom_call" | custom-call | tf_op jit(solution)/shard_map/pallas_call | solution.py:237
  115.2 7.5 %shard_map.109 = (f32[6,32,256]{2,1,0:T(8,128)S(1)}, f32[3,2,32,256]{3,2,1,0:T(8,128)S(1)}, f32[3,2,32,256]{3,2,1,0:T(8,128)S(1)}, f32[3,2,32,256]{3,2,1,0:T(8,1...) custom-call(s32[24]{0:T(128)S(1)} %copy-done.25, ...), custom_call_target="tpu_custom_call" | custom-call | tf_op jit(solution)/shard_map/pallas_call | solution.py:237
  124.7 2.6 %collective-permute-done.57.refs_4_ = f32[1,2,32,256]{3,2,1,0:T(8,128)S(1)} collective-permute-done((f32[1,2,32,256]{3,2,1,0:T(8,128)S(1)}, f32[1,2,32,256]{3,2,1,0:T(8,128)S(1)}, u32[]{:S(2)}, u32[]{:S(2)}) %collective-permute-start.57) | collective-permute-done | bytes 65568 | tf_op jit(solution)/shard_map/ppermute | solution.py:317
  128.1 1.9 collective-permute-start.55
  135.3 2.2 %collective-permute-start.25 = (f32[6,32,256]{2,1,0:T(8,128)S(1)}, f32[6,32,256]{2,1,0:T(8,128)S(1)}, u32[]{:S(2)}, u32[]{:S(2)}) collective-permute-start(f32[6,32,256]{2,1,0:T(8,128)S(1)} %get-tuple-element.124), channel_id=1, source_target_pairs={{0,4},{1,5},{2,6},{3,7},{4,0},{5,1},{6,2},{7,3},{8,12},{9,13},{10,... | collective-permute-start | bytes 589832 | tf_op jit(solution)/shard_map/ppermute | solution.py:317
  138.7 3.1 %collective-permute-done.56.refs_3_ = f32[3,2,32,256]{3,2,1,0:T(8,128)S(1)} collective-permute-done((f32[3,2,32,256]{3,2,1,0:T(8,128)S(1)}, f32[3,2,32,256]{3,2,1,0:T(8,128)S(1)}, u32[]{:S(2)}, u32[]{:S(2)}) %collective-permute-start.56) | collective-permute-done | bytes 196640 | tf_op jit(solution)/shard_map/ppermute | solution.py:317
  144.2 6.2 %collective-permute-done.26.refs_9_ = f32[6,32,256]{2,1,0:T(8,128)S(1)} collective-permute-done((f32[6,32,256]{2,1,0:T(8,128)S(1)}, f32[6,32,256]{2,1,0:T(8,128)S(1)}, u32[]{:S(2)}, u32[]{:S(2)}) %collective-permute-start.26) | collective-permute-done | bytes 196640 | tf_op jit(solution)/shard_map/ppermute | solution.py:317
  150.4 3.6 %shard_map.102 = (f32[6,32,256]{2,1,0:T(8,128)S(1)}, f32[3,2,32,256]{3,2,1,0:T(8,128)S(1)}, f32[3,2,32,256]{3,2,1,0:T(8,128)S(1)}, f32[3,2,32,256]{3,2,1,0:T(8,1...) custom-call(s32[24]{0:T(128)S(1)} %get-tuple-element.206.refs_0_, ...), custom_call_target="tpu_custom_call" | custom-call | tf_op jit(solution)/shard_map/pallas_call | solution.py:237
  158.6 3.6 %shard_map.111 = (f32[6,32,256]{2,1,0:T(8,128)S(1)}, f32[3,2,32,256]{3,2,1,0:T(8,128)S(1)}, f32[3,2,32,256]{3,2,1,0:T(8,128)S(1)}, f32[3,2,32,256]{3,2,1,0:T(8,1...) custom-call(s32[24]{0:T(128)S(1)} %get-tuple-element.206.refs_0_, ...), custom_call_target="tpu_custom_call" | custom-call | tf_op jit(solution)/shard_map/pallas_call | solution.py:237
  165.7 2.6 %collective-permute-done.66.refs_4_ = f32[1,2,32,256]{3,2,1,0:T(8,128)S(1)} collective-permute-done((f32[1,2,32,256]{3,2,1,0:T(8,128)S(1)}, f32[1,2,32,256]{3,2,1,0:T(8,128)S(1)}, u32[]{:S(2)}, u32[]{:S(2)}) %collective-permute-start.66) | collective-permute-done | bytes 65568 | tf_op jit(solution)/shard_map/ppermute | solution.py:317
  181.2 3.3 %collective-permute-done.65.refs_3_ = f32[3,2,32,256]{3,2,1,0:T(8,128)S(1)} collective-permute-done((f32[3,2,32,256]{3,2,1,0:T(8,128)S(1)}, f32[3,2,32,256]{3,2,1,0:T(8,128)S(1)}, u32[]{:S(2)}, u32[]{:S(2)}) %collective-permute-start.65) | collective-permute-done | bytes 196640 | tf_op jit(solution)/shard_map/ppermute | solution.py:317
  187.2 2.3 %shard_map.92 = (bf16[6,256,256]{2,1,0:T(8,128)(2,1)S(1)}, bf16[6,256,256]{2,1,0:T(8,128)(2,1)S(1)}) custom-call(f32[3,6,256,256]{3,2,1,0:T(8,128)} %inverse_ref.3, f32[3,6,256,256]{3,2,1,0:T(8,128)} %inverse_ref.3), custom_call_target="tpu_custom_call" | custom-call | tf_op jit(solution)/shard_map/pallas_call | solution.py:126
  191.6 4.9 %collective-permute-done.70.refs_6_ = f32[6,32,256]{2,1,0:T(8,128)S(1)} collective-permute-done((f32[6,32,256]{2,1,0:T(8,128)S(1)}, f32[6,32,256]{2,1,0:T(8,128)S(1)}, u32[]{:S(2)}, u32[]{:S(2)}) %collective-permute-start.70) | collective-permute-done | bytes 196640 | tf_op jit(solution)/shard_map/ppermute | solution.py:317
  196.5 2.6 %collective-permute-done.71.refs_7_ = f32[6,32,256]{2,1,0:T(8,128)S(1)} collective-permute-done((f32[6,32,256]{2,1,0:T(8,128)S(1)}, f32[6,32,256]{2,1,0:T(8,128)S(1)}, u32[]{:S(2)}, u32[]{:S(2)}) %collective-permute-start.71) | collective-permute-done | bytes 196640 | tf_op jit(solution)/shard_map/ppermute | solution.py:317
  (236 shorter events, 89.9 us)
Async XLA Ops:
  3.8 14.8 %collective-permute-start = (f32[6,32,256]{2,1,0:T(8,128)S(1)}, f32[6,32,256]{2,1,0:T(8,128)S(1)}, u32[]{:S(2)}, u32[]{:S(2)}) collective-permute-start(f32[6,32,256]{2,1,0:T(8,128)S(1)} %shard_map.91.refs_0_.refs_7_.refs_2_), channel_id=1, source_target_pairs={{0,4},{1,5},{2,6},{3,7},{4,0},{5,1},{6,2},{7,3},{8,12},{9,13},{10,... | collective-permute-start | bytes 589832 | tf_op jit(solution)/shard_map/ppermute | solution.py:317
  13.3 12.1 %collective-permute-start.36 = (f32[6,32,256]{2,1,0:T(8,128)S(1)}, f32[6,32,256]{2,1,0:T(8,128)S(1)}, u32[]{:S(2)}, u32[]{:S(2)}) collective-permute-start(f32[6,32,256]{2,1,0:T(8,128)S(1)} %shard_map.105.refs_0_.refs_7_.refs_2_), channel_id=1, source_target_pairs={{0,4},{1,5},{2,6},{3,7},{4,0},{5,1},{6,2},{7,3},{8,12},{9,13},{10,... | collective-permute-start | bytes 589832 | tf_op jit(solution)/shard_map/ppermute | solution.py:317
  13.8 12.1 %collective-permute-start.37 = (f32[6,32,256]{2,1,0:T(8,128)S(1)}, f32[6,32,256]{2,1,0:T(8,128)S(1)}, u32[]{:S(2)}, u32[]{:S(2)}) collective-permute-start(f32[6,32,256]{2,1,0:T(8,128)S(1)} %shard_map.105.refs_0_.refs_7_.refs_2_), channel_id=1, source_target_pairs={{0,8},{1,9},{2,10},{3,11},{4,12},{5,13},{6,14},{7,15},{8,0},{9,1},... | collective-permute-start | bytes 589832 | tf_op jit(solution)/shard_map/ppermute | solution.py:317
  34.5 22.1 %collective-permute-start.38 = (f32[3,2,32,256]{3,2,1,0:T(8,128)S(1)}, f32[3,2,32,256]{3,2,1,0:T(8,128)S(1)}, u32[]{:S(2)}, u32[]{:S(2)}) collective-permute-start(f32[3,2,32,256]{3,2,1,0:T(8,128)S(1)} %get-tuple-element.139), channel_id=1, source_target_pairs={{0,1},{1,0},{2,3},{3,2},{4,5},{5,4},{6,7},{7,6},{8,9},{9,8},{10,11... | collective-permute-start | bytes 589832 | tf_op jit(solution)/shard_map/ppermute | solution.py:317
  35.9 20.7 %collective-permute-start.39 = (f32[3,2,32,256]{3,2,1,0:T(8,128)S(1)}, f32[3,2,32,256]{3,2,1,0:T(8,128)S(1)}, u32[]{:S(2)}, u32[]{:S(2)}) collective-permute-start(f32[3,2,32,256]{3,2,1,0:T(8,128)S(1)} %get-tuple-element.140), channel_id=1, source_target_pairs={{0,2},{1,3},{2,0},{3,1},{4,6},{5,7},{6,4},{7,5},{8,10},{9,11},{10,... | collective-permute-start | bytes 589832 | tf_op jit(solution)/shard_map/ppermute | solution.py:317
  37.0 19.6 %collective-permute-start.40 = (f32[3,2,32,256]{3,2,1,0:T(8,128)S(1)}, f32[3,2,32,256]{3,2,1,0:T(8,128)S(1)}, u32[]{:S(2)}, u32[]{:S(2)}) collective-permute-start(f32[3,2,32,256]{3,2,1,0:T(8,128)S(1)} %get-tuple-element.141), channel_id=1, source_target_pairs={{0,3},{1,2},{2,1},{3,0},{4,7},{5,6},{6,5},{7,4},{8,11},{9,10},{10,... | collective-permute-start | bytes 589832 | tf_op jit(solution)/shard_map/ppermute | solution.py:317
  37.0 16.1 %collective-permute-start.43 = (f32[1,2,32,256]{3,2,1,0:T(8,128)S(1)}, f32[1,2,32,256]{3,2,1,0:T(8,128)S(1)}, u32[]{:S(2)}, u32[]{:S(2)}) collective-permute-start(f32[1,2,32,256]{3,2,1,0:T(8,128)S(1)} %get-tuple-element.144), channel_id=1, source_target_pairs={{0,6},{1,7},{2,4},{3,5},{4,2},{5,3},{6,0},{7,1},{8,14},{9,15},{10,... | collective-permute-start | bytes 196616 | tf_op jit(solution)/shard_map/ppermute | solution.py:317
  39.5 15.9 %collective-permute-start.44 = (f32[1,2,32,256]{3,2,1,0:T(8,128)S(1)}, f32[1,2,32,256]{3,2,1,0:T(8,128)S(1)}, u32[]{:S(2)}, u32[]{:S(2)}) collective-permute-start(f32[1,2,32,256]{3,2,1,0:T(8,128)S(1)} %get-tuple-element.145), channel_id=1, source_target_pairs={{0,7},{1,6},{2,5},{3,4},{4,3},{5,2},{6,1},{7,0},{8,15},{9,14},{10,... | collective-permute-start | bytes 196616 | tf_op jit(solution)/shard_map/ppermute | solution.py:317
  53.2 13.2 %collective-permute-start.10 = (f32[6,32,256]{2,1,0:T(8,128)}, f32[6,32,256]{2,1,0:T(8,128)}, u32[]{:S(2)}, u32[]{:S(2)}) collective-permute-start(f32[6,32,256]{2,1,0:T(8,128)} %shard_map.96.refs_0_.refs_7_.refs_2_), channel_id=1, source_target_pairs={{0,8},{1,9},{2,10},{3,11},{4,12},{5,13},{6,14},{7,15},{8,0},{9,1},... | collective-permute-start | bytes 589832 | tf_op jit(solution)/shard_map/ppermute | solution.py:317
  55.5 16.3 %collective-permute-start.9 = (f32[6,32,256]{2,1,0:T(8,128)}, f32[6,32,256]{2,1,0:T(8,128)}, u32[]{:S(2)}, u32[]{:S(2)}) collective-permute-start(f32[6,32,256]{2,1,0:T(8,128)} %shard_map.96.refs_0_.refs_7_.refs_2_), channel_id=1, source_target_pairs={{0,4},{1,5},{2,6},{3,7},{4,0},{5,1},{6,2},{7,3},{8,12},{9,13},{10,... | collective-permute-start | bytes 589832 | tf_op jit(solution)/shard_map/ppermute | solution.py:317
  60.8 15.8 %collective-permute-start.45 = (f32[6,32,256]{2,1,0:T(8,128)}, f32[6,32,256]{2,1,0:T(8,128)}, u32[]{:S(2)}, u32[]{:S(2)}) collective-permute-start(f32[6,32,256]{2,1,0:T(8,128)} %shard_map.107.refs_0_.refs_7_.refs_2_), channel_id=1, source_target_pairs={{0,4},{1,5},{2,6},{3,7},{4,0},{5,1},{6,2},{7,3},{8,12},{9,13},{10,... | collective-permute-start | bytes 589832 | tf_op jit(solution)/shard_map/ppermute | solution.py:317
  61.7 15.9 %collective-permute-start.46 = (f32[6,32,256]{2,1,0:T(8,128)}, f32[6,32,256]{2,1,0:T(8,128)}, u32[]{:S(2)}, u32[]{:S(2)}) collective-permute-start(f32[6,32,256]{2,1,0:T(8,128)} %shard_map.107.refs_0_.refs_7_.refs_2_), channel_id=1, source_target_pairs={{0,8},{1,9},{2,10},{3,11},{4,12},{5,13},{6,14},{7,15},{8,0},{9,1},... | collective-permute-start | bytes 589832 | tf_op jit(solution)/shard_map/ppermute | solution.py:317
  74.7 15.8 %collective-permute-start.11 = (f32[3,2,32,256]{3,2,1,0:T(8,128)S(1)}, f32[3,2,32,256]{3,2,1,0:T(8,128)S(1)}, u32[]{:S(2)}, u32[]{:S(2)}) collective-permute-start(f32[3,2,32,256]{3,2,1,0:T(8,128)S(1)} %get-tuple-element.108), channel_id=1, source_target_pairs={{0,1},{1,0},{2,3},{3,2},{4,5},{5,4},{6,7},{7,6},{8,9},{9,8},{10,11... | collective-permute-start | bytes 589832 | tf_op jit(solution)/shard_map/ppermute | solution.py:317
  89.0 21.3 %collective-permute-start.47 = (f32[3,2,32,256]{3,2,1,0:T(8,128)S(1)}, f32[3,2,32,256]{3,2,1,0:T(8,128)S(1)}, u32[]{:S(2)}, u32[]{:S(2)}) collective-permute-start(f32[3,2,32,256]{3,2,1,0:T(8,128)S(1)} %get-tuple-element.146), channel_id=1, source_target_pairs={{0,1},{1,0},{2,3},{3,2},{4,5},{5,4},{6,7},{7,6},{8,9},{9,8},{10,11... | collective-permute-start | bytes 589832 | tf_op jit(solution)/shard_map/ppermute | solution.py:317
  89.3 21.1 %collective-permute-start.48 = (f32[3,2,32,256]{3,2,1,0:T(8,128)S(1)}, f32[3,2,32,256]{3,2,1,0:T(8,128)S(1)}, u32[]{:S(2)}, u32[]{:S(2)}) collective-permute-start(f32[3,2,32,256]{3,2,1,0:T(8,128)S(1)} %get-tuple-element.147), channel_id=1, source_target_pairs={{0,2},{1,3},{2,0},{3,1},{4,6},{5,7},{6,4},{7,5},{8,10},{9,11},{10,... | collective-permute-start | bytes 589832 | tf_op jit(solution)/shard_map/ppermute | solution.py:317
  90.5 21.7 %collective-permute-start.49 = (f32[3,2,32,256]{3,2,1,0:T(8,128)S(1)}, f32[3,2,32,256]{3,2,1,0:T(8,128)S(1)}, u32[]{:S(2)}, u32[]{:S(2)}) collective-permute-start(f32[3,2,32,256]{3,2,1,0:T(8,128)S(1)} %get-tuple-element.148), channel_id=1, source_target_pairs={{0,3},{1,2},{2,1},{3,0},{4,7},{5,6},{6,5},{7,4},{8,11},{9,10},{10,... | collective-permute-start | bytes 589832 | tf_op jit(solution)/shard_map/ppermute | solution.py:317
  91.3 16.9 %collective-permute-start.52 = (f32[1,2,32,256]{3,2,1,0:T(8,128)S(1)}, f32[1,2,32,256]{3,2,1,0:T(8,128)S(1)}, u32[]{:S(2)}, u32[]{:S(2)}) collective-permute-start(f32[1,2,32,256]{3,2,1,0:T(8,128)S(1)} %get-tuple-element.151), channel_id=1, source_target_pairs={{0,6},{1,7},{2,4},{3,5},{4,2},{5,3},{6,0},{7,1},{8,14},{9,15},{10,... | collective-permute-start | bytes 196616 | tf_op jit(solution)/shard_map/ppermute | solution.py:317
  93.3 15.1 %collective-permute-start.53 = (f32[1,2,32,256]{3,2,1,0:T(8,128)S(1)}, f32[1,2,32,256]{3,2,1,0:T(8,128)S(1)}, u32[]{:S(2)}, u32[]{:S(2)}) collective-permute-start(f32[1,2,32,256]{3,2,1,0:T(8,128)S(1)} %get-tuple-element.152), channel_id=1, source_target_pairs={{0,7},{1,6},{2,5},{3,4},{4,3},{5,2},{6,1},{7,0},{8,15},{9,14},{10,... | collective-permute-start | bytes 196616 | tf_op jit(solution)/shard_map/ppermute | solution.py:317
  108.3 21.8 %collective-permute-start.18 = (f32[3,2,32,256]{3,2,1,0:T(8,128)S(1)}, f32[3,2,32,256]{3,2,1,0:T(8,128)S(1)}, u32[]{:S(2)}, u32[]{:S(2)}) collective-permute-start(f32[3,2,32,256]{3,2,1,0:T(8,128)S(1)} %get-tuple-element.116), channel_id=1, source_target_pairs={{0,1},{1,0},{2,3},{3,2},{4,5},{5,4},{6,7},{7,6},{8,9},{9,8},{10,11... | collective-permute-start | bytes 589832 | tf_op jit(solution)/shard_map/ppermute | solution.py:317
  110.4 12.4 %collective-permute-start.23 = (f32[1,2,32,256]{3,2,1,0:T(8,128)S(1)}, f32[1,2,32,256]{3,2,1,0:T(8,128)S(1)}, u32[]{:S(2)}, u32[]{:S(2)}) collective-permute-start(f32[1,2,32,256]{3,2,1,0:T(8,128)S(1)} %get-tuple-element.121), channel_id=1, source_target_pairs={{0,6},{1,7},{2,4},{3,5},{4,2},{5,3},{6,0},{7,1},{8,14},{9,15},{10,... | collective-permute-start | bytes 196616 | tf_op jit(solution)/shard_map/ppermute | solution.py:317
  112.3 12.0 %collective-permute-start.24 = (f32[1,2,32,256]{3,2,1,0:T(8,128)S(1)}, f32[1,2,32,256]{3,2,1,0:T(8,128)S(1)}, u32[]{:S(2)}, u32[]{:S(2)}) collective-permute-start(f32[1,2,32,256]{3,2,1,0:T(8,128)S(1)} %get-tuple-element.122), channel_id=1, source_target_pairs={{0,7},{1,6},{2,5},{3,4},{4,3},{5,2},{6,1},{7,0},{8,15},{9,14},{10,... | collective-permute-start | bytes 196616 | tf_op jit(solution)/shard_map/ppermute | solution.py:317
  113.0 17.1 %collective-permute-start.19 = (f32[3,2,32,256]{3,2,1,0:T(8,128)S(1)}, f32[3,2,32,256]{3,2,1,0:T(8,128)S(1)}, u32[]{:S(2)}, u32[]{:S(2)}) collective-permute-start(f32[3,2,32,256]{3,2,1,0:T(8,128)S(1)} %get-tuple-element.117), channel_id=1, source_target_pairs={{0,2},{1,3},{2,0},{3,1},{4,6},{5,7},{6,4},{7,5},{8,10},{9,11},{10,... | collective-permute-start | bytes 589832 | tf_op jit(solution)/shard_map/ppermute | solution.py:317
  114.3 17.5 %collective-permute-start.20 = (f32[3,2,32,256]{3,2,1,0:T(8,128)S(1)}, f32[3,2,32,256]{3,2,1,0:T(8,128)S(1)}, u32[]{:S(2)}, u32[]{:S(2)}) collective-permute-start(f32[3,2,32,256]{3,2,1,0:T(8,128)S(1)} %get-tuple-element.118), channel_id=1, source_target_pairs={{0,3},{1,2},{2,1},{3,0},{4,7},{5,6},{6,5},{7,4},{8,11},{9,10},{10,... | collective-permute-start | bytes 589832 | tf_op jit(solution)/shard_map/ppermute | solution.py:317
  130.0 11.7 %collective-permute-start.56 = (f32[3,2,32,256]{3,2,1,0:T(8,128)S(1)}, f32[3,2,32,256]{3,2,1,0:T(8,128)S(1)}, u32[]{:S(2)}, u32[]{:S(2)}) collective-permute-start(f32[3,2,32,256]{3,2,1,0:T(8,128)S(1)} %get-tuple-element.156), channel_id=1, source_target_pairs={{0,3},{1,2},{2,1},{3,0},{4,7},{5,6},{6,5},{7,4},{8,11},{9,10},{10,... | collective-permute-start | bytes 589832 | tf_op jit(solution)/shard_map/ppermute | solution.py:317
  137.6 12.8 %collective-permute-start.26 = (f32[6,32,256]{2,1,0:T(8,128)S(1)}, f32[6,32,256]{2,1,0:T(8,128)S(1)}, u32[]{:S(2)}, u32[]{:S(2)}) collective-permute-start(f32[6,32,256]{2,1,0:T(8,128)S(1)} %get-tuple-element.125), channel_id=1, source_target_pairs={{0,8},{1,9},{2,10},{3,11},{4,12},{5,13},{6,14},{7,15},{8,0},{9,1},... | collective-permute-start | bytes 589832 | tf_op jit(solution)/shard_map/ppermute | solution.py:317
  142.6 13.3 %collective-permute-start.61 = (f32[6,32,256]{2,1,0:T(8,128)S(1)}, f32[6,32,256]{2,1,0:T(8,128)S(1)}, u32[]{:S(2)}, u32[]{:S(2)}) collective-permute-start(f32[6,32,256]{2,1,0:T(8,128)S(1)} %get-tuple-element.162), channel_id=1, source_target_pairs={{0,4},{1,5},{2,6},{3,7},{4,0},{5,1},{6,2},{7,3},{8,12},{9,13},{10,... | collective-permute-start | bytes 589832 | tf_op jit(solution)/shard_map/ppermute | solution.py:317
  144.2 13.4 %collective-permute-start.62 = (f32[6,32,256]{2,1,0:T(8,128)S(1)}, f32[6,32,256]{2,1,0:T(8,128)S(1)}, u32[]{:S(2)}, u32[]{:S(2)}) collective-permute-start(f32[6,32,256]{2,1,0:T(8,128)S(1)} %get-tuple-element.163), channel_id=1, source_target_pairs={{0,8},{1,9},{2,10},{3,11},{4,12},{5,13},{6,14},{7,15},{8,0},{9,1},... | collective-permute-start | bytes 589832 | tf_op jit(solution)/shard_map/ppermute | solution.py:317
  154.0 16.5 %collective-permute-start.27 = (f32[3,2,32,256]{3,2,1,0:T(8,128)S(1)}, f32[3,2,32,256]{3,2,1,0:T(8,128)S(1)}, u32[]{:S(2)}, u32[]{:S(2)}) collective-permute-start(f32[3,2,32,256]{3,2,1,0:T(8,128)S(1)} %get-tuple-element.127), channel_id=1, source_target_pairs={{0,1},{1,0},{2,3},{3,2},{4,5},{5,4},{6,7},{7,6},{8,9},{9,8},{10,11... | collective-permute-start | bytes 589832 | tf_op jit(solution)/shard_map/ppermute | solution.py:317
  170.5 14.0 %collective-permute-start.65 = (f32[3,2,32,256]{3,2,1,0:T(8,128)S(1)}, f32[3,2,32,256]{3,2,1,0:T(8,128)S(1)}, u32[]{:S(2)}, u32[]{:S(2)}) collective-permute-start(f32[3,2,32,256]{3,2,1,0:T(8,128)S(1)} %get-tuple-element.167), channel_id=1, source_target_pairs={{0,3},{1,2},{2,1},{3,0},{4,7},{5,6},{6,5},{7,4},{8,11},{9,10},{10,... | collective-permute-start | bytes 589832 | tf_op jit(solution)/shard_map/ppermute | solution.py:317
  176.9 12.5 %collective-permute-start.34 = (f32[6,32,256]{2,1,0:T(8,128)S(1)}, f32[6,32,256]{2,1,0:T(8,128)S(1)}, u32[]{:S(2)}, u32[]{:S(2)}) collective-permute-start(f32[6,32,256]{2,1,0:T(8,128)S(1)} %get-tuple-element.135), channel_id=1, source_target_pairs={{0,4},{1,5},{2,6},{3,7},{4,0},{5,1},{6,2},{7,3},{8,12},{9,13},{10,... | collective-permute-start | bytes 589832 | tf_op jit(solution)/shard_map/ppermute | solution.py:317
  177.9 12.8 %collective-permute-start.35 = (f32[6,32,256]{2,1,0:T(8,128)S(1)}, f32[6,32,256]{2,1,0:T(8,128)S(1)}, u32[]{:S(2)}, u32[]{:S(2)}) collective-permute-start(f32[6,32,256]{2,1,0:T(8,128)S(1)} %get-tuple-element.136), channel_id=1, source_target_pairs={{0,8},{1,9},{2,10},{3,11},{4,12},{5,13},{6,14},{7,15},{8,0},{9,1},... | collective-permute-start | bytes 589832 | tf_op jit(solution)/shard_map/ppermute | solution.py:317
  187.2 11.9 %collective-permute-start.71 = (f32[6,32,256]{2,1,0:T(8,128)S(1)}, f32[6,32,256]{2,1,0:T(8,128)S(1)}, u32[]{:S(2)}, u32[]{:S(2)}) collective-permute-start(f32[6,32,256]{2,1,0:T(8,128)S(1)} %get-tuple-element.174), channel_id=1, source_target_pairs={{0,8},{1,9},{2,10},{3,11},{4,12},{5,13},{6,14},{7,15},{8,0},{9,1},... | collective-permute-start | bytes 589832 | tf_op jit(solution)/shard_map/ppermute | solution.py:317
  (71 other events, 648.3 us)

commit v3 on v0

v3 whole, which is shorter than its diff:
```python
import functools

import jax
import jax.numpy as jnp
from jax import lax
from jax.experimental import pallas as pl
from jax.experimental.pallas import tpu as pltpu
from jax.sharding import PartitionSpec as P

LEVELS = 3
CAP = 2
CHUNKS = 2
CORE, SIDE, LINE = 1, 2, 4
F32 = jnp.float32
BF16 = jnp.bfloat16
NT = (((1,), (1,)), ((), ()))
NN = (((1,), (0,)), ((), ()))
PARAMS = pltpu.CompilerParams(vmem_limit_bytes=20 * 1024 * 1024)
VMEM_SPEC = pl.BlockSpec(memory_space=pltpu.VMEM)


def low_bit(offset):
    return offset & -offset


def in_hbm(array):
    return pltpu.with_memory_space_constraint(array, pltpu.HBM)


def in_vmem(array):
    return pltpu.with_memory_space_constraint(array, pltpu.VMEM)


def split(value):
    high = value.astype(BF16)
    return high, (value - high.astype(F32)).astype(BF16)


def product(panel, high, low, dims):
    rows = panel.shape[0]
    panel_high, panel_low = split(panel)
    both = lax.dot_general(
        jnp.concatenate([panel_high, panel_low], axis=0), high, dims, preferred_element_type=F32
    )
    cross = lax.dot_general(panel_high, low, dims, preferred_element_type=F32)
    return both[:rows] + (both[rows:] + cross)


def line_offsets(depth):
    whole = tuple(offset for offset in range(depth) if offset % 2 == 0 or offset == 1)
    return whole, tuple(offset for offset in range(depth) if offset not in whole)


def lookup(values, index):
    hits = index[..., None] == jnp.arange(len(values))
    return jnp.sum(jnp.where(hits, jnp.array(values, jnp.int32), 0), axis=-1)


def tables(dev_rows, slot_rows, members, position):
    levels, rows, fanout = dev_rows.shape
    blocks_dev = rows // members
    width = blocks_dev * fanout
    depth = members // LINE
    whole, listed = line_offsets(depth)
    height, place = position // LINE, position % LINE

    readers = jnp.stack([position, position ^ SIDE, position ^ LINE, position ^ (LINE | SIDE)])
    lists = jnp.take(dev_rows.reshape(levels, members, width), readers, axis=1)
    slots = jnp.take(slot_rows.reshape(levels, members, width), readers, axis=1)
    positions = jnp.arange(width)
    earlier = positions[None, :] < positions[:, None]
    matches = lists[..., :, None] == lists[..., None, :]
    rank = jnp.sum(jnp.logical_and(matches, earlier), axis=-1, dtype=jnp.int32)
    code = lists * CAP + rank

    def asked(reader, offsets):
        owners = (height ^ jnp.array(offsets, jnp.int32))[:, None] * LINE + (place ^ jnp.arange(2))[None, :]
        wanted = (owners[..., None] * CAP + jnp.arange(CAP)).reshape(-1)
        found = code[:, reader, None, :] == wanted[None, :, None]
        return jnp.sum(jnp.where(found, slots[:, reader, None, :] + 1, 0), axis=2) - 1

    across = tuple(offset ^ 1 for offset in listed)
    table = jnp.concatenate([asked(1, whole), asked(2, across), asked(3, across)], axis=1)
    own_dev, own_slot, own_rank = lists[:, 0], slots[:, 0], rank[:, 0]
    flip = (own_dev % LINE) ^ place
    side, core = flip // SIDE, flip % SIDE
    offset = (own_dev // LINE) ^ height
    spot = lookup([whole.index(o) if o in whole else listed.index(o) for o in range(depth)], offset)
    is_whole = lookup([int(o in whole) for o in range(depth)], offset) == 1
    at_side = len(whole) * 2 * blocks_dev
    at_far = at_side + len(whole) * 2 * CAP
    place_of = jnp.where(
        is_whole,
        jnp.where(
            side == 0,
            (spot * 2 + core) * blocks_dev + own_slot,
            at_side + (spot * 2 + core) * CAP + own_rank,
        ),
        at_far + ((side * len(listed) + spot) * 2 + core) * CAP + own_rank,
    )
    return table.reshape(-1), place_of.reshape(-1)


COST = pl.CostEstimate(flops=600_000_000, bytes_accessed=3_000_000, transcendentals=0)


def run(kernel, out_shape, tables, operands, specs=None, scratch=(), grid=(), out_specs=None):
    return pl.pallas_call(
        kernel,
        out_shape=out_shape,
        grid_spec=pltpu.PrefetchScalarGridSpec(
            num_scalar_prefetch=len(tables),
            grid=grid,
            in_specs=specs if specs is not None else [VMEM_SPEC] * len(operands),
            out_specs=out_specs if out_specs is not None else [VMEM_SPEC] * len(out_shape),
            scratch_shapes=list(scratch),
        ),
        compiler_params=PARAMS,
        cost_estimate=COST,
    )(*tables, *operands)


def halves_kernel(*refs, streams, count):
    step = pl.program_id(0)
    for stream in range(streams):
        high, low = split(refs[stream][...])
        at = pl.ds((stream * count + step) * high.shape[0], high.shape[0])
        refs[streams][at], refs[streams + 1][at] = high, low


def halves(matrices, level, streams, width):
    points = matrices.shape[-1]
    matrices = matrices.reshape(matrices.shape[0], -1, points, points)
    total = matrices.shape[1]
    count = total // (streams * width)
    shape = pltpu.VMEM((total, points, points), BF16)
    specs = [
        pl.BlockSpec((None, width, points, points), lambda step, stream=stream: (level, stream * count + step, 0, 0))
        for stream in range(streams)
    ]
    return run(
        functools.partial(halves_kernel, streams=streams, count=count),
        [shape, shape], (), [in_hbm(matrices)] * streams, specs, grid=(count,),
    )


def first_kernel(probe_ref, inverse_ref, forward_ref):
    for g in range(inverse_ref.shape[0]):
        forward_ref[g] = product(probe_ref[g], *split(inverse_ref[g]), NT)


def first(probes, inverses, chunk):
    blocks, rows, points = probes.shape[1], probes.shape[2] // CHUNKS, probes.shape[3]
    width = blocks // 2 if blocks % 2 == 0 else blocks
    return run(
        first_kernel,
        [jax.ShapeDtypeStruct((blocks, rows, points), F32)],
        (), [in_hbm(probes), in_hbm(inverses)],
        [
            pl.BlockSpec((None, width, rows, points), lambda g: (0, g, chunk, 0)),
            pl.BlockSpec((None, width, points, points), lambda g: (0, g, 0, 0)),
        ],
        grid=(blocks // width,),
        out_specs=[pl.BlockSpec((width, rows, points), lambda g: (g, 0, 0))],
    )[0]


def pack_kernel(asked_ref, *refs, base, whole, listed):
    sources, targets = refs[: 2 * len(whole)], refs[2 * len(whole) :]
    row = 0
    for target, offsets in zip(targets, (whole, listed, listed)):
        for place, offset in enumerate(offsets):
            held = whole.index(offset if offsets is whole else offset ^ 1)
            for core in range(2):
                for rank in range(CAP):
                    slot = jnp.maximum(asked_ref[base + row * CAP + rank], 0)
                    target[(place * 2 + core) * CAP + rank] = sources[held * 2 + core][slot]
                row += 1


def pack(asked, base, held, whole, listed):
    rows, points = held[0].shape[1:]
    return run(
        functools.partial(pack_kernel, base=base, whole=whole, listed=listed),
        [
            jax.ShapeDtypeStruct((len(offsets) * 2 * CAP, rows, points), F32)
            for offsets in (whole, listed, listed)
        ],
        (asked,), held,
    )


def gather_kernel(asked_ref, local_ref, *refs, base, whole, listed, blocks):
    sources, (keep_ref, give_ref) = refs[:3], refs[3:]
    for place in range(len(whole)):
        for core, target in enumerate((keep_ref, give_ref)):
            target[place] = local_ref[pl.ds((place * 2 + core) * blocks, blocks)]
    row = 0
    for source, offsets in zip(sources, (whole, listed, listed)):
        for place, offset in enumerate(offsets):
            held = whole.index(offset if offsets is whole else offset ^ 1)
            for core, target in enumerate((keep_ref, give_ref)):
                for rank in range(CAP):
                    slot = asked_ref[base + row * CAP + rank]
                    term = source[(place * 2 + core) * CAP + rank]

                    @pl.when(slot >= 0)
                    def _(target=target, held=held, slot=slot, term=term):
                        target[held, slot] = target[held, slot] + term

                row += 1


def gather_sums(asked, base, local, moved, whole, listed, blocks):
    rows, points = local.shape[1:]
    shape = jax.ShapeDtypeStruct((len(whole), blocks, rows, points), F32)
    return run(
        functools.partial(gather_kernel, base=base, whole=whole, listed=listed, blocks=blocks),
        [shape, shape], (asked,), [local, *moved],
    )


def add_kernel(first_ref, second_ref, *targets):
    for place, target in enumerate(targets, 1):
        target[...] = first_ref[place] + second_ref[place]


def add(kept, given):
    shape = jax.ShapeDtypeStruct(kept.shape[1:], F32)
    return run(add_kernel, [shape] * (kept.shape[0] - 1), (), [kept, given])


def solve_kernel(
    place_ref, panel_ref, *refs, has_fetch, has_left, has_parts, base, level, chunk, whole, listed, blocks, fanout, adds
):
    refs = list(refs)

    def take(count):
        taken, refs[:count] = refs[:count], []
        return taken

    inverse_refs = take(2)
    coupling_refs = take(2) if has_fetch or has_parts else None
    near_refs = take(2 * len(whole)) if has_fetch else []
    far_refs = take(3) if has_fetch else []
    sum_refs = take(2 + adds) if not has_fetch else []
    (out_ref,) = take(1)
    part_refs = take(4) if has_parts else []
    pan_ref = take(1)[0] if has_fetch else None
    hold_ref = take(1)[0] if has_parts else None
    rows = out_ref.shape[1]
    start = 0
    for ref in near_refs + far_refs:
        pan_ref[pl.ds(start, ref.shape[0])] = ref[...]
        start += ref.shape[0]
    if has_parts:
        hold_ref[...] = jnp.zeros(hold_ref.shape, F32)
    for g in range(blocks):
        inverse = [ref[level * blocks + g] for ref in inverse_refs]
        if has_fetch:
            value = panel_ref[level, g, pl.ds(chunk * rows, rows)]
            for k in range(fanout):
                coupling = [ref[g * fanout + k] for ref in coupling_refs]
                value = value - product(pan_ref[place_ref[base + g * fanout + k]], *coupling, NT)
            value = product(value, *inverse, NT)
        else:
            value = panel_ref[g] - sum_refs[0][0, g] - sum_refs[1][0, g]
            for ref in sum_refs[2:]:
                value = value - ref[g]
        if has_left:
            value = product(value, *inverse, NN)
        out_ref[g] = value
        if has_parts:
            for k in range(fanout):
                coupling = [ref[g * fanout + k] for ref in coupling_refs]
                at = place_ref[base + g * fanout + k]
                hold_ref[at] = hold_ref[at] + product(value, *coupling, NN)
    start = 0
    for ref in part_refs:
        ref[...] = hold_ref[pl.ds(start, ref.shape[0])]
        start += ref.shape[0]


def solve(
    places, base, panel, rows, level, chunk, inverse, coupling, whole, listed, blocks,
    near=None, far=None, sums=None, left=False,
):
    points = panel.shape[-1]
    has_fetch = near is not None
    has_parts = left and coupling is not None
    fanout = coupling[0].shape[0] // blocks if coupling is not None else 0
    operands = [panel, *[in_vmem(array) for array in [*inverse, *(coupling if coupling is not None else [])]]]
    operands += [*near, *far] if has_fetch else sums
    out_shapes = [jax.ShapeDtypeStruct((blocks, rows, points), F32)]
    sizes = [len(whole) * 2 * blocks, len(whole) * 2 * CAP, len(listed) * 2 * CAP, len(listed) * 2 * CAP]
    scratch = [pltpu.VMEM((sum(sizes), rows, points), F32)] * (has_fetch + has_parts)
    if has_parts:
        out_shapes += [jax.ShapeDtypeStruct((size, rows, points), F32) for size in sizes]
    kernel = functools.partial(
        solve_kernel, has_fetch=has_fetch, has_left=left, has_parts=has_parts, base=base, level=level, chunk=chunk,
        whole=whole, listed=listed, blocks=blocks, fanout=fanout, adds=0 if has_fetch else len(sums) - 2,
    )
    results = run(kernel, out_shapes, (places,), operands, scratch=scratch)
    return results[0], results[1:]


def flip_move(array, bits):
    members = lax.axis_size("blk")
    return lax.ppermute(array, "blk", [(source, source ^ bits) for source in range(members)])


def local(probes, inverses, couplings, neighbour_devices, neighbour_slots):
    members = lax.axis_size("blk")
    position = lax.axis_index("blk")
    blocks, fanout = probes.shape[1], couplings.shape[2]
    rows = probes.shape[2] // CHUNKS
    depth = members // LINE
    whole, listed = line_offsets(depth)
    asked, places = tables(neighbour_devices, neighbour_slots, members, position)
    asked_size, place_size = asked.shape[0] // (LEVELS - 1), places.shape[0] // (LEVELS - 1)
    travel = sorted(whole[1:], key=lambda offset: (offset.bit_count(), -offset))
    shared = {}
    columns = [None] * CHUNKS

    def chain(chunk):
        call = functools.partial(
            solve, places, rows=rows, chunk=chunk, whole=whole, listed=listed, blocks=blocks
        )
        forward = [first(probes, inverses, chunk)]
        solved = [None] * LEVELS
        parts = None
        for level in range(1, LEVELS):
            held = {0: forward[-1]}
            for offset in travel:
                bit = low_bit(offset)
                held[offset] = flip_move(held[offset ^ bit], bit * LINE)
            near = [array for offset in whole for array in (held[offset], flip_move(held[offset], CORE))]
            yield
            packs = pack(asked, (level - 1) * asked_size, near, whole, listed)
            far = [flip_move(array, bits) for array, bits in zip(packs, (SIDE, LINE, LINE | SIDE))]
            yield
            result, parts = call(
                base=(level - 1) * place_size, panel=shared["probes"], level=level, inverse=shared["inverse"],
                coupling=shared["coupling"][level - 1], near=near, far=far, left=level == LEVELS - 1,
            )
            forward.append(result)
        solved[LEVELS - 1] = forward.pop()
        for level in range(LEVELS - 2, -1, -1):
            moved = [flip_move(array, bits) for array, bits in zip(parts[1:], (SIDE, LINE, LINE | SIDE))]
            yield
            kept, gift = gather_sums(asked, level * asked_size, parts[0], moved, whole, listed, blocks)
            given = flip_move(gift, CORE)
            yield
            totals = dict(zip(whole[1:], add(kept, given)))
            addends = []
            for offset in travel[::-1]:
                bit = low_bit(offset)
                arrived = flip_move(totals[offset], bit * LINE)
                if offset == bit:
                    addends.append(arrived)
                else:
                    totals[offset ^ bit] = totals[offset ^ bit] + arrived
            yield
            solved[level], parts = call(
                base=max(level - 1, 0) * place_size, panel=forward[level], level=level, inverse=shared["inverse"],
                coupling=shared["coupling"][level - 1] if level else None, sums=[kept, given, *addends], left=True,
            )
        columns[chunk] = jnp.stack(solved)
        yield

    def prepare_couplings(level):
        shared.setdefault("coupling", {})[level] = halves(couplings, level, 4, max(1, blocks * fanout // 12))

    def prepare_inverses():
        every = inverses.reshape(1, -1, *inverses.shape[2:])
        shared["inverse"] = halves(every, 0, 3, blocks // 2 if blocks % 2 == 0 else blocks)
        shared["probes"] = probes

    chains = [chain(chunk) for chunk in range(CHUNKS)]
    for stage in range(4 * LEVELS):
        if stage == 1:
            prepare_inverses()
            for level in range(LEVELS - 1):
                prepare_couplings(level)
        for steps in chains:
            next(steps, None)
    return jnp.concatenate(columns, axis=2)


def solution(mesh):
    return jax.shard_map(
        local,
        mesh=mesh,
        in_specs=(
            P(None, ("grp", "blk"), None, None),
            P(None, ("grp", "blk"), None, None),
            P(None, ("grp", "blk"), None, None, None),
            P(None, "grp", None),
            P(None, "grp", None),
        ),
        out_specs=P(None, ("grp", "blk"), None, None),
        check_vma=False,
    )
```

time: 371 us -> 182 us (0.49)
  waiting for transfers between devices: 258 us -> 79.8 us
  matrix products: 54.7 us -> 0 us
  Pallas kernels: 0 us -> 47 us
  starting transfers between devices: 18.9 us -> 49.1 us
  local copies, waits for them, and re-layouts: 22.7 us -> 2.55 us
  between operations: 13.6 us -> 0.5 us
    reduce_scatter x2 -> x0, waiting for transfers between devices: 176 us -> none  [local(): lax.psum_scatter(summed.reshape(blocks_dev * lax.axis_size('blk'), probe_...]
    all_to_all x2 -> x0, waiting for transfers between devices: 81.7 us -> none  [local(): lax.all_to_all(outgoing, 'blk', split_axis=0, concat_axis=0, tiled=True)]
    ppermute x0 -> x56, waiting for transfers between devices: none -> 79.8 us  [flip_move(): lax.ppermute(array, 'blk', [(source, source ^ bits) for source in range(m...]
    dot_general x12 -> x0, matrix products: 54.7 us -> none  [the longest x2 18.8 us: local(): jnp.einsum('bkpi,bkji->bpj', fetched, couplings[height - 1], precision=la...]
    ppermute x0 -> x56, starting transfers between devices: none -> 49.1 us  [flip_move(): lax.ppermute(array, 'blk', [(source, source ^ bits) for source in range(m...]
    pallas_call x0 -> x25, Pallas kernels: none -> 47 us  [run(): pl.pallas_call(kernel, out_shape=out_shape, grid_spec=pltpu.PrefetchScala...]
    all_to_all x2 -> x0, starting transfers between devices: 18.6 us -> none  [local(): lax.all_to_all(outgoing, 'blk', split_axis=0, concat_axis=0, tiled=True)]
    dot_general x2 -> x0, local copies, waits for them, and re-layouts: 12.6 us -> none  [local(): summed = jnp.dot(selector, partials, precision=lax.Precision.HIGHEST)]
  transfers between devices with their start and end apart: 4 -> 56, of which waited for: 4 -> 31; matrix products, arithmetic and copies ran while one was open for 0% -> 2% of each run, Pallas kernels for 0% -> 24%
where the time goes in v3:
time: 182 us; the launch traced here: 181 us
  waiting for transfers between devices  79.8 us (44%)
  starting transfers between devices  49.1 us (27%)
  Pallas kernels  47 us (26%)
  local copies, waits for them, and re-layouts  2.55 us (1%)
  other arithmetic  2.54 us (1%)
    ppermute x56, waiting for transfers between devices, flip_move(): lax.ppermute(array, 'blk', [(source, source ^ bits) for source in range(m...  79.8 us
    ppermute x56, starting transfers between devices, flip_move(): lax.ppermute(array, 'blk', [(source, source ^ bits) for source in range(m...  49.1 us
    pallas_call x25, Pallas kernels, run(): pl.pallas_call(kernel, out_shape=out_shape, grid_spec=pltpu.PrefetchScala...  47 us
  transfers between devices with their start and end apart: 56, of which 31 were waited for; matrix products, arithmetic and copies ran while one was open for 2% of the time, Pallas kernels for 24%

profile of v3, /device:TPU:0, one launch (start us, length us, event | category | flops | bytes accessed | tf_op | source)
XLA Modules:
  0.0 181.4 jit_solution(12961413925035369055)
XLA Ops:
  1.9 3.1 %collective-permute-start.1 = (f32[6,32,256]{2,1,0:T(8,128)S(1)}, f32[6,32,256]{2,1,0:T(8,128)S(1)}, u32[]{:S(2)}, u32[]{:S(2)}) collective-permute-start(f32[6,32,256]{2,1,0:T(8,128)S(1)} %shard_map.100.refs_0_.refs_4_.panel_ref), channel_id=1, source_target_pairs={{0,4},{1,5},{2,6},{3,7},{4,0},{5,1},{6,2},{7,3},{8,12},{9,13},{10,... | collective-permute-start | bytes 589832 | tf_op jit(solution)/shard_map/ppermute | solution.py:309
  5.0 2.6 %collective-permute-start.3 = (f32[6,32,256]{2,1,0:T(8,128)S(1)}, f32[6,32,256]{2,1,0:T(8,128)S(1)}, u32[]{:S(2)}, u32[]{:S(2)}) collective-permute-start(f32[6,32,256]{2,1,0:T(8,128)S(1)} %shard_map.100.refs_0_.refs_4_.panel_ref), channel_id=1, source_target_pairs={{0,8},{1,9},{2,10},{3,11},{4,12},{5,13},{6,14},{7,15},{8,0},{9,1},... | collective-permute-start | bytes 589832 | tf_op jit(solution)/shard_map/ppermute | solution.py:309
  16.2 6.3 %collective-permute-done.29.refs_2_.refs_6_ = f32[6,32,256]{2,1,0:T(8,128)S(1)} collective-permute-done((f32[6,32,256]{2,1,0:T(8,128)S(1)}, f32[6,32,256]{2,1,0:T(8,128)S(1)}, u32[]{:S(2)}, u32[]{:S(2)}) %collective-permute-start.29) | collective-permute-done | bytes 196640 | tf_op jit(solution)/shard_map/ppermute | solution.py:309
  22.5 2.6 %collective-permute-done.31.refs_4_.refs_8_ = f32[6,32,256]{2,1,0:T(8,128)S(1)} collective-permute-done((f32[6,32,256]{2,1,0:T(8,128)S(1)}, f32[6,32,256]{2,1,0:T(8,128)S(1)}, u32[]{:S(2)}, u32[]{:S(2)}) %collective-permute-start.31) | collective-permute-done | bytes 196640 | tf_op jit(solution)/shard_map/ppermute | solution.py:309
  34.3 2.7 %shard_map.101 = (bf16[18,256,256]{2,1,0:T(8,128)(2,1)S(1)}, bf16[18,256,256]{2,1,0:T(8,128)(2,1)S(1)}) custom-call(f32[1,18,256,256]{3,2,1,0:T(8,128)} %bitcast.58, f32[1,18,256,256]{3,2,1,0:T(8,128)} %bitcast.59, f32[1,18,256,256]{3,2,1,0:T(8,128)} %bitcast.60), custom_call_target="tpu_custom_call" | custom-call | flops 600000000 | bytes 3000000 | tf_op jit(solution)/shard_map/pallas_call | solution.py:108
  37.0 4.0 %shard_map.102 = (bf16[24,256,256]{2,1,0:T(8,128)(2,1)S(1)}, bf16[24,256,256]{2,1,0:T(8,128)(2,1)S(1)}) custom-call(f32[2,24,256,256]{3,2,1,0:T(8,128)} %bitcast.50, f32[2,24,256,256]{3,2,1,0:T(8,128)} %bitcast.51, f32[2,24,256,256]{3,2,1,0:T(8,128)} %bitcast.52, f32[2,24,256,256]{3,2,1,0:T(8,128)} %bitcast.53), custom_call_target="tpu_custom_call" | custom-call | flops 600000000 | bytes 3000000 | tf_op jit(solution)/shard_map/pallas_call | solution.py:108
  41.1 2.8 %collective-permute-done.5.refs_10_ = f32[12,32,256]{2,1,0:T(8,128)S(1)} collective-permute-done((f32[12,32,256]{2,1,0:T(8,128)S(1)}, f32[12,32,256]{2,1,0:T(8,128)S(1)}, u32[]{:S(2)}, u32[]{:S(2)}) %collective-permute-start.5) | collective-permute-done | bytes 393248 | tf_op jit(solution)/shard_map/ppermute | solution.py:309
  43.9 3.5 %shard_map.104.refs_0_.refs_4_.panel_ref = f32[6,32,256]{2,1,0:T(8,128)S(1)} custom-call(s32[48]{0:T(128)S(1)} %fusion.6.place_ref, f32[3,6,64,256]{3,2,1,0:T(8,128)S(1)} %copy-done, bf16[18,256,256]{2,1,0:T(8,128)(2,1)S(1)} %get-tuple-element.60.refs_0_, bf16[18,256,256]{2,1,0:T(8,128)(2,1)S(1)} %get-tuple-element.61.refs_1_, ...), custom_call_target="tpu_custom_call" | custom-call | flops 600000000 | bytes 3000000 | tf_op jit(solution)/shard_map/pallas_call | solution.py:108
  47.8 2.6 %collective-permute-start.11 = (f32[6,32,256]{2,1,0:T(8,128)S(1)}, f32[6,32,256]{2,1,0:T(8,128)S(1)}, u32[]{:S(2)}, u32[]{:S(2)}) collective-permute-start(f32[6,32,256]{2,1,0:T(8,128)S(1)} %shard_map.104.refs_0_.refs_4_.panel_ref), channel_id=1, source_target_pairs={{0,8},{1,9},{2,10},{3,11},{4,12},{5,13},{6,14},{7,15},{8,0},{9,1},... | collective-permute-start | bytes 589832 | tf_op jit(solution)/shard_map/ppermute | solution.py:309
  51.9 3.5 %shard_map.116.refs_0_.refs_4_.panel_ref = f32[6,32,256]{2,1,0:T(8,128)S(1)} custom-call(s32[48]{0:T(128)S(1)} %fusion.6.place_ref, f32[3,6,64,256]{3,2,1,0:T(8,128)S(1)} %copy-done, bf16[18,256,256]{2,1,0:T(8,128)(2,1)S(1)} %get-tuple-element.60.refs_0_, bf16[18,256,256]{2,1,0:T(8,128)(2,1)S(1)} %get-tuple-element.61.refs_1_, ...), custom_call_target="tpu_custom_call" | custom-call | flops 600000000 | bytes 3000000 | tf_op jit(solution)/shard_map/pallas_call | solution.py:108
  55.8 2.6 %collective-permute-start.39 = (f32[6,32,256]{2,1,0:T(8,128)S(1)}, f32[6,32,256]{2,1,0:T(8,128)S(1)}, u32[]{:S(2)}, u32[]{:S(2)}) collective-permute-start(f32[6,32,256]{2,1,0:T(8,128)S(1)} %shard_map.116.refs_0_.refs_4_.panel_ref), channel_id=1, source_target_pairs={{0,8},{1,9},{2,10},{3,11},{4,12},{5,13},{6,14},{7,15},{8,0},{9,1},... | collective-permute-start | bytes 589832 | tf_op jit(solution)/shard_map/ppermute | solution.py:309
  59.4 6.6 %collective-permute-done.37.refs_2_.refs_6_ = f32[6,32,256]{2,1,0:T(8,128)S(1)} collective-permute-done((f32[6,32,256]{2,1,0:T(8,128)S(1)}, f32[6,32,256]{2,1,0:T(8,128)S(1)}, u32[]{:S(2)}, u32[]{:S(2)}) %collective-permute-start.37) | collective-permute-done | bytes 196640 | tf_op jit(solution)/shard_map/ppermute | solution.py:309
  71.2 2.5 %collective-permute-start.15 = (f32[4,32,256]{2,1,0:T(8,128)S(1)}, f32[4,32,256]{2,1,0:T(8,128)S(1)}, u32[]{:S(2)}, u32[]{:S(2)}) collective-permute-start(f32[4,32,256]{2,1,0:T(8,128)S(1)} %get-tuple-element.71), channel_id=1, source_target_pairs={{0,6},{1,7},{2,4},{3,5},{4,2},{5,3},{6,0},{7,1},{8,14},{9,15},{10,... | collective-permute-start | bytes 393224 | tf_op jit(solution)/shard_map/ppermute | solution.py:309
  74.0 3.4 %collective-permute-done.14.refs_11_ = f32[4,32,256]{2,1,0:T(8,128)S(1)} collective-permute-done((f32[4,32,256]{2,1,0:T(8,128)S(1)}, f32[4,32,256]{2,1,0:T(8,128)S(1)}, u32[]{:S(2)}, u32[]{:S(2)}) %collective-permute-start.14) | collective-permute-done | bytes 131104 | tf_op jit(solution)/shard_map/ppermute | solution.py:309
  78.3 4.1 %shard_map.105 = (bf16[24,256,256]{2,1,0:T(8,128)(2,1)S(1)}, bf16[24,256,256]{2,1,0:T(8,128)(2,1)S(1)}) custom-call(f32[2,24,256,256]{3,2,1,0:T(8,128)} %bitcast.54, f32[2,24,256,256]{3,2,1,0:T(8,128)} %bitcast.55, f32[2,24,256,256]{3,2,1,0:T(8,128)} %bitcast.56, f32[2,24,256,256]{3,2,1,0:T(8,128)} %bitcast.57), custom_call_target="tpu_custom_call" | custom-call | flops 600000000 | bytes 3000000 | tf_op jit(solution)/shard_map/pallas_call | solution.py:108
  84.5 6.2 %shard_map.107 = (f32[6,32,256]{2,1,0:T(8,128)S(1)}, f32[36,32,256]{2,1,0:T(8,128)S(1)}, f32[12,32,256]{2,1,0:T(8,128)S(1)}, f32[4,32,256]{2,1,0:T(8,128)S(1)}, f32[4,32,256]{2,1,0:T(8,128)S(1)}) custom-call(s32[48]{0:T(128)S(1)} %fusion.6.place_ref, f32[3,6,64,256]{3,2,1,0:T(8,128)S(1)} %copy-done, bf16[18,256,256]{2,1,0:T(8,128)(2,1)S(1)} %get-tuple-element.60.refs_0_, ...), custom_call_target="tpu_custom_call" | custom-call | flops 600000000 | bytes 3000000 | tf_op jit(solution)/shard_map/pallas_call | solution.py:108
  90.8 2.5 %collective-permute-start.16 = (f32[12,32,256]{2,1,0:T(8,128)S(1)}, f32[12,32,256]{2,1,0:T(8,128)S(1)}, u32[]{:S(2)}, u32[]{:S(2)}) collective-permute-start(f32[12,32,256]{2,1,0:T(8,128)S(1)} %get-tuple-element.73), channel_id=1, source_target_pairs={{0,2},{1,3},{2,0},{3,1},{4,6},{5,7},{6,4},{7,5},{8,10},{9,11},{10,... | collective-permute-start | bytes 1179656 | tf_op jit(solution)/shard_map/ppermute | solution.py:309
  93.5 6.2 %shard_map.118 = (f32[6,32,256]{2,1,0:T(8,128)S(1)}, f32[36,32,256]{2,1,0:T(8,128)S(1)}, f32[12,32,256]{2,1,0:T(8,128)S(1)}, f32[4,32,256]{2,1,0:T(8,128)S(1)}, f32[4,32,256]{2,1,0:T(8,128)S(1)}) custom-call(s32[48]{0:T(128)S(1)} %fusion.6.place_ref, f32[3,6,64,256]{3,2,1,0:T(8,128)S(1)} %copy-done, bf16[18,256,256]{2,1,0:T(8,128)(2,1)S(1)} %get-tuple-element.60.refs_0_, ...), custom_call_target="tpu_custom_call" | custom-call | flops 600000000 | bytes 3000000 | tf_op jit(solution)/shard_map/pallas_call | solution.py:108
  103.6 4.2 %collective-permute-done.17.refs_1_ = f32[4,32,256]{2,1,0:T(8,128)S(1)} collective-permute-done((f32[4,32,256]{2,1,0:T(8,128)S(1)}, f32[4,32,256]{2,1,0:T(8,128)S(1)}, u32[]{:S(2)}, u32[]{:S(2)}) %collective-permute-start.17) | collective-permute-done | bytes 131104 | tf_op jit(solution)/shard_map/ppermute | solution.py:309
  107.8 2.8 %collective-permute-done.18.refs_2_ = f32[4,32,256]{2,1,0:T(8,128)S(1)} collective-permute-done((f32[4,32,256]{2,1,0:T(8,128)S(1)}, f32[4,32,256]{2,1,0:T(8,128)S(1)}, u32[]{:S(2)}, u32[]{:S(2)}) %collective-permute-start.18) | collective-permute-done | bytes 131104 | tf_op jit(solution)/shard_map/ppermute | solution.py:309
  117.5 2.6 %collective-permute-start.21 = (f32[6,32,256]{2,1,0:T(8,128)S(1)}, f32[6,32,256]{2,1,0:T(8,128)S(1)}, u32[]{:S(2)}, u32[]{:S(2)}) collective-permute-start(f32[6,32,256]{2,1,0:T(8,128)S(1)} %get-tuple-element.79), channel_id=1, source_target_pairs={{0,8},{1,9},{2,10},{3,11},{4,12},{5,13},{6,14},{7,15},{8,0},{9,1},... | collective-permute-start | bytes 589832 | tf_op jit(solution)/shard_map/ppermute | solution.py:309
  122.3 6.5 %collective-permute-done.20.refs_6_ = f32[6,32,256]{2,1,0:T(8,128)S(1)} collective-permute-done((f32[6,32,256]{2,1,0:T(8,128)S(1)}, f32[6,32,256]{2,1,0:T(8,128)S(1)}, u32[]{:S(2)}, u32[]{:S(2)}) %collective-permute-start.20) | collective-permute-done | bytes 196640 | tf_op jit(solution)/shard_map/ppermute | solution.py:309
  130.5 2.8 %shard_map.110 = (f32[6,32,256]{2,1,0:T(8,128)S(1)}, f32[36,32,256]{2,1,0:T(8,128)S(1)}, f32[12,32,256]{2,1,0:T(8,128)S(1)}, f32[4,32,256]{2,1,0:T(8,128)S(1)}, f32[4,32,256]{2,1,0:T(8,128)S(1)}) custom-call(s32[48]{0:T(128)S(1)} %fusion.6.place_ref, f32[6,32,256]{2,1,0:T(8,128)S(1)} %shard_map.104.refs_0_.refs_4_.panel_ref, ...), custom_call_target="tpu_custom_call" | custom-call | flops 600000000 | bytes 3000000 | tf_op jit(solution)/shard_map/pallas_call | solution.py:108
  138.2 2.8 %shard_map.121 = (f32[6,32,256]{2,1,0:T(8,128)S(1)}, f32[36,32,256]{2,1,0:T(8,128)S(1)}, f32[12,32,256]{2,1,0:T(8,128)S(1)}, f32[4,32,256]{2,1,0:T(8,128)S(1)}, f32[4,32,256]{2,1,0:T(8,128)S(1)}) custom-call(s32[48]{0:T(128)S(1)} %fusion.6.place_ref, f32[6,32,256]{2,1,0:T(8,128)S(1)} %shard_map.116.refs_0_.refs_4_.panel_ref, ...), custom_call_target="tpu_custom_call" | custom-call | flops 600000000 | bytes 3000000 | tf_op jit(solution)/shard_map/pallas_call | solution.py:108
  144.8 4.2 %collective-permute-done.23.refs_1_ = f32[4,32,256]{2,1,0:T(8,128)S(1)} collective-permute-done((f32[4,32,256]{2,1,0:T(8,128)S(1)}, f32[4,32,256]{2,1,0:T(8,128)S(1)}, u32[]{:S(2)}, u32[]{:S(2)}) %collective-permute-start.23) | collective-permute-done | bytes 131104 | tf_op jit(solution)/shard_map/ppermute | solution.py:309
  149.2 2.5 %collective-permute-done.24.refs_2_ = f32[4,32,256]{2,1,0:T(8,128)S(1)} collective-permute-done((f32[4,32,256]{2,1,0:T(8,128)S(1)}, f32[4,32,256]{2,1,0:T(8,128)S(1)}, u32[]{:S(2)}, u32[]{:S(2)}) %collective-permute-start.24) | collective-permute-done | bytes 131104 | tf_op jit(solution)/shard_map/ppermute | solution.py:309
  153.2 2.3 %collective-permute-done.52.refs_2_ = f32[4,32,256]{2,1,0:T(8,128)S(1)} collective-permute-done((f32[4,32,256]{2,1,0:T(8,128)S(1)}, f32[4,32,256]{2,1,0:T(8,128)S(1)}, u32[]{:S(2)}, u32[]{:S(2)}) %collective-permute-start.52) | collective-permute-done | bytes 131104 | tf_op jit(solution)/shard_map/ppermute | solution.py:309
  158.8 2.5 %collective-permute-start.27 = (f32[6,32,256]{2,1,0:T(8,128)S(1)}, f32[6,32,256]{2,1,0:T(8,128)S(1)}, u32[]{:S(2)}, u32[]{:S(2)}) collective-permute-start(f32[6,32,256]{2,1,0:T(8,128)S(1)} %get-tuple-element.87), channel_id=1, source_target_pairs={{0,8},{1,9},{2,10},{3,11},{4,12},{5,13},{6,14},{7,15},{8,0},{9,1},... | collective-permute-start | bytes 589832 | tf_op jit(solution)/shard_map/ppermute | solution.py:309
  163.3 5.3 %collective-permute-done.26.refs_4_ = f32[6,32,256]{2,1,0:T(8,128)S(1)} collective-permute-done((f32[6,32,256]{2,1,0:T(8,128)S(1)}, f32[6,32,256]{2,1,0:T(8,128)S(1)}, u32[]{:S(2)}, u32[]{:S(2)}) %collective-permute-start.26) | collective-permute-done | bytes 196640 | tf_op jit(solution)/shard_map/ppermute | solution.py:309
  168.6 3.2 %collective-permute-done.27.refs_5_ = f32[6,32,256]{2,1,0:T(8,128)S(1)} collective-permute-done((f32[6,32,256]{2,1,0:T(8,128)S(1)}, f32[6,32,256]{2,1,0:T(8,128)S(1)}, u32[]{:S(2)}, u32[]{:S(2)}) %collective-permute-start.27) | collective-permute-done | bytes 196640 | tf_op jit(solution)/shard_map/ppermute | solution.py:309
  172.7 3.9 %collective-permute-done.54.refs_4_ = f32[6,32,256]{2,1,0:T(8,128)S(1)} collective-permute-done((f32[6,32,256]{2,1,0:T(8,128)S(1)}, f32[6,32,256]{2,1,0:T(8,128)S(1)}, u32[]{:S(2)}, u32[]{:S(2)}) %collective-permute-start.54) | collective-permute-done | bytes 196640 | tf_op jit(solution)/shard_map/ppermute | solution.py:309
  176.6 2.8 %collective-permute-done.55.refs_5_ = f32[6,32,256]{2,1,0:T(8,128)S(1)} collective-permute-done((f32[6,32,256]{2,1,0:T(8,128)S(1)}, f32[6,32,256]{2,1,0:T(8,128)S(1)}, u32[]{:S(2)}, u32[]{:S(2)}) %collective-permute-start.55) | collective-permute-done | bytes 196640 | tf_op jit(solution)/shard_map/ppermute | solution.py:309
  (162 shorter events, 64.7 us)
Async XLA Ops:
  1.9 12.9 %collective-permute-start.1 = (f32[6,32,256]{2,1,0:T(8,128)S(1)}, f32[6,32,256]{2,1,0:T(8,128)S(1)}, u32[]{:S(2)}, u32[]{:S(2)}) collective-permute-start(f32[6,32,256]{2,1,0:T(8,128)S(1)} %shard_map.100.refs_0_.refs_4_.panel_ref), channel_id=1, source_target_pairs={{0,4},{1,5},{2,6},{3,7},{4,0},{5,1},{6,2},{7,3},{8,12},{9,13},{10,... | collective-permute-start | bytes 589832 | tf_op jit(solution)/shard_map/ppermute | solution.py:309
  5.0 10.6 %collective-permute-start.3 = (f32[6,32,256]{2,1,0:T(8,128)S(1)}, f32[6,32,256]{2,1,0:T(8,128)S(1)}, u32[]{:S(2)}, u32[]{:S(2)}) collective-permute-start(f32[6,32,256]{2,1,0:T(8,128)S(1)} %shard_map.100.refs_0_.refs_4_.panel_ref), channel_id=1, source_target_pairs={{0,8},{1,9},{2,10},{3,11},{4,12},{5,13},{6,14},{7,15},{8,0},{9,1},... | collective-permute-start | bytes 589832 | tf_op jit(solution)/shard_map/ppermute | solution.py:309
  9.5 12.9 %collective-permute-start.29 = (f32[6,32,256]{2,1,0:T(8,128)S(1)}, f32[6,32,256]{2,1,0:T(8,128)S(1)}, u32[]{:S(2)}, u32[]{:S(2)}) collective-permute-start(f32[6,32,256]{2,1,0:T(8,128)S(1)} %shard_map.114.refs_0_.refs_4_.panel_ref), channel_id=1, source_target_pairs={{0,4},{1,5},{2,6},{3,7},{4,0},{5,1},{6,2},{7,3},{8,12},{9,13},{10,... | collective-permute-start | bytes 589832 | tf_op jit(solution)/shard_map/ppermute | solution.py:309
  10.0 15.0 %collective-permute-start.31 = (f32[6,32,256]{2,1,0:T(8,128)S(1)}, f32[6,32,256]{2,1,0:T(8,128)S(1)}, u32[]{:S(2)}, u32[]{:S(2)}) collective-permute-start(f32[6,32,256]{2,1,0:T(8,128)S(1)} %shard_map.114.refs_0_.refs_4_.panel_ref), channel_id=1, source_target_pairs={{0,8},{1,9},{2,10},{3,11},{4,12},{5,13},{6,14},{7,15},{8,0},{9,1},... | collective-permute-start | bytes 589832 | tf_op jit(solution)/shard_map/ppermute | solution.py:309
  14.9 13.4 %collective-permute-start.28 = (f32[6,32,256]{2,1,0:T(8,128)S(1)}, f32[6,32,256]{2,1,0:T(8,128)S(1)}, u32[]{:S(2)}, u32[]{:S(2)}) collective-permute-start(f32[6,32,256]{2,1,0:T(8,128)S(1)} %shard_map.114.refs_0_.refs_4_.panel_ref), channel_id=1, source_target_pairs={{0,1},{1,0},{2,3},{3,2},{4,5},{5,4},{6,7},{7,6},{8,9},{9,8},{10,11... | collective-permute-start | bytes 589832 | tf_op jit(solution)/shard_map/ppermute | solution.py:309
  26.3 17.6 %collective-permute-start.5 = (f32[12,32,256]{2,1,0:T(8,128)S(1)}, f32[12,32,256]{2,1,0:T(8,128)S(1)}, u32[]{:S(2)}, u32[]{:S(2)}) collective-permute-start(f32[12,32,256]{2,1,0:T(8,128)S(1)} %get-tuple-element.64), channel_id=1, source_target_pairs={{0,2},{1,3},{2,0},{3,1},{4,6},{5,7},{6,4},{7,5},{8,10},{9,11},{10,... | collective-permute-start | bytes 1179656 | tf_op jit(solution)/shard_map/ppermute | solution.py:309
  28.3 12.8 %collective-permute-start.7 = (f32[4,32,256]{2,1,0:T(8,128)S(1)}, f32[4,32,256]{2,1,0:T(8,128)S(1)}, u32[]{:S(2)}, u32[]{:S(2)}) collective-permute-start(f32[4,32,256]{2,1,0:T(8,128)S(1)} %get-tuple-element.66), channel_id=1, source_target_pairs={{0,6},{1,7},{2,4},{3,5},{4,2},{5,3},{6,0},{7,1},{8,14},{9,15},{10,... | collective-permute-start | bytes 393224 | tf_op jit(solution)/shard_map/ppermute | solution.py:309
  30.4 21.4 %collective-permute-start.33 = (f32[12,32,256]{2,1,0:T(8,128)S(1)}, f32[12,32,256]{2,1,0:T(8,128)S(1)}, u32[]{:S(2)}, u32[]{:S(2)}) collective-permute-start(f32[12,32,256]{2,1,0:T(8,128)S(1)} %get-tuple-element.90), channel_id=1, source_target_pairs={{0,2},{1,3},{2,0},{3,1},{4,6},{5,7},{6,4},{7,5},{8,10},{9,11},{10,... | collective-permute-start | bytes 1179656 | tf_op jit(solution)/shard_map/ppermute | solution.py:309
  32.1 18.3 %collective-permute-start.34 = (f32[4,32,256]{2,1,0:T(8,128)S(1)}, f32[4,32,256]{2,1,0:T(8,128)S(1)}, u32[]{:S(2)}, u32[]{:S(2)}) collective-permute-start(f32[4,32,256]{2,1,0:T(8,128)S(1)} %get-tuple-element.91), channel_id=1, source_target_pairs={{0,4},{1,5},{2,6},{3,7},{4,0},{5,1},{6,2},{7,3},{8,12},{9,13},{10,... | collective-permute-start | bytes 393224 | tf_op jit(solution)/shard_map/ppermute | solution.py:309
  34.2 16.2 %collective-permute-start.35 = (f32[4,32,256]{2,1,0:T(8,128)S(1)}, f32[4,32,256]{2,1,0:T(8,128)S(1)}, u32[]{:S(2)}, u32[]{:S(2)}) collective-permute-start(f32[4,32,256]{2,1,0:T(8,128)S(1)} %get-tuple-element.92), channel_id=1, source_target_pairs={{0,6},{1,7},{2,4},{3,5},{4,2},{5,3},{6,0},{7,1},{8,14},{9,15},{10,... | collective-permute-start | bytes 393224 | tf_op jit(solution)/shard_map/ppermute | solution.py:309
  47.4 11.1 %collective-permute-start.9 = (f32[6,32,256]{2,1,0:T(8,128)S(1)}, f32[6,32,256]{2,1,0:T(8,128)S(1)}, u32[]{:S(2)}, u32[]{:S(2)}) collective-permute-start(f32[6,32,256]{2,1,0:T(8,128)S(1)} %shard_map.104.refs_0_.refs_4_.panel_ref), channel_id=1, source_target_pairs={{0,4},{1,5},{2,6},{3,7},{4,0},{5,1},{6,2},{7,3},{8,12},{9,13},{10,... | collective-permute-start | bytes 589832 | tf_op jit(solution)/shard_map/ppermute | solution.py:309
  47.8 11.1 %collective-permute-start.11 = (f32[6,32,256]{2,1,0:T(8,128)S(1)}, f32[6,32,256]{2,1,0:T(8,128)S(1)}, u32[]{:S(2)}, u32[]{:S(2)}) collective-permute-start(f32[6,32,256]{2,1,0:T(8,128)S(1)} %shard_map.104.refs_0_.refs_4_.panel_ref), channel_id=1, source_target_pairs={{0,8},{1,9},{2,10},{3,11},{4,12},{5,13},{6,14},{7,15},{8,0},{9,1},... | collective-permute-start | bytes 589832 | tf_op jit(solution)/shard_map/ppermute | solution.py:309
  55.4 10.7 %collective-permute-start.37 = (f32[6,32,256]{2,1,0:T(8,128)S(1)}, f32[6,32,256]{2,1,0:T(8,128)S(1)}, u32[]{:S(2)}, u32[]{:S(2)}) collective-permute-start(f32[6,32,256]{2,1,0:T(8,128)S(1)} %shard_map.116.refs_0_.refs_4_.panel_ref), channel_id=1, source_target_pairs={{0,4},{1,5},{2,6},{3,7},{4,0},{5,1},{6,2},{7,3},{8,12},{9,13},{10,... | collective-permute-start | bytes 589832 | tf_op jit(solution)/shard_map/ppermute | solution.py:309
  55.8 11.5 %collective-permute-start.39 = (f32[6,32,256]{2,1,0:T(8,128)S(1)}, f32[6,32,256]{2,1,0:T(8,128)S(1)}, u32[]{:S(2)}, u32[]{:S(2)}) collective-permute-start(f32[6,32,256]{2,1,0:T(8,128)S(1)} %shard_map.116.refs_0_.refs_4_.panel_ref), channel_id=1, source_target_pairs={{0,8},{1,9},{2,10},{3,11},{4,12},{5,13},{6,14},{7,15},{8,0},{9,1},... | collective-permute-start | bytes 589832 | tf_op jit(solution)/shard_map/ppermute | solution.py:309
  59.0 10.5 %collective-permute-start.36 = (f32[6,32,256]{2,1,0:T(8,128)S(1)}, f32[6,32,256]{2,1,0:T(8,128)S(1)}, u32[]{:S(2)}, u32[]{:S(2)}) collective-permute-start(f32[6,32,256]{2,1,0:T(8,128)S(1)} %shard_map.116.refs_0_.refs_4_.panel_ref), channel_id=1, source_target_pairs={{0,1},{1,0},{2,3},{3,2},{4,5},{5,4},{6,7},{7,6},{8,9},{9,8},{10,11... | collective-permute-start | bytes 589832 | tf_op jit(solution)/shard_map/ppermute | solution.py:309
  67.9 16.6 %collective-permute-start.13 = (f32[12,32,256]{2,1,0:T(8,128)S(1)}, f32[12,32,256]{2,1,0:T(8,128)S(1)}, u32[]{:S(2)}, u32[]{:S(2)}) collective-permute-start(f32[12,32,256]{2,1,0:T(8,128)S(1)} %get-tuple-element.69), channel_id=1, source_target_pairs={{0,2},{1,3},{2,0},{3,1},{4,6},{5,7},{6,4},{7,5},{8,10},{9,11},{10,... | collective-permute-start | bytes 1179656 | tf_op jit(solution)/shard_map/ppermute | solution.py:309
  70.1 23.4 %collective-permute-start.41 = (f32[12,32,256]{2,1,0:T(8,128)S(1)}, f32[12,32,256]{2,1,0:T(8,128)S(1)}, u32[]{:S(2)}, u32[]{:S(2)}) collective-permute-start(f32[12,32,256]{2,1,0:T(8,128)S(1)} %get-tuple-element.93), channel_id=1, source_target_pairs={{0,2},{1,3},{2,0},{3,1},{4,6},{5,7},{6,4},{7,5},{8,10},{9,11},{10,... | collective-permute-start | bytes 1179656 | tf_op jit(solution)/shard_map/ppermute | solution.py:309
  71.2 11.2 %collective-permute-start.15 = (f32[4,32,256]{2,1,0:T(8,128)S(1)}, f32[4,32,256]{2,1,0:T(8,128)S(1)}, u32[]{:S(2)}, u32[]{:S(2)}) collective-permute-start(f32[4,32,256]{2,1,0:T(8,128)S(1)} %get-tuple-element.71), channel_id=1, source_target_pairs={{0,6},{1,7},{2,4},{3,5},{4,2},{5,3},{6,0},{7,1},{8,14},{9,15},{10,... | collective-permute-start | bytes 393224 | tf_op jit(solution)/shard_map/ppermute | solution.py:309
  73.7 19.7 %collective-permute-start.42 = (f32[4,32,256]{2,1,0:T(8,128)S(1)}, f32[4,32,256]{2,1,0:T(8,128)S(1)}, u32[]{:S(2)}, u32[]{:S(2)}) collective-permute-start(f32[4,32,256]{2,1,0:T(8,128)S(1)} %get-tuple-element.94), channel_id=1, source_target_pairs={{0,4},{1,5},{2,6},{3,7},{4,0},{5,1},{6,2},{7,3},{8,12},{9,13},{10,... | collective-permute-start | bytes 393224 | tf_op jit(solution)/shard_map/ppermute | solution.py:309
  77.3 16.0 %collective-permute-start.43 = (f32[4,32,256]{2,1,0:T(8,128)S(1)}, f32[4,32,256]{2,1,0:T(8,128)S(1)}, u32[]{:S(2)}, u32[]{:S(2)}) collective-permute-start(f32[4,32,256]{2,1,0:T(8,128)S(1)} %get-tuple-element.95), channel_id=1, source_target_pairs={{0,6},{1,7},{2,4},{3,5},{4,2},{5,3},{6,0},{7,1},{8,14},{9,15},{10,... | collective-permute-start | bytes 393224 | tf_op jit(solution)/shard_map/ppermute | solution.py:309
  90.8 19.8 %collective-permute-start.16 = (f32[12,32,256]{2,1,0:T(8,128)S(1)}, f32[12,32,256]{2,1,0:T(8,128)S(1)}, u32[]{:S(2)}, u32[]{:S(2)}) collective-permute-start(f32[12,32,256]{2,1,0:T(8,128)S(1)} %get-tuple-element.73), channel_id=1, source_target_pairs={{0,2},{1,3},{2,0},{3,1},{4,6},{5,7},{6,4},{7,5},{8,10},{9,11},{10,... | collective-permute-start | bytes 1179656 | tf_op jit(solution)/shard_map/ppermute | solution.py:309
  99.8 16.4 %collective-permute-start.44 = (f32[12,32,256]{2,1,0:T(8,128)S(1)}, f32[12,32,256]{2,1,0:T(8,128)S(1)}, u32[]{:S(2)}, u32[]{:S(2)}) collective-permute-start(f32[12,32,256]{2,1,0:T(8,128)S(1)} %get-tuple-element.97), channel_id=1, source_target_pairs={{0,2},{1,3},{2,0},{3,1},{4,6},{5,7},{6,4},{7,5},{8,10},{9,11},{10,... | collective-permute-start | bytes 1179656 | tf_op jit(solution)/shard_map/ppermute | solution.py:309
  117.2 11.7 %collective-permute-start.20 = (f32[6,32,256]{2,1,0:T(8,128)S(1)}, f32[6,32,256]{2,1,0:T(8,128)S(1)}, u32[]{:S(2)}, u32[]{:S(2)}) collective-permute-start(f32[6,32,256]{2,1,0:T(8,128)S(1)} %get-tuple-element.78), channel_id=1, source_target_pairs={{0,4},{1,5},{2,6},{3,7},{4,0},{5,1},{6,2},{7,3},{8,12},{9,13},{10,... | collective-permute-start | bytes 589832 | tf_op jit(solution)/shard_map/ppermute | solution.py:309
  117.5 13.0 %collective-permute-start.21 = (f32[6,32,256]{2,1,0:T(8,128)S(1)}, f32[6,32,256]{2,1,0:T(8,128)S(1)}, u32[]{:S(2)}, u32[]{:S(2)}) collective-permute-start(f32[6,32,256]{2,1,0:T(8,128)S(1)} %get-tuple-element.79), channel_id=1, source_target_pairs={{0,8},{1,9},{2,10},{3,11},{4,12},{5,13},{6,14},{7,15},{8,0},{9,1},... | collective-permute-start | bytes 589832 | tf_op jit(solution)/shard_map/ppermute | solution.py:309
  120.2 16.7 %collective-permute-start.48 = (f32[6,32,256]{2,1,0:T(8,128)S(1)}, f32[6,32,256]{2,1,0:T(8,128)S(1)}, u32[]{:S(2)}, u32[]{:S(2)}) collective-permute-start(f32[6,32,256]{2,1,0:T(8,128)S(1)} %get-tuple-element.102), channel_id=1, source_target_pairs={{0,4},{1,5},{2,6},{3,7},{4,0},{5,1},{6,2},{7,3},{8,12},{9,13},{10,... | collective-permute-start | bytes 589832 | tf_op jit(solution)/shard_map/ppermute | solution.py:309
  120.3 17.9 %collective-permute-start.49 = (f32[6,32,256]{2,1,0:T(8,128)S(1)}, f32[6,32,256]{2,1,0:T(8,128)S(1)}, u32[]{:S(2)}, u32[]{:S(2)}) collective-permute-start(f32[6,32,256]{2,1,0:T(8,128)S(1)} %get-tuple-element.103), channel_id=1, source_target_pairs={{0,8},{1,9},{2,10},{3,11},{4,12},{5,13},{6,14},{7,15},{8,0},{9,1},... | collective-permute-start | bytes 589832 | tf_op jit(solution)/shard_map/ppermute | solution.py:309
  133.3 18.5 %collective-permute-start.22 = (f32[12,32,256]{2,1,0:T(8,128)S(1)}, f32[12,32,256]{2,1,0:T(8,128)S(1)}, u32[]{:S(2)}, u32[]{:S(2)}) collective-permute-start(f32[12,32,256]{2,1,0:T(8,128)S(1)} %get-tuple-element.81), channel_id=1, source_target_pairs={{0,2},{1,3},{2,0},{3,1},{4,6},{5,7},{6,4},{7,5},{8,10},{9,11},{10,... | collective-permute-start | bytes 1179656 | tf_op jit(solution)/shard_map/ppermute | solution.py:309
  141.0 15.0 %collective-permute-start.50 = (f32[12,32,256]{2,1,0:T(8,128)S(1)}, f32[12,32,256]{2,1,0:T(8,128)S(1)}, u32[]{:S(2)}, u32[]{:S(2)}) collective-permute-start(f32[12,32,256]{2,1,0:T(8,128)S(1)} %get-tuple-element.105), channel_id=1, source_target_pairs={{0,2},{1,3},{2,0},{3,1},{4,6},{5,7},{6,4},{7,5},{8,10},{9,11},{10,... | collective-permute-start | bytes 1179656 | tf_op jit(solution)/shard_map/ppermute | solution.py:309
  156.9 11.6 %collective-permute-start.26 = (f32[6,32,256]{2,1,0:T(8,128)S(1)}, f32[6,32,256]{2,1,0:T(8,128)S(1)}, u32[]{:S(2)}, u32[]{:S(2)}) collective-permute-start(f32[6,32,256]{2,1,0:T(8,128)S(1)} %get-tuple-element.86), channel_id=1, source_target_pairs={{0,4},{1,5},{2,6},{3,7},{4,0},{5,1},{6,2},{7,3},{8,12},{9,13},{10,... | collective-permute-start | bytes 589832 | tf_op jit(solution)/shard_map/ppermute | solution.py:309
  158.8 13.0 %collective-permute-start.27 = (f32[6,32,256]{2,1,0:T(8,128)S(1)}, f32[6,32,256]{2,1,0:T(8,128)S(1)}, u32[]{:S(2)}, u32[]{:S(2)}) collective-permute-start(f32[6,32,256]{2,1,0:T(8,128)S(1)} %get-tuple-element.87), channel_id=1, source_target_pairs={{0,8},{1,9},{2,10},{3,11},{4,12},{5,13},{6,14},{7,15},{8,0},{9,1},... | collective-permute-start | bytes 589832 | tf_op jit(solution)/shard_map/ppermute | solution.py:309
  161.4 15.3 %collective-permute-start.54 = (f32[6,32,256]{2,1,0:T(8,128)S(1)}, f32[6,32,256]{2,1,0:T(8,128)S(1)}, u32[]{:S(2)}, u32[]{:S(2)}) collective-permute-start(f32[6,32,256]{2,1,0:T(8,128)S(1)} %get-tuple-element.110), channel_id=1, source_target_pairs={{0,4},{1,5},{2,6},{3,7},{4,0},{5,1},{6,2},{7,3},{8,12},{9,13},{10,... | collective-permute-start | bytes 589832 | tf_op jit(solution)/shard_map/ppermute | solution.py:309
  161.5 17.9 %collective-permute-start.55 = (f32[6,32,256]{2,1,0:T(8,128)S(1)}, f32[6,32,256]{2,1,0:T(8,128)S(1)}, u32[]{:S(2)}, u32[]{:S(2)}) collective-permute-start(f32[6,32,256]{2,1,0:T(8,128)S(1)} %get-tuple-element.111), channel_id=1, source_target_pairs={{0,8},{1,9},{2,10},{3,11},{4,12},{5,13},{6,14},{7,15},{8,0},{9,1},... | collective-permute-start | bytes 589832 | tf_op jit(solution)/shard_map/ppermute | solution.py:309
  (29 other events, 211.4 us)

commit v4 on v3

--- a/solution.py
+++ b/solution.py
@@ -10,6 +10,7 @@
 LEVELS = 3
 CAP = 2
 CHUNKS = 2
+STAGGERED = (1,)
 CORE, SIDE, LINE = 1, 2, 4
 F32 = jnp.float32
 BF16 = jnp.bfloat16
@@ -319,7 +320,7 @@
     asked, places = tables(neighbour_devices, neighbour_slots, members, position)
     asked_size, place_size = asked.shape[0] // (LEVELS - 1), places.shape[0] // (LEVELS - 1)
     travel = sorted(whole[1:], key=lambda offset: (offset.bit_count(), -offset))
-    shared = {}
+    shared, ahead = {}, {}
     columns = [None] * CHUNKS
 
     def chain(chunk):
@@ -334,9 +335,15 @@
             for offset in travel:
                 bit = low_bit(offset)
                 held[offset] = flip_move(held[offset ^ bit], bit * LINE)
-            near = [array for offset in whole for array in (held[offset], flip_move(held[offset], CORE))]
-            yield
+            near = []
+            for offset in whole:
+                swapped = held[offset]
+                if offset and (level, chunk - 1) in ahead:
+                    swapped, _ = lax.optimization_barrier((swapped, ahead[level, chunk - 1]))
+                near += [held[offset], flip_move(swapped, CORE)]
             packs = pack(asked, (level - 1) * asked_size, near, whole, listed)
+            if level in STAGGERED:
+                ahead[level, chunk] = packs[0]
             far = [flip_move(array, bits) for array, bits in zip(packs, (SIDE, LINE, LINE | SIDE))]
             yield
             result, parts = call(

time: 182 us -> 181 us (level)
  transfers between devices with their start and end apart: 56 -> 56, of which waited for: 31 -> 32; matrix products, arithmetic and copies ran while one was open for 2% -> 2% of each run, Pallas kernels for 24% -> 24%
where the time goes in v4:
time: 181 us
  waiting for transfers between devices  78.9 us (44%)
  starting transfers between devices  49.1 us (27%)
  Pallas kernels  47 us (26%)
  local copies, waits for them, and re-layouts  2.55 us (1%)
  other arithmetic  2.53 us (1%)
    ppermute x56, waiting for transfers between devices, flip_move(): lax.ppermute(array, 'blk', [(source, source ^ bits) for source in range(m...  78.9 us
    ppermute x56, starting transfers between devices, flip_move(): lax.ppermute(array, 'blk', [(source, source ^ bits) for source in range(m...  49.1 us
    pallas_call x25, Pallas kernels, run(): pl.pallas_call(kernel, out_shape=out_shape, grid_spec=pltpu.PrefetchScala...  47 us
  transfers between devices with their start and end apart: 56, of which 32 were waited for; matrix products, arithmetic and copies ran while one was open for 2% of the time, Pallas kernels for 24%

profile of v4, /device:TPU:0, one launch (start us, length us, event | category | flops | bytes accessed | tf_op | source)
XLA Modules:
  0.0 180.6 jit_solution(6776188412982434880)
XLA Ops:
  1.9 3.1 %collective-permute-start.1 = (f32[6,32,256]{2,1,0:T(8,128)S(1)}, f32[6,32,256]{2,1,0:T(8,128)S(1)}, u32[]{:S(2)}, u32[]{:S(2)}) collective-permute-start(f32[6,32,256]{2,1,0:T(8,128)S(1)} %shard_map.100.refs_0_.refs_4_.panel_ref), channel_id=1, source_target_pairs={{0,4},{1,5},{2,6},{3,7},{4,0},{5,1},{6,2},{7,3},{8,12},{9,13},{10,... | collective-permute-start | bytes 589832 | tf_op jit(solution)/shard_map/ppermute | solution.py:310
  5.0 2.6 %collective-permute-start.3 = (f32[6,32,256]{2,1,0:T(8,128)S(1)}, f32[6,32,256]{2,1,0:T(8,128)S(1)}, u32[]{:S(2)}, u32[]{:S(2)}) collective-permute-start(f32[6,32,256]{2,1,0:T(8,128)S(1)} %shard_map.100.refs_0_.refs_4_.panel_ref), channel_id=1, source_target_pairs={{0,8},{1,9},{2,10},{3,11},{4,12},{5,13},{6,14},{7,15},{8,0},{9,1},... | collective-permute-start | bytes 589832 | tf_op jit(solution)/shard_map/ppermute | solution.py:310
  17.7 4.8 %collective-permute-done.29.refs_2_.refs_6_ = f32[6,32,256]{2,1,0:T(8,128)S(1)} collective-permute-done((f32[6,32,256]{2,1,0:T(8,128)S(1)}, f32[6,32,256]{2,1,0:T(8,128)S(1)}, u32[]{:S(2)}, u32[]{:S(2)}) %collective-permute-start.29) | collective-permute-done | bytes 196640 | tf_op jit(solution)/shard_map/ppermute | solution.py:310
  22.5 2.6 %collective-permute-done.31.refs_4_.refs_8_ = f32[6,32,256]{2,1,0:T(8,128)S(1)} collective-permute-done((f32[6,32,256]{2,1,0:T(8,128)S(1)}, f32[6,32,256]{2,1,0:T(8,128)S(1)}, u32[]{:S(2)}, u32[]{:S(2)}) %collective-permute-start.31) | collective-permute-done | bytes 196640 | tf_op jit(solution)/shard_map/ppermute | solution.py:310
  33.5 2.7 %shard_map.101 = (bf16[18,256,256]{2,1,0:T(8,128)(2,1)S(1)}, bf16[18,256,256]{2,1,0:T(8,128)(2,1)S(1)}) custom-call(f32[1,18,256,256]{3,2,1,0:T(8,128)} %bitcast.58, f32[1,18,256,256]{3,2,1,0:T(8,128)} %bitcast.59, f32[1,18,256,256]{3,2,1,0:T(8,128)} %bitcast.60), custom_call_target="tpu_custom_call" | custom-call | flops 600000000 | bytes 3000000 | tf_op jit(solution)/shard_map/pallas_call | solution.py:109
  36.2 4.0 %shard_map.102 = (bf16[24,256,256]{2,1,0:T(8,128)(2,1)S(1)}, bf16[24,256,256]{2,1,0:T(8,128)(2,1)S(1)}) custom-call(f32[2,24,256,256]{3,2,1,0:T(8,128)} %bitcast.50, f32[2,24,256,256]{3,2,1,0:T(8,128)} %bitcast.51, f32[2,24,256,256]{3,2,1,0:T(8,128)} %bitcast.52, f32[2,24,256,256]{3,2,1,0:T(8,128)} %bitcast.53), custom_call_target="tpu_custom_call" | custom-call | flops 600000000 | bytes 3000000 | tf_op jit(solution)/shard_map/pallas_call | solution.py:109
  40.2 2.8 %collective-permute-done.5.refs_10_ = f32[12,32,256]{2,1,0:T(8,128)S(1)} collective-permute-done((f32[12,32,256]{2,1,0:T(8,128)S(1)}, f32[12,32,256]{2,1,0:T(8,128)S(1)}, u32[]{:S(2)}, u32[]{:S(2)}) %collective-permute-start.5) | collective-permute-done | bytes 393248 | tf_op jit(solution)/shard_map/ppermute | solution.py:310
  43.1 3.5 %shard_map.104.refs_0_.refs_4_.panel_ref = f32[6,32,256]{2,1,0:T(8,128)S(1)} custom-call(s32[48]{0:T(128)S(1)} %fusion.6.place_ref, f32[3,6,64,256]{3,2,1,0:T(8,128)S(1)} %copy-done, bf16[18,256,256]{2,1,0:T(8,128)(2,1)S(1)} %get-tuple-element.62.refs_0_, bf16[18,256,256]{2,1,0:T(8,128)(2,1)S(1)} %get-tuple-element.63.refs_1_, ...), custom_call_target="tpu_custom_call" | custom-call | flops 600000000 | bytes 3000000 | tf_op jit(solution)/shard_map/pallas_call | solution.py:109
  47.0 2.6 %collective-permute-start.11 = (f32[6,32,256]{2,1,0:T(8,128)S(1)}, f32[6,32,256]{2,1,0:T(8,128)S(1)}, u32[]{:S(2)}, u32[]{:S(2)}) collective-permute-start(f32[6,32,256]{2,1,0:T(8,128)S(1)} %shard_map.104.refs_0_.refs_4_.panel_ref), channel_id=1, source_target_pairs={{0,8},{1,9},{2,10},{3,11},{4,12},{5,13},{6,14},{7,15},{8,0},{9,1},... | collective-permute-start | bytes 589832 | tf_op jit(solution)/shard_map/ppermute | solution.py:310
  51.0 3.5 %shard_map.116.refs_0_.refs_4_.panel_ref = f32[6,32,256]{2,1,0:T(8,128)S(1)} custom-call(s32[48]{0:T(128)S(1)} %fusion.6.place_ref, f32[3,6,64,256]{3,2,1,0:T(8,128)S(1)} %copy-done, bf16[18,256,256]{2,1,0:T(8,128)(2,1)S(1)} %get-tuple-element.62.refs_0_, bf16[18,256,256]{2,1,0:T(8,128)(2,1)S(1)} %get-tuple-element.63.refs_1_, ...), custom_call_target="tpu_custom_call" | custom-call | flops 600000000 | bytes 3000000 | tf_op jit(solution)/shard_map/pallas_call | solution.py:109
  55.0 2.6 %collective-permute-start.39 = (f32[6,32,256]{2,1,0:T(8,128)S(1)}, f32[6,32,256]{2,1,0:T(8,128)S(1)}, u32[]{:S(2)}, u32[]{:S(2)}) collective-permute-start(f32[6,32,256]{2,1,0:T(8,128)S(1)} %shard_map.116.refs_0_.refs_4_.panel_ref), channel_id=1, source_target_pairs={{0,8},{1,9},{2,10},{3,11},{4,12},{5,13},{6,14},{7,15},{8,0},{9,1},... | collective-permute-start | bytes 589832 | tf_op jit(solution)/shard_map/ppermute | solution.py:310
  58.6 6.6 %collective-permute-done.37.refs_2_.refs_6_ = f32[6,32,256]{2,1,0:T(8,128)S(1)} collective-permute-done((f32[6,32,256]{2,1,0:T(8,128)S(1)}, f32[6,32,256]{2,1,0:T(8,128)S(1)}, u32[]{:S(2)}, u32[]{:S(2)}) %collective-permute-start.37) | collective-permute-done | bytes 196640 | tf_op jit(solution)/shard_map/ppermute | solution.py:310
  70.4 2.5 %collective-permute-start.15 = (f32[4,32,256]{2,1,0:T(8,128)S(1)}, f32[4,32,256]{2,1,0:T(8,128)S(1)}, u32[]{:S(2)}, u32[]{:S(2)}) collective-permute-start(f32[4,32,256]{2,1,0:T(8,128)S(1)} %get-tuple-element.73), channel_id=1, source_target_pairs={{0,6},{1,7},{2,4},{3,5},{4,2},{5,3},{6,0},{7,1},{8,14},{9,15},{10,... | collective-permute-start | bytes 393224 | tf_op jit(solution)/shard_map/ppermute | solution.py:310
  73.1 3.4 %collective-permute-done.14.refs_11_ = f32[4,32,256]{2,1,0:T(8,128)S(1)} collective-permute-done((f32[4,32,256]{2,1,0:T(8,128)S(1)}, f32[4,32,256]{2,1,0:T(8,128)S(1)}, u32[]{:S(2)}, u32[]{:S(2)}) %collective-permute-start.14) | collective-permute-done | bytes 131104 | tf_op jit(solution)/shard_map/ppermute | solution.py:310
  77.5 4.1 %shard_map.105 = (bf16[24,256,256]{2,1,0:T(8,128)(2,1)S(1)}, bf16[24,256,256]{2,1,0:T(8,128)(2,1)S(1)}) custom-call(f32[2,24,256,256]{3,2,1,0:T(8,128)} %bitcast.54, f32[2,24,256,256]{3,2,1,0:T(8,128)} %bitcast.55, f32[2,24,256,256]{3,2,1,0:T(8,128)} %bitcast.56, f32[2,24,256,256]{3,2,1,0:T(8,128)} %bitcast.57), custom_call_target="tpu_custom_call" | custom-call | flops 600000000 | bytes 3000000 | tf_op jit(solution)/shard_map/pallas_call | solution.py:109
  83.7 6.2 %shard_map.107 = (f32[6,32,256]{2,1,0:T(8,128)S(1)}, f32[36,32,256]{2,1,0:T(8,128)S(1)}, f32[12,32,256]{2,1,0:T(8,128)S(1)}, f32[4,32,256]{2,1,0:T(8,128)S(1)}, f32[4,32,256]{2,1,0:T(8,128)S(1)}) custom-call(s32[48]{0:T(128)S(1)} %fusion.6.place_ref, f32[3,6,64,256]{3,2,1,0:T(8,128)S(1)} %copy-done, bf16[18,256,256]{2,1,0:T(8,128)(2,1)S(1)} %get-tuple-element.62.refs_0_, ...), custom_call_target="tpu_custom_call" | custom-call | flops 600000000 | bytes 3000000 | tf_op jit(solution)/shard_map/pallas_call | solution.py:109
  90.0 2.5 %collective-permute-start.16 = (f32[12,32,256]{2,1,0:T(8,128)S(1)}, f32[12,32,256]{2,1,0:T(8,128)S(1)}, u32[]{:S(2)}, u32[]{:S(2)}) collective-permute-start(f32[12,32,256]{2,1,0:T(8,128)S(1)} %get-tuple-element.75), channel_id=1, source_target_pairs={{0,2},{1,3},{2,0},{3,1},{4,6},{5,7},{6,4},{7,5},{8,10},{9,11},{10,... | collective-permute-start | bytes 1179656 | tf_op jit(solution)/shard_map/ppermute | solution.py:310
  92.7 6.2 %shard_map.118 = (f32[6,32,256]{2,1,0:T(8,128)S(1)}, f32[36,32,256]{2,1,0:T(8,128)S(1)}, f32[12,32,256]{2,1,0:T(8,128)S(1)}, f32[4,32,256]{2,1,0:T(8,128)S(1)}, f32[4,32,256]{2,1,0:T(8,128)S(1)}) custom-call(s32[48]{0:T(128)S(1)} %fusion.6.place_ref, f32[3,6,64,256]{3,2,1,0:T(8,128)S(1)} %copy-done, bf16[18,256,256]{2,1,0:T(8,128)(2,1)S(1)} %get-tuple-element.62.refs_0_, ...), custom_call_target="tpu_custom_call" | custom-call | flops 600000000 | bytes 3000000 | tf_op jit(solution)/shard_map/pallas_call | solution.py:109
  102.8 4.2 %collective-permute-done.17.refs_1_ = f32[4,32,256]{2,1,0:T(8,128)S(1)} collective-permute-done((f32[4,32,256]{2,1,0:T(8,128)S(1)}, f32[4,32,256]{2,1,0:T(8,128)S(1)}, u32[]{:S(2)}, u32[]{:S(2)}) %collective-permute-start.17) | collective-permute-done | bytes 131104 | tf_op jit(solution)/shard_map/ppermute | solution.py:310
  107.0 2.8 %collective-permute-done.18.refs_2_ = f32[4,32,256]{2,1,0:T(8,128)S(1)} collective-permute-done((f32[4,32,256]{2,1,0:T(8,128)S(1)}, f32[4,32,256]{2,1,0:T(8,128)S(1)}, u32[]{:S(2)}, u32[]{:S(2)}) %collective-permute-start.18) | collective-permute-done | bytes 131104 | tf_op jit(solution)/shard_map/ppermute | solution.py:310
  116.7 2.6 %collective-permute-start.21 = (f32[6,32,256]{2,1,0:T(8,128)S(1)}, f32[6,32,256]{2,1,0:T(8,128)S(1)}, u32[]{:S(2)}, u32[]{:S(2)}) collective-permute-start(f32[6,32,256]{2,1,0:T(8,128)S(1)} %get-tuple-element.81), channel_id=1, source_target_pairs={{0,8},{1,9},{2,10},{3,11},{4,12},{5,13},{6,14},{7,15},{8,0},{9,1},... | collective-permute-start | bytes 589832 | tf_op jit(solution)/shard_map/ppermute | solution.py:310
  121.5 6.5 %collective-permute-done.20.refs_6_ = f32[6,32,256]{2,1,0:T(8,128)S(1)} collective-permute-done((f32[6,32,256]{2,1,0:T(8,128)S(1)}, f32[6,32,256]{2,1,0:T(8,128)S(1)}, u32[]{:S(2)}, u32[]{:S(2)}) %collective-permute-start.20) | collective-permute-done | bytes 196640 | tf_op jit(solution)/shard_map/ppermute | solution.py:310
  129.7 2.8 %shard_map.110 = (f32[6,32,256]{2,1,0:T(8,128)S(1)}, f32[36,32,256]{2,1,0:T(8,128)S(1)}, f32[12,32,256]{2,1,0:T(8,128)S(1)}, f32[4,32,256]{2,1,0:T(8,128)S(1)}, f32[4,32,256]{2,1,0:T(8,128)S(1)}) custom-call(s32[48]{0:T(128)S(1)} %fusion.6.place_ref, f32[6,32,256]{2,1,0:T(8,128)S(1)} %shard_map.104.refs_0_.refs_4_.panel_ref, ...), custom_call_target="tpu_custom_call" | custom-call | flops 600000000 | bytes 3000000 | tf_op jit(solution)/shard_map/pallas_call | solution.py:109
  137.4 2.8 %shard_map.121 = (f32[6,32,256]{2,1,0:T(8,128)S(1)}, f32[36,32,256]{2,1,0:T(8,128)S(1)}, f32[12,32,256]{2,1,0:T(8,128)S(1)}, f32[4,32,256]{2,1,0:T(8,128)S(1)}, f32[4,32,256]{2,1,0:T(8,128)S(1)}) custom-call(s32[48]{0:T(128)S(1)} %fusion.6.place_ref, f32[6,32,256]{2,1,0:T(8,128)S(1)} %shard_map.116.refs_0_.refs_4_.panel_ref, ...), custom_call_target="tpu_custom_call" | custom-call | flops 600000000 | bytes 3000000 | tf_op jit(solution)/shard_map/pallas_call | solution.py:109
  144.0 4.2 %collective-permute-done.23.refs_1_ = f32[4,32,256]{2,1,0:T(8,128)S(1)} collective-permute-done((f32[4,32,256]{2,1,0:T(8,128)S(1)}, f32[4,32,256]{2,1,0:T(8,128)S(1)}, u32[]{:S(2)}, u32[]{:S(2)}) %collective-permute-start.23) | collective-permute-done | bytes 131104 | tf_op jit(solution)/shard_map/ppermute | solution.py:310
  148.4 2.5 %collective-permute-done.24.refs_2_ = f32[4,32,256]{2,1,0:T(8,128)S(1)} collective-permute-done((f32[4,32,256]{2,1,0:T(8,128)S(1)}, f32[4,32,256]{2,1,0:T(8,128)S(1)}, u32[]{:S(2)}, u32[]{:S(2)}) %collective-permute-start.24) | collective-permute-done | bytes 131104 | tf_op jit(solution)/shard_map/ppermute | solution.py:310
  152.3 2.3 %collective-permute-done.52.refs_2_ = f32[4,32,256]{2,1,0:T(8,128)S(1)} collective-permute-done((f32[4,32,256]{2,1,0:T(8,128)S(1)}, f32[4,32,256]{2,1,0:T(8,128)S(1)}, u32[]{:S(2)}, u32[]{:S(2)}) %collective-permute-start.52) | collective-permute-done | bytes 131104 | tf_op jit(solution)/shard_map/ppermute | solution.py:310
  158.0 2.5 %collective-permute-start.27 = (f32[6,32,256]{2,1,0:T(8,128)S(1)}, f32[6,32,256]{2,1,0:T(8,128)S(1)}, u32[]{:S(2)}, u32[]{:S(2)}) collective-permute-start(f32[6,32,256]{2,1,0:T(8,128)S(1)} %get-tuple-element.89), channel_id=1, source_target_pairs={{0,8},{1,9},{2,10},{3,11},{4,12},{5,13},{6,14},{7,15},{8,0},{9,1},... | collective-permute-start | bytes 589832 | tf_op jit(solution)/shard_map/ppermute | solution.py:310
  162.5 5.3 %collective-permute-done.26.refs_4_ = f32[6,32,256]{2,1,0:T(8,128)S(1)} collective-permute-done((f32[6,32,256]{2,1,0:T(8,128)S(1)}, f32[6,32,256]{2,1,0:T(8,128)S(1)}, u32[]{:S(2)}, u32[]{:S(2)}) %collective-permute-start.26) | collective-permute-done | bytes 196640 | tf_op jit(solution)/shard_map/ppermute | solution.py:310
  167.7 3.2 %collective-permute-done.27.refs_5_ = f32[6,32,256]{2,1,0:T(8,128)S(1)} collective-permute-done((f32[6,32,256]{2,1,0:T(8,128)S(1)}, f32[6,32,256]{2,1,0:T(8,128)S(1)}, u32[]{:S(2)}, u32[]{:S(2)}) %collective-permute-start.27) | collective-permute-done | bytes 196640 | tf_op jit(solution)/shard_map/ppermute | solution.py:310
  171.9 3.9 %collective-permute-done.54.refs_4_ = f32[6,32,256]{2,1,0:T(8,128)S(1)} collective-permute-done((f32[6,32,256]{2,1,0:T(8,128)S(1)}, f32[6,32,256]{2,1,0:T(8,128)S(1)}, u32[]{:S(2)}, u32[]{:S(2)}) %collective-permute-start.54) | collective-permute-done | bytes 196640 | tf_op jit(solution)/shard_map/ppermute | solution.py:310
  175.8 2.8 %collective-permute-done.55.refs_5_ = f32[6,32,256]{2,1,0:T(8,128)S(1)} collective-permute-done((f32[6,32,256]{2,1,0:T(8,128)S(1)}, f32[6,32,256]{2,1,0:T(8,128)S(1)}, u32[]{:S(2)}, u32[]{:S(2)}) %collective-permute-start.55) | collective-permute-done | bytes 196640 | tf_op jit(solution)/shard_map/ppermute | solution.py:310
  (162 shorter events, 65.3 us)
Async XLA Ops:
  1.9 12.9 %collective-permute-start.1 = (f32[6,32,256]{2,1,0:T(8,128)S(1)}, f32[6,32,256]{2,1,0:T(8,128)S(1)}, u32[]{:S(2)}, u32[]{:S(2)}) collective-permute-start(f32[6,32,256]{2,1,0:T(8,128)S(1)} %shard_map.100.refs_0_.refs_4_.panel_ref), channel_id=1, source_target_pairs={{0,4},{1,5},{2,6},{3,7},{4,0},{5,1},{6,2},{7,3},{8,12},{9,13},{10,... | collective-permute-start | bytes 589832 | tf_op jit(solution)/shard_map/ppermute | solution.py:310
  5.0 10.6 %collective-permute-start.3 = (f32[6,32,256]{2,1,0:T(8,128)S(1)}, f32[6,32,256]{2,1,0:T(8,128)S(1)}, u32[]{:S(2)}, u32[]{:S(2)}) collective-permute-start(f32[6,32,256]{2,1,0:T(8,128)S(1)} %shard_map.100.refs_0_.refs_4_.panel_ref), channel_id=1, source_target_pairs={{0,8},{1,9},{2,10},{3,11},{4,12},{5,13},{6,14},{7,15},{8,0},{9,1},... | collective-permute-start | bytes 589832 | tf_op jit(solution)/shard_map/ppermute | solution.py:310
  9.5 12.9 %collective-permute-start.29 = (f32[6,32,256]{2,1,0:T(8,128)S(1)}, f32[6,32,256]{2,1,0:T(8,128)S(1)}, u32[]{:S(2)}, u32[]{:S(2)}) collective-permute-start(f32[6,32,256]{2,1,0:T(8,128)S(1)} %shard_map.114.refs_0_.refs_4_.panel_ref), channel_id=1, source_target_pairs={{0,4},{1,5},{2,6},{3,7},{4,0},{5,1},{6,2},{7,3},{8,12},{9,13},{10,... | collective-permute-start | bytes 589832 | tf_op jit(solution)/shard_map/ppermute | solution.py:310
  10.0 15.0 %collective-permute-start.31 = (f32[6,32,256]{2,1,0:T(8,128)S(1)}, f32[6,32,256]{2,1,0:T(8,128)S(1)}, u32[]{:S(2)}, u32[]{:S(2)}) collective-permute-start(f32[6,32,256]{2,1,0:T(8,128)S(1)} %shard_map.114.refs_0_.refs_4_.panel_ref), channel_id=1, source_target_pairs={{0,8},{1,9},{2,10},{3,11},{4,12},{5,13},{6,14},{7,15},{8,0},{9,1},... | collective-permute-start | bytes 589832 | tf_op jit(solution)/shard_map/ppermute | solution.py:310
  15.9 11.5 %collective-permute-start.28 = (f32[6,32,256]{2,1,0:T(8,128)S(1)}, f32[6,32,256]{2,1,0:T(8,128)S(1)}, u32[]{:S(2)}, u32[]{:S(2)}) collective-permute-start(f32[6,32,256]{2,1,0:T(8,128)S(1)} %shard_map.114.refs_0_.refs_4_.panel_ref), channel_id=1, source_target_pairs={{0,1},{1,0},{2,3},{3,2},{4,5},{5,4},{6,7},{7,6},{8,9},{9,8},{10,11... | collective-permute-start | bytes 589832 | tf_op jit(solution)/shard_map/ppermute | solution.py:310
  25.5 17.5 %collective-permute-start.5 = (f32[12,32,256]{2,1,0:T(8,128)S(1)}, f32[12,32,256]{2,1,0:T(8,128)S(1)}, u32[]{:S(2)}, u32[]{:S(2)}) collective-permute-start(f32[12,32,256]{2,1,0:T(8,128)S(1)} %get-tuple-element.66), channel_id=1, source_target_pairs={{0,2},{1,3},{2,0},{3,1},{4,6},{5,7},{6,4},{7,5},{8,10},{9,11},{10,... | collective-permute-start | bytes 1179656 | tf_op jit(solution)/shard_map/ppermute | solution.py:310
  27.5 12.8 %collective-permute-start.7 = (f32[4,32,256]{2,1,0:T(8,128)S(1)}, f32[4,32,256]{2,1,0:T(8,128)S(1)}, u32[]{:S(2)}, u32[]{:S(2)}) collective-permute-start(f32[4,32,256]{2,1,0:T(8,128)S(1)} %get-tuple-element.68), channel_id=1, source_target_pairs={{0,6},{1,7},{2,4},{3,5},{4,2},{5,3},{6,0},{7,1},{8,14},{9,15},{10,... | collective-permute-start | bytes 393224 | tf_op jit(solution)/shard_map/ppermute | solution.py:310
  29.6 21.4 %collective-permute-start.33 = (f32[12,32,256]{2,1,0:T(8,128)S(1)}, f32[12,32,256]{2,1,0:T(8,128)S(1)}, u32[]{:S(2)}, u32[]{:S(2)}) collective-permute-start(f32[12,32,256]{2,1,0:T(8,128)S(1)} %get-tuple-element.94), channel_id=1, source_target_pairs={{0,2},{1,3},{2,0},{3,1},{4,6},{5,7},{6,4},{7,5},{8,10},{9,11},{10,... | collective-permute-start | bytes 1179656 | tf_op jit(solution)/shard_map/ppermute | solution.py:310
  31.2 18.3 %collective-permute-start.34 = (f32[4,32,256]{2,1,0:T(8,128)S(1)}, f32[4,32,256]{2,1,0:T(8,128)S(1)}, u32[]{:S(2)}, u32[]{:S(2)}) collective-permute-start(f32[4,32,256]{2,1,0:T(8,128)S(1)} %get-tuple-element.95), channel_id=1, source_target_pairs={{0,4},{1,5},{2,6},{3,7},{4,0},{5,1},{6,2},{7,3},{8,12},{9,13},{10,... | collective-permute-start | bytes 393224 | tf_op jit(solution)/shard_map/ppermute | solution.py:310
  33.4 16.2 %collective-permute-start.35 = (f32[4,32,256]{2,1,0:T(8,128)S(1)}, f32[4,32,256]{2,1,0:T(8,128)S(1)}, u32[]{:S(2)}, u32[]{:S(2)}) collective-permute-start(f32[4,32,256]{2,1,0:T(8,128)S(1)} %get-tuple-element.96), channel_id=1, source_target_pairs={{0,6},{1,7},{2,4},{3,5},{4,2},{5,3},{6,0},{7,1},{8,14},{9,15},{10,... | collective-permute-start | bytes 393224 | tf_op jit(solution)/shard_map/ppermute | solution.py:310
  46.6 11.1 %collective-permute-start.9 = (f32[6,32,256]{2,1,0:T(8,128)S(1)}, f32[6,32,256]{2,1,0:T(8,128)S(1)}, u32[]{:S(2)}, u32[]{:S(2)}) collective-permute-start(f32[6,32,256]{2,1,0:T(8,128)S(1)} %shard_map.104.refs_0_.refs_4_.panel_ref), channel_id=1, source_target_pairs={{0,4},{1,5},{2,6},{3,7},{4,0},{5,1},{6,2},{7,3},{8,12},{9,13},{10,... | collective-permute-start | bytes 589832 | tf_op jit(solution)/shard_map/ppermute | solution.py:310
  47.0 11.1 %collective-permute-start.11 = (f32[6,32,256]{2,1,0:T(8,128)S(1)}, f32[6,32,256]{2,1,0:T(8,128)S(1)}, u32[]{:S(2)}, u32[]{:S(2)}) collective-permute-start(f32[6,32,256]{2,1,0:T(8,128)S(1)} %shard_map.104.refs_0_.refs_4_.panel_ref), channel_id=1, source_target_pairs={{0,8},{1,9},{2,10},{3,11},{4,12},{5,13},{6,14},{7,15},{8,0},{9,1},... | collective-permute-start | bytes 589832 | tf_op jit(solution)/shard_map/ppermute | solution.py:310
  54.5 10.7 %collective-permute-start.37 = (f32[6,32,256]{2,1,0:T(8,128)S(1)}, f32[6,32,256]{2,1,0:T(8,128)S(1)}, u32[]{:S(2)}, u32[]{:S(2)}) collective-permute-start(f32[6,32,256]{2,1,0:T(8,128)S(1)} %shard_map.116.refs_0_.refs_4_.panel_ref), channel_id=1, source_target_pairs={{0,4},{1,5},{2,6},{3,7},{4,0},{5,1},{6,2},{7,3},{8,12},{9,13},{10,... | collective-permute-start | bytes 589832 | tf_op jit(solution)/shard_map/ppermute | solution.py:310
  55.0 11.4 %collective-permute-start.39 = (f32[6,32,256]{2,1,0:T(8,128)S(1)}, f32[6,32,256]{2,1,0:T(8,128)S(1)}, u32[]{:S(2)}, u32[]{:S(2)}) collective-permute-start(f32[6,32,256]{2,1,0:T(8,128)S(1)} %shard_map.116.refs_0_.refs_4_.panel_ref), channel_id=1, source_target_pairs={{0,8},{1,9},{2,10},{3,11},{4,12},{5,13},{6,14},{7,15},{8,0},{9,1},... | collective-permute-start | bytes 589832 | tf_op jit(solution)/shard_map/ppermute | solution.py:310
  58.1 10.5 %collective-permute-start.36 = (f32[6,32,256]{2,1,0:T(8,128)S(1)}, f32[6,32,256]{2,1,0:T(8,128)S(1)}, u32[]{:S(2)}, u32[]{:S(2)}) collective-permute-start(f32[6,32,256]{2,1,0:T(8,128)S(1)} %shard_map.116.refs_0_.refs_4_.panel_ref), channel_id=1, source_target_pairs={{0,1},{1,0},{2,3},{3,2},{4,5},{5,4},{6,7},{7,6},{8,9},{9,8},{10,11... | collective-permute-start | bytes 589832 | tf_op jit(solution)/shard_map/ppermute | solution.py:310
  67.1 16.6 %collective-permute-start.13 = (f32[12,32,256]{2,1,0:T(8,128)S(1)}, f32[12,32,256]{2,1,0:T(8,128)S(1)}, u32[]{:S(2)}, u32[]{:S(2)}) collective-permute-start(f32[12,32,256]{2,1,0:T(8,128)S(1)} %get-tuple-element.71), channel_id=1, source_target_pairs={{0,2},{1,3},{2,0},{3,1},{4,6},{5,7},{6,4},{7,5},{8,10},{9,11},{10,... | collective-permute-start | bytes 1179656 | tf_op jit(solution)/shard_map/ppermute | solution.py:310
  69.3 23.4 %collective-permute-start.41 = (f32[12,32,256]{2,1,0:T(8,128)S(1)}, f32[12,32,256]{2,1,0:T(8,128)S(1)}, u32[]{:S(2)}, u32[]{:S(2)}) collective-permute-start(f32[12,32,256]{2,1,0:T(8,128)S(1)} %get-tuple-element.97), channel_id=1, source_target_pairs={{0,2},{1,3},{2,0},{3,1},{4,6},{5,7},{6,4},{7,5},{8,10},{9,11},{10,... | collective-permute-start | bytes 1179656 | tf_op jit(solution)/shard_map/ppermute | solution.py:310
  70.4 11.2 %collective-permute-start.15 = (f32[4,32,256]{2,1,0:T(8,128)S(1)}, f32[4,32,256]{2,1,0:T(8,128)S(1)}, u32[]{:S(2)}, u32[]{:S(2)}) collective-permute-start(f32[4,32,256]{2,1,0:T(8,128)S(1)} %get-tuple-element.73), channel_id=1, source_target_pairs={{0,6},{1,7},{2,4},{3,5},{4,2},{5,3},{6,0},{7,1},{8,14},{9,15},{10,... | collective-permute-start | bytes 393224 | tf_op jit(solution)/shard_map/ppermute | solution.py:310
  72.8 19.7 %collective-permute-start.42 = (f32[4,32,256]{2,1,0:T(8,128)S(1)}, f32[4,32,256]{2,1,0:T(8,128)S(1)}, u32[]{:S(2)}, u32[]{:S(2)}) collective-permute-start(f32[4,32,256]{2,1,0:T(8,128)S(1)} %get-tuple-element.98), channel_id=1, source_target_pairs={{0,4},{1,5},{2,6},{3,7},{4,0},{5,1},{6,2},{7,3},{8,12},{9,13},{10,... | collective-permute-start | bytes 393224 | tf_op jit(solution)/shard_map/ppermute | solution.py:310
  76.5 16.0 %collective-permute-start.43 = (f32[4,32,256]{2,1,0:T(8,128)S(1)}, f32[4,32,256]{2,1,0:T(8,128)S(1)}, u32[]{:S(2)}, u32[]{:S(2)}) collective-permute-start(f32[4,32,256]{2,1,0:T(8,128)S(1)} %get-tuple-element.99), channel_id=1, source_target_pairs={{0,6},{1,7},{2,4},{3,5},{4,2},{5,3},{6,0},{7,1},{8,14},{9,15},{10,... | collective-permute-start | bytes 393224 | tf_op jit(solution)/shard_map/ppermute | solution.py:310
  90.0 19.8 %collective-permute-start.16 = (f32[12,32,256]{2,1,0:T(8,128)S(1)}, f32[12,32,256]{2,1,0:T(8,128)S(1)}, u32[]{:S(2)}, u32[]{:S(2)}) collective-permute-start(f32[12,32,256]{2,1,0:T(8,128)S(1)} %get-tuple-element.75), channel_id=1, source_target_pairs={{0,2},{1,3},{2,0},{3,1},{4,6},{5,7},{6,4},{7,5},{8,10},{9,11},{10,... | collective-permute-start | bytes 1179656 | tf_op jit(solution)/shard_map/ppermute | solution.py:310
  99.0 16.4 %collective-permute-start.44 = (f32[12,32,256]{2,1,0:T(8,128)S(1)}, f32[12,32,256]{2,1,0:T(8,128)S(1)}, u32[]{:S(2)}, u32[]{:S(2)}) collective-permute-start(f32[12,32,256]{2,1,0:T(8,128)S(1)} %get-tuple-element.101), channel_id=1, source_target_pairs={{0,2},{1,3},{2,0},{3,1},{4,6},{5,7},{6,4},{7,5},{8,10},{9,11},{10,... | collective-permute-start | bytes 1179656 | tf_op jit(solution)/shard_map/ppermute | solution.py:310
  116.3 11.6 %collective-permute-start.20 = (f32[6,32,256]{2,1,0:T(8,128)S(1)}, f32[6,32,256]{2,1,0:T(8,128)S(1)}, u32[]{:S(2)}, u32[]{:S(2)}) collective-permute-start(f32[6,32,256]{2,1,0:T(8,128)S(1)} %get-tuple-element.80), channel_id=1, source_target_pairs={{0,4},{1,5},{2,6},{3,7},{4,0},{5,1},{6,2},{7,3},{8,12},{9,13},{10,... | collective-permute-start | bytes 589832 | tf_op jit(solution)/shard_map/ppermute | solution.py:310
  116.7 13.0 %collective-permute-start.21 = (f32[6,32,256]{2,1,0:T(8,128)S(1)}, f32[6,32,256]{2,1,0:T(8,128)S(1)}, u32[]{:S(2)}, u32[]{:S(2)}) collective-permute-start(f32[6,32,256]{2,1,0:T(8,128)S(1)} %get-tuple-element.81), channel_id=1, source_target_pairs={{0,8},{1,9},{2,10},{3,11},{4,12},{5,13},{6,14},{7,15},{8,0},{9,1},... | collective-permute-start | bytes 589832 | tf_op jit(solution)/shard_map/ppermute | solution.py:310
  119.3 16.7 %collective-permute-start.48 = (f32[6,32,256]{2,1,0:T(8,128)S(1)}, f32[6,32,256]{2,1,0:T(8,128)S(1)}, u32[]{:S(2)}, u32[]{:S(2)}) collective-permute-start(f32[6,32,256]{2,1,0:T(8,128)S(1)} %get-tuple-element.106), channel_id=1, source_target_pairs={{0,4},{1,5},{2,6},{3,7},{4,0},{5,1},{6,2},{7,3},{8,12},{9,13},{10,... | collective-permute-start | bytes 589832 | tf_op jit(solution)/shard_map/ppermute | solution.py:310
  119.5 17.9 %collective-permute-start.49 = (f32[6,32,256]{2,1,0:T(8,128)S(1)}, f32[6,32,256]{2,1,0:T(8,128)S(1)}, u32[]{:S(2)}, u32[]{:S(2)}) collective-permute-start(f32[6,32,256]{2,1,0:T(8,128)S(1)} %get-tuple-element.107), channel_id=1, source_target_pairs={{0,8},{1,9},{2,10},{3,11},{4,12},{5,13},{6,14},{7,15},{8,0},{9,1},... | collective-permute-start | bytes 589832 | tf_op jit(solution)/shard_map/ppermute | solution.py:310
  132.4 18.5 %collective-permute-start.22 = (f32[12,32,256]{2,1,0:T(8,128)S(1)}, f32[12,32,256]{2,1,0:T(8,128)S(1)}, u32[]{:S(2)}, u32[]{:S(2)}) collective-permute-start(f32[12,32,256]{2,1,0:T(8,128)S(1)} %get-tuple-element.83), channel_id=1, source_target_pairs={{0,2},{1,3},{2,0},{3,1},{4,6},{5,7},{6,4},{7,5},{8,10},{9,11},{10,... | collective-permute-start | bytes 1179656 | tf_op jit(solution)/shard_map/ppermute | solution.py:310
  140.2 15.0 %collective-permute-start.50 = (f32[12,32,256]{2,1,0:T(8,128)S(1)}, f32[12,32,256]{2,1,0:T(8,128)S(1)}, u32[]{:S(2)}, u32[]{:S(2)}) collective-permute-start(f32[12,32,256]{2,1,0:T(8,128)S(1)} %get-tuple-element.109), channel_id=1, source_target_pairs={{0,2},{1,3},{2,0},{3,1},{4,6},{5,7},{6,4},{7,5},{8,10},{9,11},{10,... | collective-permute-start | bytes 1179656 | tf_op jit(solution)/shard_map/ppermute | solution.py:310
  156.1 11.6 %collective-permute-start.26 = (f32[6,32,256]{2,1,0:T(8,128)S(1)}, f32[6,32,256]{2,1,0:T(8,128)S(1)}, u32[]{:S(2)}, u32[]{:S(2)}) collective-permute-start(f32[6,32,256]{2,1,0:T(8,128)S(1)} %get-tuple-element.88), channel_id=1, source_target_pairs={{0,4},{1,5},{2,6},{3,7},{4,0},{5,1},{6,2},{7,3},{8,12},{9,13},{10,... | collective-permute-start | bytes 589832 | tf_op jit(solution)/shard_map/ppermute | solution.py:310
  158.0 13.0 %collective-permute-start.27 = (f32[6,32,256]{2,1,0:T(8,128)S(1)}, f32[6,32,256]{2,1,0:T(8,128)S(1)}, u32[]{:S(2)}, u32[]{:S(2)}) collective-permute-start(f32[6,32,256]{2,1,0:T(8,128)S(1)} %get-tuple-element.89), channel_id=1, source_target_pairs={{0,8},{1,9},{2,10},{3,11},{4,12},{5,13},{6,14},{7,15},{8,0},{9,1},... | collective-permute-start | bytes 589832 | tf_op jit(solution)/shard_map/ppermute | solution.py:310
  160.5 15.3 %collective-permute-start.54 = (f32[6,32,256]{2,1,0:T(8,128)S(1)}, f32[6,32,256]{2,1,0:T(8,128)S(1)}, u32[]{:S(2)}, u32[]{:S(2)}) collective-permute-start(f32[6,32,256]{2,1,0:T(8,128)S(1)} %get-tuple-element.114), channel_id=1, source_target_pairs={{0,4},{1,5},{2,6},{3,7},{4,0},{5,1},{6,2},{7,3},{8,12},{9,13},{10,... | collective-permute-start | bytes 589832 | tf_op jit(solution)/shard_map/ppermute | solution.py:310
  160.7 17.9 %collective-permute-start.55 = (f32[6,32,256]{2,1,0:T(8,128)S(1)}, f32[6,32,256]{2,1,0:T(8,128)S(1)}, u32[]{:S(2)}, u32[]{:S(2)}) collective-permute-start(f32[6,32,256]{2,1,0:T(8,128)S(1)} %get-tuple-element.115), channel_id=1, source_target_pairs={{0,8},{1,9},{2,10},{3,11},{4,12},{5,13},{6,14},{7,15},{8,0},{9,1},... | collective-permute-start | bytes 589832 | tf_op jit(solution)/shard_map/ppermute | solution.py:310
  (29 other events, 197.8 us)

commit v5 on v4

--- a/solution.py
+++ b/solution.py
@@ -18,6 +18,7 @@
 NN = (((1,), (0,)), ((), ()))
 PARAMS = pltpu.CompilerParams(vmem_limit_bytes=20 * 1024 * 1024)
 VMEM_SPEC = pl.BlockSpec(memory_space=pltpu.VMEM)
+ANY_SPEC = pl.BlockSpec(memory_space=pl.ANY)
 
 
 def low_bit(offset):
@@ -303,6 +304,31 @@
     )
     results = run(kernel, out_shapes, (places,), operands, scratch=scratch)
     return results[0], results[1:]
+
+
+def place_kernel(*refs, spots, count):
+    sources, target, sems = refs[: len(spots)], refs[count], refs[count + 1]
+    copies = []
+    for index, (source, (level, chunk)) in enumerate(zip(sources, spots)):
+        rows = source.shape[1]
+        goal = target.at[level, :, pl.ds(chunk * rows, rows)]
+        copies.append(pltpu.make_async_copy(source, goal, sems.at[index]))
+        copies[-1].start()
+    for copy in copies:
+        copy.wait()
+
+
+def place(pieces, shape, target=None):
+    operands = [*pieces.values(), *([] if target is None else [target])]
+    return pl.pallas_call(
+        functools.partial(place_kernel, spots=tuple(pieces), count=len(operands)),
+        out_shape=pltpu.HBM(shape, F32),
+        in_specs=[ANY_SPEC] * len(operands),
+        out_specs=ANY_SPEC,
+        scratch_shapes=[pltpu.SemaphoreType.DMA((len(pieces),))],
+        input_output_aliases={} if target is None else {len(pieces): 0},
+        compiler_params=PARAMS,
+    )(*operands)
 
 
 def flip_move(array, bits):
@@ -372,7 +398,7 @@
                 base=max(level - 1, 0) * place_size, panel=forward[level], level=level, inverse=shared["inverse"],
                 coupling=shared["coupling"][level - 1] if level else None, sums=[kept, given, *addends], left=True,
             )
-        columns[chunk] = jnp.stack(solved)
+        columns[chunk] = solved
         yield
 
     def prepare_couplings(level):
@@ -391,7 +417,11 @@
                 prepare_couplings(level)
         for steps in chains:
             next(steps, None)
-    return jnp.concatenate(columns, axis=2)
+    pieces = {(level, chunk): columns[chunk][level] for chunk in range(CHUNKS) for level in range(LEVELS)}
+    output = place({spot: array for spot, array in pieces.items() if spot[0]}, probes.shape)
+    for chunk in range(CHUNKS):
+        output = place({(0, chunk): pieces[0, chunk]}, probes.shape, output)
+    return output
 
 
 def solution(mesh):

time: 181 us -> 179 us (0.989)
  waiting for transfers between devices: 78.9 us -> 75.4 us
  Pallas kernels: 47 us -> 49.3 us
    ppermute x56, waiting for transfers between devices: 78.9 us -> 75.4 us  [flip_move(): lax.ppermute(array, 'blk', [(source, source ^ bits) for source in range(m...]
    pallas_call x0 -> x3, Pallas kernels: none -> 2.29 us  [place(): pl.pallas_call(functools.partial(place_kernel, spots=tuple(pieces), count...]
  transfers between devices with their start and end apart: 56 -> 56, of which waited for: 32 -> 31; matrix products, arithmetic and copies ran while one was open for 2% -> 2% of each run, Pallas kernels for 24% -> 26%
where the time goes in v5:
time: 179 us
  waiting for transfers between devices  75.4 us (42%)
  starting transfers between devices  49.8 us (28%)
  Pallas kernels  49.3 us (28%)
  local copies, waits for them, and re-layouts  2.55 us (1%)
    ppermute x56, waiting for transfers between devices, flip_move(): lax.ppermute(array, 'blk', [(source, source ^ bits) for source in range(m...  75.4 us
    ppermute x56, starting transfers between devices, flip_move(): lax.ppermute(array, 'blk', [(source, source ^ bits) for source in range(m...  49.8 us
    pallas_call x25, Pallas kernels, run(): pl.pallas_call(kernel, out_shape=out_shape, grid_spec=pltpu.PrefetchScala...  47 us
  transfers between devices with their start and end apart: 56, of which 31 were waited for; matrix products, arithmetic and copies ran while one was open for 2% of the time, Pallas kernels for 26%

profile of v5, /device:TPU:0, one launch (start us, length us, event | category | flops | bytes accessed | tf_op | source)
XLA Modules:
  0.0 179.2 jit_solution(13259604730940409492)
XLA Ops:
  1.9 4.1 %collective-permute-start.5 = (f32[6,32,256]{2,1,0:T(8,128)S(1)}, f32[6,32,256]{2,1,0:T(8,128)S(1)}, u32[]{:S(2)}, u32[]{:S(2)}) collective-permute-start(f32[6,32,256]{2,1,0:T(8,128)S(1)} %shard_map.103.refs_0_.refs_4_.panel_ref), channel_id=1, source_target_pairs={{0,8},{1,9},{2,10},{3,11},{4,12},{5,13},{6,14},{7,15},{8,0},{9,1},... | collective-permute-start | bytes 589832 | tf_op jit(solution)/shard_map/ppermute | solution.py:336
  13.5 3.4 %collective-permute-done.5.refs_4_.refs_8_ = f32[6,32,256]{2,1,0:T(8,128)S(1)} collective-permute-done((f32[6,32,256]{2,1,0:T(8,128)S(1)}, f32[6,32,256]{2,1,0:T(8,128)S(1)}, u32[]{:S(2)}, u32[]{:S(2)}) %collective-permute-start.5) | collective-permute-done | bytes 196640 | tf_op jit(solution)/shard_map/ppermute | solution.py:336
  19.2 4.5 %collective-permute-done.8.refs_4_.refs_8_ = f32[6,32,256]{2,1,0:T(8,128)S(1)} collective-permute-done((f32[6,32,256]{2,1,0:T(8,128)S(1)}, f32[6,32,256]{2,1,0:T(8,128)S(1)}, u32[]{:S(2)}, u32[]{:S(2)}) %collective-permute-start.8) | collective-permute-done | bytes 196640 | tf_op jit(solution)/shard_map/ppermute | solution.py:336
  34.2 2.7 %shard_map.101 = (bf16[18,256,256]{2,1,0:T(8,128)(2,1)S(1)}, bf16[18,256,256]{2,1,0:T(8,128)(2,1)S(1)}) custom-call(f32[1,18,256,256]{3,2,1,0:T(8,128)} %bitcast.46, f32[1,18,256,256]{3,2,1,0:T(8,128)} %bitcast.47, f32[1,18,256,256]{3,2,1,0:T(8,128)} %bitcast.48), custom_call_target="tpu_custom_call" | custom-call | flops 600000000 | bytes 3000000 | tf_op jit(solution)/shard_map/pallas_call | solution.py:110
  37.0 4.0 %shard_map.102 = (bf16[24,256,256]{2,1,0:T(8,128)(2,1)S(1)}, bf16[24,256,256]{2,1,0:T(8,128)(2,1)S(1)}) custom-call(f32[2,24,256,256]{3,2,1,0:T(8,128)} %bitcast.38, f32[2,24,256,256]{3,2,1,0:T(8,128)} %bitcast.39, f32[2,24,256,256]{3,2,1,0:T(8,128)} %bitcast.40, f32[2,24,256,256]{3,2,1,0:T(8,128)} %bitcast.41), custom_call_target="tpu_custom_call" | custom-call | flops 600000000 | bytes 3000000 | tf_op jit(solution)/shard_map/pallas_call | solution.py:110
  42.4 3.5 %shard_map.116.refs_0_.refs_4_.panel_ref = f32[6,32,256]{2,1,0:T(8,128)S(1)} custom-call(s32[48]{0:T(128)S(1)} %fusion.6.place_ref, f32[3,6,64,256]{3,2,1,0:T(8,128)S(1)} %copy-done, bf16[18,256,256]{2,1,0:T(8,128)(2,1)S(1)} %get-tuple-element.62.refs_0_, bf16[18,256,256]{2,1,0:T(8,128)(2,1)S(1)} %get-tuple-element.63.refs_1_, ...), custom_call_target="tpu_custom_call" | custom-call | flops 600000000 | bytes 3000000 | tf_op jit(solution)/shard_map/pallas_call | solution.py:110
  47.4 2.4 %collective-permute-start.37 = (f32[6,32,256]{2,1,0:T(8,128)S(1)}, f32[6,32,256]{2,1,0:T(8,128)S(1)}, u32[]{:S(2)}, u32[]{:S(2)}) collective-permute-start(f32[6,32,256]{2,1,0:T(8,128)S(1)} %shard_map.116.refs_0_.refs_4_.panel_ref), channel_id=1, source_target_pairs={{0,4},{1,5},{2,6},{3,7},{4,0},{5,1},{6,2},{7,3},{8,12},{9,13},{10,... | collective-permute-start | bytes 589832 | tf_op jit(solution)/shard_map/ppermute | solution.py:336
  49.9 3.5 %shard_map.106.refs_0_.refs_4_.panel_ref = f32[6,32,256]{2,1,0:T(8,128)S(1)} custom-call(s32[48]{0:T(128)S(1)} %fusion.6.place_ref, f32[3,6,64,256]{3,2,1,0:T(8,128)S(1)} %copy-done, bf16[18,256,256]{2,1,0:T(8,128)(2,1)S(1)} %get-tuple-element.62.refs_0_, bf16[18,256,256]{2,1,0:T(8,128)(2,1)S(1)} %get-tuple-element.63.refs_1_, ...), custom_call_target="tpu_custom_call" | custom-call | flops 600000000 | bytes 3000000 | tf_op jit(solution)/shard_map/pallas_call | solution.py:110
  54.9 2.5 %collective-permute-start.14 = (f32[6,32,256]{2,1,0:T(8,128)S(1)}, f32[6,32,256]{2,1,0:T(8,128)S(1)}, u32[]{:S(2)}, u32[]{:S(2)}) collective-permute-start(f32[6,32,256]{2,1,0:T(8,128)S(1)} %shard_map.106.refs_0_.refs_4_.panel_ref), channel_id=1, source_target_pairs={{0,4},{1,5},{2,6},{3,7},{4,0},{5,1},{6,2},{7,3},{8,12},{9,13},{10,... | collective-permute-start | bytes 589832 | tf_op jit(solution)/shard_map/ppermute | solution.py:336
  57.9 7.6 %collective-permute-done.16.refs_4_.refs_8_ = f32[6,32,256]{2,1,0:T(8,128)S(1)} collective-permute-done((f32[6,32,256]{2,1,0:T(8,128)S(1)}, f32[6,32,256]{2,1,0:T(8,128)S(1)}, u32[]{:S(2)}, u32[]{:S(2)}) %collective-permute-start.16) | collective-permute-done | bytes 196640 | tf_op jit(solution)/shard_map/ppermute | solution.py:336
  69.4 3.0 %collective-permute-start.43 = (f32[4,32,256]{2,1,0:T(8,128)S(1)}, f32[4,32,256]{2,1,0:T(8,128)S(1)}, u32[]{:S(2)}, u32[]{:S(2)}) collective-permute-start(f32[4,32,256]{2,1,0:T(8,128)S(1)} %get-tuple-element.97), channel_id=1, source_target_pairs={{0,6},{1,7},{2,4},{3,5},{4,2},{5,3},{6,0},{7,1},{8,14},{9,15},{10,... | collective-permute-start | bytes 393224 | tf_op jit(solution)/shard_map/ppermute | solution.py:336
  72.4 3.4 %collective-permute-done.42.refs_11_ = f32[4,32,256]{2,1,0:T(8,128)S(1)} collective-permute-done((f32[4,32,256]{2,1,0:T(8,128)S(1)}, f32[4,32,256]{2,1,0:T(8,128)S(1)}, u32[]{:S(2)}, u32[]{:S(2)}) %collective-permute-start.42) | collective-permute-done | bytes 131104 | tf_op jit(solution)/shard_map/ppermute | solution.py:336
  76.5 4.1 %shard_map.107 = (bf16[24,256,256]{2,1,0:T(8,128)(2,1)S(1)}, bf16[24,256,256]{2,1,0:T(8,128)(2,1)S(1)}) custom-call(f32[2,24,256,256]{3,2,1,0:T(8,128)} %bitcast.42, f32[2,24,256,256]{3,2,1,0:T(8,128)} %bitcast.43, f32[2,24,256,256]{3,2,1,0:T(8,128)} %bitcast.44, f32[2,24,256,256]{3,2,1,0:T(8,128)} %bitcast.45), custom_call_target="tpu_custom_call" | custom-call | flops 600000000 | bytes 3000000 | tf_op jit(solution)/shard_map/pallas_call | solution.py:110
  80.6 3.7 %collective-permute-done.41.refs_10_ = f32[12,32,256]{2,1,0:T(8,128)S(1)} collective-permute-done((f32[12,32,256]{2,1,0:T(8,128)S(1)}, f32[12,32,256]{2,1,0:T(8,128)S(1)}, u32[]{:S(2)}, u32[]{:S(2)}) %collective-permute-start.41) | collective-permute-done | bytes 393248 | tf_op jit(solution)/shard_map/ppermute | solution.py:336
  84.3 6.3 %shard_map.118 = (f32[6,32,256]{2,1,0:T(8,128)S(1)}, f32[36,32,256]{2,1,0:T(8,128)S(1)}, f32[12,32,256]{2,1,0:T(8,128)S(1)}, f32[4,32,256]{2,1,0:T(8,128)S(1)}, f32[4,32,256]{2,1,0:T(8,128)S(1)}) custom-call(s32[48]{0:T(128)S(1)} %fusion.6.place_ref, f32[3,6,64,256]{3,2,1,0:T(8,128)S(1)} %copy-done, bf16[18,256,256]{2,1,0:T(8,128)(2,1)S(1)} %get-tuple-element.62.refs_0_, ...), custom_call_target="tpu_custom_call" | custom-call | flops 600000000 | bytes 3000000 | tf_op jit(solution)/shard_map/pallas_call | solution.py:110
  92.7 6.3 %shard_map.109 = (f32[6,32,256]{2,1,0:T(8,128)S(1)}, f32[36,32,256]{2,1,0:T(8,128)S(1)}, f32[12,32,256]{2,1,0:T(8,128)S(1)}, f32[4,32,256]{2,1,0:T(8,128)S(1)}, f32[4,32,256]{2,1,0:T(8,128)S(1)}) custom-call(s32[48]{0:T(128)S(1)} %fusion.6.place_ref, f32[3,6,64,256]{3,2,1,0:T(8,128)S(1)} %copy-done, bf16[18,256,256]{2,1,0:T(8,128)(2,1)S(1)} %get-tuple-element.62.refs_0_, ...), custom_call_target="tpu_custom_call" | custom-call | flops 600000000 | bytes 3000000 | tf_op jit(solution)/shard_map/pallas_call | solution.py:110
  102.6 4.4 %collective-permute-done.45.refs_1_ = f32[4,32,256]{2,1,0:T(8,128)S(1)} collective-permute-done((f32[4,32,256]{2,1,0:T(8,128)S(1)}, f32[4,32,256]{2,1,0:T(8,128)S(1)}, u32[]{:S(2)}, u32[]{:S(2)}) %collective-permute-start.45) | collective-permute-done | bytes 131104 | tf_op jit(solution)/shard_map/ppermute | solution.py:336
  107.0 2.7 %collective-permute-done.46.refs_2_ = f32[4,32,256]{2,1,0:T(8,128)S(1)} collective-permute-done((f32[4,32,256]{2,1,0:T(8,128)S(1)}, f32[4,32,256]{2,1,0:T(8,128)S(1)}, u32[]{:S(2)}, u32[]{:S(2)}) %collective-permute-start.46) | collective-permute-done | bytes 131104 | tf_op jit(solution)/shard_map/ppermute | solution.py:336
  115.5 2.1 %collective-permute-start.49 = (f32[6,32,256]{2,1,0:T(8,128)S(1)}, f32[6,32,256]{2,1,0:T(8,128)S(1)}, u32[]{:S(2)}, u32[]{:S(2)}) collective-permute-start(f32[6,32,256]{2,1,0:T(8,128)S(1)} %get-tuple-element.105), channel_id=1, source_target_pairs={{0,8},{1,9},{2,10},{3,11},{4,12},{5,13},{6,14},{7,15},{8,0},{9,1},... | collective-permute-start | bytes 589832 | tf_op jit(solution)/shard_map/ppermute | solution.py:336
  118.2 2.2 %collective-permute-start.26 = (f32[6,32,256]{2,1,0:T(8,128)S(1)}, f32[6,32,256]{2,1,0:T(8,128)S(1)}, u32[]{:S(2)}, u32[]{:S(2)}) collective-permute-start(f32[6,32,256]{2,1,0:T(8,128)S(1)} %get-tuple-element.84), channel_id=1, source_target_pairs={{0,8},{1,9},{2,10},{3,11},{4,12},{5,13},{6,14},{7,15},{8,0},{9,1},... | collective-permute-start | bytes 589832 | tf_op jit(solution)/shard_map/ppermute | solution.py:336
  120.4 6.1 %collective-permute-done.48.refs_6_ = f32[6,32,256]{2,1,0:T(8,128)S(1)} collective-permute-done((f32[6,32,256]{2,1,0:T(8,128)S(1)}, f32[6,32,256]{2,1,0:T(8,128)S(1)}, u32[]{:S(2)}, u32[]{:S(2)}) %collective-permute-start.48) | collective-permute-done | bytes 196640 | tf_op jit(solution)/shard_map/ppermute | solution.py:336
  126.5 2.0 %collective-permute-done.49.refs_7_ = f32[6,32,256]{2,1,0:T(8,128)S(1)} collective-permute-done((f32[6,32,256]{2,1,0:T(8,128)S(1)}, f32[6,32,256]{2,1,0:T(8,128)S(1)}, u32[]{:S(2)}, u32[]{:S(2)}) %collective-permute-start.49) | collective-permute-done | bytes 196640 | tf_op jit(solution)/shard_map/ppermute | solution.py:336
  128.4 2.8 %shard_map.121 = (f32[6,32,256]{2,1,0:T(8,128)S(1)}, f32[36,32,256]{2,1,0:T(8,128)S(1)}, f32[12,32,256]{2,1,0:T(8,128)S(1)}, f32[4,32,256]{2,1,0:T(8,128)S(1)}, f32[4,32,256]{2,1,0:T(8,128)S(1)}) custom-call(s32[48]{0:T(128)S(1)} %fusion.6.place_ref, f32[6,32,256]{2,1,0:T(8,128)S(1)} %shard_map.116.refs_0_.refs_4_.panel_ref, ...), custom_call_target="tpu_custom_call" | custom-call | flops 600000000 | bytes 3000000 | tf_op jit(solution)/shard_map/pallas_call | solution.py:110
  136.3 2.8 %shard_map.112 = (f32[6,32,256]{2,1,0:T(8,128)S(1)}, f32[36,32,256]{2,1,0:T(8,128)S(1)}, f32[12,32,256]{2,1,0:T(8,128)S(1)}, f32[4,32,256]{2,1,0:T(8,128)S(1)}, f32[4,32,256]{2,1,0:T(8,128)S(1)}) custom-call(s32[48]{0:T(128)S(1)} %fusion.6.place_ref, f32[6,32,256]{2,1,0:T(8,128)S(1)} %shard_map.106.refs_0_.refs_4_.panel_ref, ...), custom_call_target="tpu_custom_call" | custom-call | flops 600000000 | bytes 3000000 | tf_op jit(solution)/shard_map/pallas_call | solution.py:110
  140.7 2.0 %collective-permute-start.52 = (f32[4,32,256]{2,1,0:T(8,128)S(1)}, f32[4,32,256]{2,1,0:T(8,128)S(1)}, u32[]{:S(2)}, u32[]{:S(2)}) collective-permute-start(f32[4,32,256]{2,1,0:T(8,128)S(1)} %get-tuple-element.109), channel_id=1, source_target_pairs={{0,6},{1,7},{2,4},{3,5},{4,2},{5,3},{6,0},{7,1},{8,14},{9,15},{10,... | collective-permute-start | bytes 393224 | tf_op jit(solution)/shard_map/ppermute | solution.py:336
  142.7 4.4 %collective-permute-done.51.refs_1_ = f32[4,32,256]{2,1,0:T(8,128)S(1)} collective-permute-done((f32[4,32,256]{2,1,0:T(8,128)S(1)}, f32[4,32,256]{2,1,0:T(8,128)S(1)}, u32[]{:S(2)}, u32[]{:S(2)}) %collective-permute-start.51) | collective-permute-done | bytes 131104 | tf_op jit(solution)/shard_map/ppermute | solution.py:336
  147.1 2.9 %collective-permute-done.52.refs_2_ = f32[4,32,256]{2,1,0:T(8,128)S(1)} collective-permute-done((f32[4,32,256]{2,1,0:T(8,128)S(1)}, f32[4,32,256]{2,1,0:T(8,128)S(1)}, u32[]{:S(2)}, u32[]{:S(2)}) %collective-permute-start.52) | collective-permute-done | bytes 131104 | tf_op jit(solution)/shard_map/ppermute | solution.py:336
  159.0 2.5 %collective-permute-start.32 = (f32[6,32,256]{2,1,0:T(8,128)S(1)}, f32[6,32,256]{2,1,0:T(8,128)S(1)}, u32[]{:S(2)}, u32[]{:S(2)}) collective-permute-start(f32[6,32,256]{2,1,0:T(8,128)S(1)} %get-tuple-element.92), channel_id=1, source_target_pairs={{0,8},{1,9},{2,10},{3,11},{4,12},{5,13},{6,14},{7,15},{8,0},{9,1},... | collective-permute-start | bytes 589832 | tf_op jit(solution)/shard_map/ppermute | solution.py:336
  162.4 4.8 %collective-permute-done.54.refs_4_ = f32[6,32,256]{2,1,0:T(8,128)S(1)} collective-permute-done((f32[6,32,256]{2,1,0:T(8,128)S(1)}, f32[6,32,256]{2,1,0:T(8,128)S(1)}, u32[]{:S(2)}, u32[]{:S(2)}) %collective-permute-start.54) | collective-permute-done | bytes 196640 | tf_op jit(solution)/shard_map/ppermute | solution.py:336
  167.3 2.2 %collective-permute-done.55.refs_5_ = f32[6,32,256]{2,1,0:T(8,128)S(1)} collective-permute-done((f32[6,32,256]{2,1,0:T(8,128)S(1)}, f32[6,32,256]{2,1,0:T(8,128)S(1)}, u32[]{:S(2)}, u32[]{:S(2)}) %collective-permute-start.55) | collective-permute-done | bytes 196640 | tf_op jit(solution)/shard_map/ppermute | solution.py:336
  171.1 4.2 %collective-permute-done.31.refs_4_ = f32[6,32,256]{2,1,0:T(8,128)S(1)} collective-permute-done((f32[6,32,256]{2,1,0:T(8,128)S(1)}, f32[6,32,256]{2,1,0:T(8,128)S(1)}, u32[]{:S(2)}, u32[]{:S(2)}) %collective-permute-start.31) | collective-permute-done | bytes 196640 | tf_op jit(solution)/shard_map/ppermute | solution.py:336
  175.3 2.2 %collective-permute-done.32.refs_5_ = f32[6,32,256]{2,1,0:T(8,128)S(1)} collective-permute-done((f32[6,32,256]{2,1,0:T(8,128)S(1)}, f32[6,32,256]{2,1,0:T(8,128)S(1)}, u32[]{:S(2)}, u32[]{:S(2)}) %collective-permute-start.32) | collective-permute-done | bytes 196640 | tf_op jit(solution)/shard_map/ppermute | solution.py:336
  (164 shorter events, 63.4 us)
Async XLA Ops:
  1.9 15.0 %collective-permute-start.5 = (f32[6,32,256]{2,1,0:T(8,128)S(1)}, f32[6,32,256]{2,1,0:T(8,128)S(1)}, u32[]{:S(2)}, u32[]{:S(2)}) collective-permute-start(f32[6,32,256]{2,1,0:T(8,128)S(1)} %shard_map.103.refs_0_.refs_4_.panel_ref), channel_id=1, source_target_pairs={{0,8},{1,9},{2,10},{3,11},{4,12},{5,13},{6,14},{7,15},{8,0},{9,1},... | collective-permute-start | bytes 589832 | tf_op jit(solution)/shard_map/ppermute | solution.py:336
  6.0 10.9 %collective-permute-start.3 = (f32[6,32,256]{2,1,0:T(8,128)S(1)}, f32[6,32,256]{2,1,0:T(8,128)S(1)}, u32[]{:S(2)}, u32[]{:S(2)}) collective-permute-start(f32[6,32,256]{2,1,0:T(8,128)S(1)} %shard_map.103.refs_0_.refs_4_.panel_ref), channel_id=1, source_target_pairs={{0,4},{1,5},{2,6},{3,7},{4,0},{5,1},{6,2},{7,3},{8,12},{9,13},{10,... | collective-permute-start | bytes 589832 | tf_op jit(solution)/shard_map/ppermute | solution.py:336
  7.6 10.1 %collective-permute-start.2 = (f32[6,32,256]{2,1,0:T(8,128)S(1)}, f32[6,32,256]{2,1,0:T(8,128)S(1)}, u32[]{:S(2)}, u32[]{:S(2)}) collective-permute-start(f32[6,32,256]{2,1,0:T(8,128)S(1)} %shard_map.103.refs_0_.refs_4_.panel_ref), channel_id=1, source_target_pairs={{0,1},{1,0},{2,3},{3,2},{4,5},{5,4},{6,7},{7,6},{8,9},{9,8},{10,11... | collective-permute-start | bytes 589832 | tf_op jit(solution)/shard_map/ppermute | solution.py:336
  9.5 14.2 %collective-permute-start.8 = (f32[6,32,256]{2,1,0:T(8,128)S(1)}, f32[6,32,256]{2,1,0:T(8,128)S(1)}, u32[]{:S(2)}, u32[]{:S(2)}) collective-permute-start(f32[6,32,256]{2,1,0:T(8,128)S(1)} %shard_map.100.refs_0_.refs_4_.panel_ref), channel_id=1, source_target_pairs={{0,8},{1,9},{2,10},{3,11},{4,12},{5,13},{6,14},{7,15},{8,0},{9,1},... | collective-permute-start | bytes 589832 | tf_op jit(solution)/shard_map/ppermute | solution.py:336
  9.9 14.0 %collective-permute-start.1 = (f32[6,32,256]{2,1,0:T(8,128)S(1)}, f32[6,32,256]{2,1,0:T(8,128)S(1)}, u32[]{:S(2)}, u32[]{:S(2)}) collective-permute-start(f32[6,32,256]{2,1,0:T(8,128)S(1)} %shard_map.100.refs_0_.refs_4_.panel_ref), channel_id=1, source_target_pairs={{0,4},{1,5},{2,6},{3,7},{4,0},{5,1},{6,2},{7,3},{8,12},{9,13},{10,... | collective-permute-start | bytes 589832 | tf_op jit(solution)/shard_map/ppermute | solution.py:336
  17.7 10.2 %collective-permute-start = (f32[6,32,256]{2,1,0:T(8,128)S(1)}, f32[6,32,256]{2,1,0:T(8,128)S(1)}, u32[]{:S(2)}, u32[]{:S(2)}) collective-permute-start(f32[6,32,256]{2,1,0:T(8,128)S(1)} %shard_map.100.refs_0_.refs_4_.panel_ref), channel_id=1, source_target_pairs={{0,1},{1,0},{2,3},{3,2},{4,5},{5,4},{6,7},{7,6},{8,9},{9,8},{10,11... | collective-permute-start | bytes 589832 | tf_op jit(solution)/shard_map/ppermute | solution.py:336
  24.8 17.6 %collective-permute-start.33 = (f32[12,32,256]{2,1,0:T(8,128)S(1)}, f32[12,32,256]{2,1,0:T(8,128)S(1)}, u32[]{:S(2)}, u32[]{:S(2)}) collective-permute-start(f32[12,32,256]{2,1,0:T(8,128)S(1)} %get-tuple-element.66), channel_id=1, source_target_pairs={{0,2},{1,3},{2,0},{3,1},{4,6},{5,7},{6,4},{7,5},{8,10},{9,11},{10,... | collective-permute-start | bytes 1179656 | tf_op jit(solution)/shard_map/ppermute | solution.py:336
  27.9 13.1 %collective-permute-start.35 = (f32[4,32,256]{2,1,0:T(8,128)S(1)}, f32[4,32,256]{2,1,0:T(8,128)S(1)}, u32[]{:S(2)}, u32[]{:S(2)}) collective-permute-start(f32[4,32,256]{2,1,0:T(8,128)S(1)} %get-tuple-element.94), channel_id=1, source_target_pairs={{0,6},{1,7},{2,4},{3,5},{4,2},{5,3},{6,0},{7,1},{8,14},{9,15},{10,... | collective-permute-start | bytes 393224 | tf_op jit(solution)/shard_map/ppermute | solution.py:336
  28.9 21.0 %collective-permute-start.10 = (f32[12,32,256]{2,1,0:T(8,128)S(1)}, f32[12,32,256]{2,1,0:T(8,128)S(1)}, u32[]{:S(2)}, u32[]{:S(2)}) collective-permute-start(f32[12,32,256]{2,1,0:T(8,128)S(1)} %get-tuple-element.69), channel_id=1, source_target_pairs={{0,2},{1,3},{2,0},{3,1},{4,6},{5,7},{6,4},{7,5},{8,10},{9,11},{10,... | collective-permute-start | bytes 1179656 | tf_op jit(solution)/shard_map/ppermute | solution.py:336
  30.6 19.2 %collective-permute-start.11 = (f32[4,32,256]{2,1,0:T(8,128)S(1)}, f32[4,32,256]{2,1,0:T(8,128)S(1)}, u32[]{:S(2)}, u32[]{:S(2)}) collective-permute-start(f32[4,32,256]{2,1,0:T(8,128)S(1)} %get-tuple-element.70), channel_id=1, source_target_pairs={{0,4},{1,5},{2,6},{3,7},{4,0},{5,1},{6,2},{7,3},{8,12},{9,13},{10,... | collective-permute-start | bytes 393224 | tf_op jit(solution)/shard_map/ppermute | solution.py:336
  32.8 17.0 %collective-permute-start.12 = (f32[4,32,256]{2,1,0:T(8,128)S(1)}, f32[4,32,256]{2,1,0:T(8,128)S(1)}, u32[]{:S(2)}, u32[]{:S(2)}) collective-permute-start(f32[4,32,256]{2,1,0:T(8,128)S(1)} %get-tuple-element.71), channel_id=1, source_target_pairs={{0,6},{1,7},{2,4},{3,5},{4,2},{5,3},{6,0},{7,1},{8,14},{9,15},{10,... | collective-permute-start | bytes 393224 | tf_op jit(solution)/shard_map/ppermute | solution.py:336
  45.9 11.4 %collective-permute-start.39 = (f32[6,32,256]{2,1,0:T(8,128)S(1)}, f32[6,32,256]{2,1,0:T(8,128)S(1)}, u32[]{:S(2)}, u32[]{:S(2)}) collective-permute-start(f32[6,32,256]{2,1,0:T(8,128)S(1)} %shard_map.116.refs_0_.refs_4_.panel_ref), channel_id=1, source_target_pairs={{0,8},{1,9},{2,10},{3,11},{4,12},{5,13},{6,14},{7,15},{8,0},{9,1},... | collective-permute-start | bytes 589832 | tf_op jit(solution)/shard_map/ppermute | solution.py:336
  53.4 12.1 %collective-permute-start.16 = (f32[6,32,256]{2,1,0:T(8,128)S(1)}, f32[6,32,256]{2,1,0:T(8,128)S(1)}, u32[]{:S(2)}, u32[]{:S(2)}) collective-permute-start(f32[6,32,256]{2,1,0:T(8,128)S(1)} %shard_map.106.refs_0_.refs_4_.panel_ref), channel_id=1, source_target_pairs={{0,8},{1,9},{2,10},{3,11},{4,12},{5,13},{6,14},{7,15},{8,0},{9,1},... | collective-permute-start | bytes 589832 | tf_op jit(solution)/shard_map/ppermute | solution.py:336
  54.9 10.7 %collective-permute-start.14 = (f32[6,32,256]{2,1,0:T(8,128)S(1)}, f32[6,32,256]{2,1,0:T(8,128)S(1)}, u32[]{:S(2)}, u32[]{:S(2)}) collective-permute-start(f32[6,32,256]{2,1,0:T(8,128)S(1)} %shard_map.106.refs_0_.refs_4_.panel_ref), channel_id=1, source_target_pairs={{0,4},{1,5},{2,6},{3,7},{4,0},{5,1},{6,2},{7,3},{8,12},{9,13},{10,... | collective-permute-start | bytes 589832 | tf_op jit(solution)/shard_map/ppermute | solution.py:336
  57.8 10.4 %collective-permute-start.13 = (f32[6,32,256]{2,1,0:T(8,128)S(1)}, f32[6,32,256]{2,1,0:T(8,128)S(1)}, u32[]{:S(2)}, u32[]{:S(2)}) collective-permute-start(f32[6,32,256]{2,1,0:T(8,128)S(1)} %shard_map.106.refs_0_.refs_4_.panel_ref), channel_id=1, source_target_pairs={{0,1},{1,0},{2,3},{3,2},{4,5},{5,4},{6,7},{7,6},{8,9},{9,8},{10,11... | collective-permute-start | bytes 589832 | tf_op jit(solution)/shard_map/ppermute | solution.py:336
  66.7 17.7 %collective-permute-start.41 = (f32[12,32,256]{2,1,0:T(8,128)S(1)}, f32[12,32,256]{2,1,0:T(8,128)S(1)}, u32[]{:S(2)}, u32[]{:S(2)}) collective-permute-start(f32[12,32,256]{2,1,0:T(8,128)S(1)} %get-tuple-element.95), channel_id=1, source_target_pairs={{0,2},{1,3},{2,0},{3,1},{4,6},{5,7},{6,4},{7,5},{8,10},{9,11},{10,... | collective-permute-start | bytes 1179656 | tf_op jit(solution)/shard_map/ppermute | solution.py:336
  68.8 23.9 %collective-permute-start.18 = (f32[12,32,256]{2,1,0:T(8,128)S(1)}, f32[12,32,256]{2,1,0:T(8,128)S(1)}, u32[]{:S(2)}, u32[]{:S(2)}) collective-permute-start(f32[12,32,256]{2,1,0:T(8,128)S(1)} %get-tuple-element.74), channel_id=1, source_target_pairs={{0,2},{1,3},{2,0},{3,1},{4,6},{5,7},{6,4},{7,5},{8,10},{9,11},{10,... | collective-permute-start | bytes 1179656 | tf_op jit(solution)/shard_map/ppermute | solution.py:336
  69.4 11.2 %collective-permute-start.43 = (f32[4,32,256]{2,1,0:T(8,128)S(1)}, f32[4,32,256]{2,1,0:T(8,128)S(1)}, u32[]{:S(2)}, u32[]{:S(2)}) collective-permute-start(f32[4,32,256]{2,1,0:T(8,128)S(1)} %get-tuple-element.97), channel_id=1, source_target_pairs={{0,6},{1,7},{2,4},{3,5},{4,2},{5,3},{6,0},{7,1},{8,14},{9,15},{10,... | collective-permute-start | bytes 393224 | tf_op jit(solution)/shard_map/ppermute | solution.py:336
  72.4 19.8 %collective-permute-start.19 = (f32[4,32,256]{2,1,0:T(8,128)S(1)}, f32[4,32,256]{2,1,0:T(8,128)S(1)}, u32[]{:S(2)}, u32[]{:S(2)}) collective-permute-start(f32[4,32,256]{2,1,0:T(8,128)S(1)} %get-tuple-element.75), channel_id=1, source_target_pairs={{0,4},{1,5},{2,6},{3,7},{4,0},{5,1},{6,2},{7,3},{8,12},{9,13},{10,... | collective-permute-start | bytes 393224 | tf_op jit(solution)/shard_map/ppermute | solution.py:336
  75.8 16.3 %collective-permute-start.20 = (f32[4,32,256]{2,1,0:T(8,128)S(1)}, f32[4,32,256]{2,1,0:T(8,128)S(1)}, u32[]{:S(2)}, u32[]{:S(2)}) collective-permute-start(f32[4,32,256]{2,1,0:T(8,128)S(1)} %get-tuple-element.76), channel_id=1, source_target_pairs={{0,6},{1,7},{2,4},{3,5},{4,2},{5,3},{6,0},{7,1},{8,14},{9,15},{10,... | collective-permute-start | bytes 393224 | tf_op jit(solution)/shard_map/ppermute | solution.py:336
  90.6 19.2 %collective-permute-start.44 = (f32[12,32,256]{2,1,0:T(8,128)S(1)}, f32[12,32,256]{2,1,0:T(8,128)S(1)}, u32[]{:S(2)}, u32[]{:S(2)}) collective-permute-start(f32[12,32,256]{2,1,0:T(8,128)S(1)} %get-tuple-element.99), channel_id=1, source_target_pairs={{0,2},{1,3},{2,0},{3,1},{4,6},{5,7},{6,4},{7,5},{8,10},{9,11},{10,... | collective-permute-start | bytes 1179656 | tf_op jit(solution)/shard_map/ppermute | solution.py:336
  99.0 15.3 %collective-permute-start.21 = (f32[12,32,256]{2,1,0:T(8,128)S(1)}, f32[12,32,256]{2,1,0:T(8,128)S(1)}, u32[]{:S(2)}, u32[]{:S(2)}) collective-permute-start(f32[12,32,256]{2,1,0:T(8,128)S(1)} %get-tuple-element.78), channel_id=1, source_target_pairs={{0,2},{1,3},{2,0},{3,1},{4,6},{5,7},{6,4},{7,5},{8,10},{9,11},{10,... | collective-permute-start | bytes 1179656 | tf_op jit(solution)/shard_map/ppermute | solution.py:336
  115.3 11.2 %collective-permute-start.48 = (f32[6,32,256]{2,1,0:T(8,128)S(1)}, f32[6,32,256]{2,1,0:T(8,128)S(1)}, u32[]{:S(2)}, u32[]{:S(2)}) collective-permute-start(f32[6,32,256]{2,1,0:T(8,128)S(1)} %get-tuple-element.104), channel_id=1, source_target_pairs={{0,4},{1,5},{2,6},{3,7},{4,0},{5,1},{6,2},{7,3},{8,12},{9,13},{10,... | collective-permute-start | bytes 589832 | tf_op jit(solution)/shard_map/ppermute | solution.py:336
  115.5 13.0 %collective-permute-start.49 = (f32[6,32,256]{2,1,0:T(8,128)S(1)}, f32[6,32,256]{2,1,0:T(8,128)S(1)}, u32[]{:S(2)}, u32[]{:S(2)}) collective-permute-start(f32[6,32,256]{2,1,0:T(8,128)S(1)} %get-tuple-element.105), channel_id=1, source_target_pairs={{0,8},{1,9},{2,10},{3,11},{4,12},{5,13},{6,14},{7,15},{8,0},{9,1},... | collective-permute-start | bytes 589832 | tf_op jit(solution)/shard_map/ppermute | solution.py:336
  117.7 16.8 %collective-permute-start.25 = (f32[6,32,256]{2,1,0:T(8,128)S(1)}, f32[6,32,256]{2,1,0:T(8,128)S(1)}, u32[]{:S(2)}, u32[]{:S(2)}) collective-permute-start(f32[6,32,256]{2,1,0:T(8,128)S(1)} %get-tuple-element.83), channel_id=1, source_target_pairs={{0,4},{1,5},{2,6},{3,7},{4,0},{5,1},{6,2},{7,3},{8,12},{9,13},{10,... | collective-permute-start | bytes 589832 | tf_op jit(solution)/shard_map/ppermute | solution.py:336
  118.2 18.1 %collective-permute-start.26 = (f32[6,32,256]{2,1,0:T(8,128)S(1)}, f32[6,32,256]{2,1,0:T(8,128)S(1)}, u32[]{:S(2)}, u32[]{:S(2)}) collective-permute-start(f32[6,32,256]{2,1,0:T(8,128)S(1)} %get-tuple-element.84), channel_id=1, source_target_pairs={{0,8},{1,9},{2,10},{3,11},{4,12},{5,13},{6,14},{7,15},{8,0},{9,1},... | collective-permute-start | bytes 589832 | tf_op jit(solution)/shard_map/ppermute | solution.py:336
  131.2 18.8 %collective-permute-start.50 = (f32[12,32,256]{2,1,0:T(8,128)S(1)}, f32[12,32,256]{2,1,0:T(8,128)S(1)}, u32[]{:S(2)}, u32[]{:S(2)}) collective-permute-start(f32[12,32,256]{2,1,0:T(8,128)S(1)} %get-tuple-element.107), channel_id=1, source_target_pairs={{0,2},{1,3},{2,0},{3,1},{4,6},{5,7},{6,4},{7,5},{8,10},{9,11},{10,... | collective-permute-start | bytes 1179656 | tf_op jit(solution)/shard_map/ppermute | solution.py:336
  139.1 16.3 %collective-permute-start.27 = (f32[12,32,256]{2,1,0:T(8,128)S(1)}, f32[12,32,256]{2,1,0:T(8,128)S(1)}, u32[]{:S(2)}, u32[]{:S(2)}) collective-permute-start(f32[12,32,256]{2,1,0:T(8,128)S(1)} %get-tuple-element.86), channel_id=1, source_target_pairs={{0,2},{1,3},{2,0},{3,1},{4,6},{5,7},{6,4},{7,5},{8,10},{9,11},{10,... | collective-permute-start | bytes 1179656 | tf_op jit(solution)/shard_map/ppermute | solution.py:336
  156.4 10.9 %collective-permute-start.54 = (f32[6,32,256]{2,1,0:T(8,128)S(1)}, f32[6,32,256]{2,1,0:T(8,128)S(1)}, u32[]{:S(2)}, u32[]{:S(2)}) collective-permute-start(f32[6,32,256]{2,1,0:T(8,128)S(1)} %get-tuple-element.112), channel_id=1, source_target_pairs={{0,4},{1,5},{2,6},{3,7},{4,0},{5,1},{6,2},{7,3},{8,12},{9,13},{10,... | collective-permute-start | bytes 589832 | tf_op jit(solution)/shard_map/ppermute | solution.py:336
  156.5 13.0 %collective-permute-start.55 = (f32[6,32,256]{2,1,0:T(8,128)S(1)}, f32[6,32,256]{2,1,0:T(8,128)S(1)}, u32[]{:S(2)}, u32[]{:S(2)}) collective-permute-start(f32[6,32,256]{2,1,0:T(8,128)S(1)} %get-tuple-element.113), channel_id=1, source_target_pairs={{0,8},{1,9},{2,10},{3,11},{4,12},{5,13},{6,14},{7,15},{8,0},{9,1},... | collective-permute-start | bytes 589832 | tf_op jit(solution)/shard_map/ppermute | solution.py:336
  158.4 16.9 %collective-permute-start.31 = (f32[6,32,256]{2,1,0:T(8,128)S(1)}, f32[6,32,256]{2,1,0:T(8,128)S(1)}, u32[]{:S(2)}, u32[]{:S(2)}) collective-permute-start(f32[6,32,256]{2,1,0:T(8,128)S(1)} %get-tuple-element.91), channel_id=1, source_target_pairs={{0,4},{1,5},{2,6},{3,7},{4,0},{5,1},{6,2},{7,3},{8,12},{9,13},{10,... | collective-permute-start | bytes 589832 | tf_op jit(solution)/shard_map/ppermute | solution.py:336
  159.0 18.5 %collective-permute-start.32 = (f32[6,32,256]{2,1,0:T(8,128)S(1)}, f32[6,32,256]{2,1,0:T(8,128)S(1)}, u32[]{:S(2)}, u32[]{:S(2)}) collective-permute-start(f32[6,32,256]{2,1,0:T(8,128)S(1)} %get-tuple-element.92), channel_id=1, source_target_pairs={{0,8},{1,9},{2,10},{3,11},{4,12},{5,13},{6,14},{7,15},{8,0},{9,1},... | collective-permute-start | bytes 589832 | tf_op jit(solution)/shard_map/ppermute | solution.py:336
  (29 other events, 196.5 us)

commit v6 on v5

--- a/solution.py
+++ b/solution.py
@@ -345,7 +345,7 @@
     whole, listed = line_offsets(depth)
     asked, places = tables(neighbour_devices, neighbour_slots, members, position)
     asked_size, place_size = asked.shape[0] // (LEVELS - 1), places.shape[0] // (LEVELS - 1)
-    travel = sorted(whole[1:], key=lambda offset: (offset.bit_count(), -offset))
+    travel = sorted(whole[1:], key=lambda offset: (offset.bit_count(), offset))
     shared, ahead = {}, {}
     columns = [None] * CHUNKS
 

time: 179 us -> 179 us (level)
  transfers between devices with their start and end apart: 56 -> 56, of which waited for: 31 -> 29; matrix products, arithmetic and copies ran while one was open for 2% -> 2% of each run, Pallas kernels for 26% -> 26%
where the time goes in v6:
time: 179 us
  waiting for transfers between devices  73.7 us (41%)
  starting transfers between devices  51.3 us (29%)
  Pallas kernels  49.3 us (28%)
  local copies, waits for them, and re-layouts  2.55 us (1%)
    ppermute x56, waiting for transfers between devices, flip_move(): lax.ppermute(array, 'blk', [(source, source ^ bits) for source in range(m...  73.7 us
    ppermute x56, starting transfers between devices, flip_move(): lax.ppermute(array, 'blk', [(source, source ^ bits) for source in range(m...  51.3 us
    pallas_call x25, Pallas kernels, run(): pl.pallas_call(kernel, out_shape=out_shape, grid_spec=pltpu.PrefetchScala...  47 us
  transfers between devices with their start and end apart: 56, of which 29 were waited for; matrix products, arithmetic and copies ran while one was open for 2% of the time, Pallas kernels for 26%

profile of v6, /device:TPU:0, one launch (start us, length us, event | category | flops | bytes accessed | tf_op | source)
XLA Modules:
  0.0 179.0 jit_solution(16912517626059394578)
XLA Ops:
  1.9 4.1 %collective-permute-start.5 = (f32[6,32,256]{2,1,0:T(8,128)S(1)}, f32[6,32,256]{2,1,0:T(8,128)S(1)}, u32[]{:S(2)}, u32[]{:S(2)}) collective-permute-start(f32[6,32,256]{2,1,0:T(8,128)S(1)} %shard_map.103.refs_0_.refs_4_.panel_ref), channel_id=1, source_target_pairs={{0,8},{1,9},{2,10},{3,11},{4,12},{5,13},{6,14},{7,15},{8,0},{9,1},... | collective-permute-start | bytes 589832 | tf_op jit(solution)/shard_map/ppermute | solution.py:336
  7.6 1.9 %shard_map.100.refs_0_.refs_4_.panel_ref = f32[6,32,256]{2,1,0:T(8,128)S(1)} custom-call(f32[3,6,64,256]{3,2,1,0:T(8,128)} %panel_ref.7, f32[3,6,256,256]{3,2,1,0:T(8,128)} %inverse_ref.3), custom_call_target="tpu_custom_call" | custom-call | flops 600000000 | bytes 3000000 | tf_op jit(solution)/shard_map/pallas_call | solution.py:110
  13.5 3.4 %collective-permute-done.5.refs_4_.refs_8_ = f32[6,32,256]{2,1,0:T(8,128)S(1)} collective-permute-done((f32[6,32,256]{2,1,0:T(8,128)S(1)}, f32[6,32,256]{2,1,0:T(8,128)S(1)}, u32[]{:S(2)}, u32[]{:S(2)}) %collective-permute-start.5) | collective-permute-done | bytes 196640 | tf_op jit(solution)/shard_map/ppermute | solution.py:336
  19.2 4.5 %collective-permute-done.8.refs_4_.refs_8_ = f32[6,32,256]{2,1,0:T(8,128)S(1)} collective-permute-done((f32[6,32,256]{2,1,0:T(8,128)S(1)}, f32[6,32,256]{2,1,0:T(8,128)S(1)}, u32[]{:S(2)}, u32[]{:S(2)}) %collective-permute-start.8) | collective-permute-done | bytes 196640 | tf_op jit(solution)/shard_map/ppermute | solution.py:336
  34.2 2.7 %shard_map.101 = (bf16[18,256,256]{2,1,0:T(8,128)(2,1)S(1)}, bf16[18,256,256]{2,1,0:T(8,128)(2,1)S(1)}) custom-call(f32[1,18,256,256]{3,2,1,0:T(8,128)} %bitcast.46, f32[1,18,256,256]{3,2,1,0:T(8,128)} %bitcast.47, f32[1,18,256,256]{3,2,1,0:T(8,128)} %bitcast.48), custom_call_target="tpu_custom_call" | custom-call | flops 600000000 | bytes 3000000 | tf_op jit(solution)/shard_map/pallas_call | solution.py:110
  37.0 4.0 %shard_map.102 = (bf16[24,256,256]{2,1,0:T(8,128)(2,1)S(1)}, bf16[24,256,256]{2,1,0:T(8,128)(2,1)S(1)}) custom-call(f32[2,24,256,256]{3,2,1,0:T(8,128)} %bitcast.38, f32[2,24,256,256]{3,2,1,0:T(8,128)} %bitcast.39, f32[2,24,256,256]{3,2,1,0:T(8,128)} %bitcast.40, f32[2,24,256,256]{3,2,1,0:T(8,128)} %bitcast.41), custom_call_target="tpu_custom_call" | custom-call | flops 600000000 | bytes 3000000 | tf_op jit(solution)/shard_map/pallas_call | solution.py:110
  42.4 3.5 %shard_map.116.refs_0_.refs_4_.panel_ref = f32[6,32,256]{2,1,0:T(8,128)S(1)} custom-call(s32[48]{0:T(128)S(1)} %fusion.6.place_ref, f32[3,6,64,256]{3,2,1,0:T(8,128)S(1)} %copy-done, bf16[18,256,256]{2,1,0:T(8,128)(2,1)S(1)} %get-tuple-element.62.refs_0_, bf16[18,256,256]{2,1,0:T(8,128)(2,1)S(1)} %get-tuple-element.63.refs_1_, ...), custom_call_target="tpu_custom_call" | custom-call | flops 600000000 | bytes 3000000 | tf_op jit(solution)/shard_map/pallas_call | solution.py:110
  47.4 2.4 %collective-permute-start.37 = (f32[6,32,256]{2,1,0:T(8,128)S(1)}, f32[6,32,256]{2,1,0:T(8,128)S(1)}, u32[]{:S(2)}, u32[]{:S(2)}) collective-permute-start(f32[6,32,256]{2,1,0:T(8,128)S(1)} %shard_map.116.refs_0_.refs_4_.panel_ref), channel_id=1, source_target_pairs={{0,4},{1,5},{2,6},{3,7},{4,0},{5,1},{6,2},{7,3},{8,12},{9,13},{10,... | collective-permute-start | bytes 589832 | tf_op jit(solution)/shard_map/ppermute | solution.py:336
  49.9 3.5 %shard_map.106.refs_0_.refs_4_.panel_ref = f32[6,32,256]{2,1,0:T(8,128)S(1)} custom-call(s32[48]{0:T(128)S(1)} %fusion.6.place_ref, f32[3,6,64,256]{3,2,1,0:T(8,128)S(1)} %copy-done, bf16[18,256,256]{2,1,0:T(8,128)(2,1)S(1)} %get-tuple-element.62.refs_0_, bf16[18,256,256]{2,1,0:T(8,128)(2,1)S(1)} %get-tuple-element.63.refs_1_, ...), custom_call_target="tpu_custom_call" | custom-call | flops 600000000 | bytes 3000000 | tf_op jit(solution)/shard_map/pallas_call | solution.py:110
  54.9 2.5 %collective-permute-start.14 = (f32[6,32,256]{2,1,0:T(8,128)S(1)}, f32[6,32,256]{2,1,0:T(8,128)S(1)}, u32[]{:S(2)}, u32[]{:S(2)}) collective-permute-start(f32[6,32,256]{2,1,0:T(8,128)S(1)} %shard_map.106.refs_0_.refs_4_.panel_ref), channel_id=1, source_target_pairs={{0,4},{1,5},{2,6},{3,7},{4,0},{5,1},{6,2},{7,3},{8,12},{9,13},{10,... | collective-permute-start | bytes 589832 | tf_op jit(solution)/shard_map/ppermute | solution.py:336
  57.9 7.6 %collective-permute-done.16.refs_4_.refs_8_ = f32[6,32,256]{2,1,0:T(8,128)S(1)} collective-permute-done((f32[6,32,256]{2,1,0:T(8,128)S(1)}, f32[6,32,256]{2,1,0:T(8,128)S(1)}, u32[]{:S(2)}, u32[]{:S(2)}) %collective-permute-start.16) | collective-permute-done | bytes 196640 | tf_op jit(solution)/shard_map/ppermute | solution.py:336
  69.4 3.0 %collective-permute-start.43 = (f32[4,32,256]{2,1,0:T(8,128)S(1)}, f32[4,32,256]{2,1,0:T(8,128)S(1)}, u32[]{:S(2)}, u32[]{:S(2)}) collective-permute-start(f32[4,32,256]{2,1,0:T(8,128)S(1)} %get-tuple-element.97), channel_id=1, source_target_pairs={{0,6},{1,7},{2,4},{3,5},{4,2},{5,3},{6,0},{7,1},{8,14},{9,15},{10,... | collective-permute-start | bytes 393224 | tf_op jit(solution)/shard_map/ppermute | solution.py:336
  72.4 3.4 %collective-permute-done.42.refs_11_ = f32[4,32,256]{2,1,0:T(8,128)S(1)} collective-permute-done((f32[4,32,256]{2,1,0:T(8,128)S(1)}, f32[4,32,256]{2,1,0:T(8,128)S(1)}, u32[]{:S(2)}, u32[]{:S(2)}) %collective-permute-start.42) | collective-permute-done | bytes 131104 | tf_op jit(solution)/shard_map/ppermute | solution.py:336
  76.5 4.1 %shard_map.107 = (bf16[24,256,256]{2,1,0:T(8,128)(2,1)S(1)}, bf16[24,256,256]{2,1,0:T(8,128)(2,1)S(1)}) custom-call(f32[2,24,256,256]{3,2,1,0:T(8,128)} %bitcast.42, f32[2,24,256,256]{3,2,1,0:T(8,128)} %bitcast.43, f32[2,24,256,256]{3,2,1,0:T(8,128)} %bitcast.44, f32[2,24,256,256]{3,2,1,0:T(8,128)} %bitcast.45), custom_call_target="tpu_custom_call" | custom-call | flops 600000000 | bytes 3000000 | tf_op jit(solution)/shard_map/pallas_call | solution.py:110
  80.6 3.7 %collective-permute-done.41.refs_10_ = f32[12,32,256]{2,1,0:T(8,128)S(1)} collective-permute-done((f32[12,32,256]{2,1,0:T(8,128)S(1)}, f32[12,32,256]{2,1,0:T(8,128)S(1)}, u32[]{:S(2)}, u32[]{:S(2)}) %collective-permute-start.41) | collective-permute-done | bytes 393248 | tf_op jit(solution)/shard_map/ppermute | solution.py:336
  84.3 6.3 %shard_map.118 = (f32[6,32,256]{2,1,0:T(8,128)S(1)}, f32[36,32,256]{2,1,0:T(8,128)S(1)}, f32[12,32,256]{2,1,0:T(8,128)S(1)}, f32[4,32,256]{2,1,0:T(8,128)S(1)}, f32[4,32,256]{2,1,0:T(8,128)S(1)}) custom-call(s32[48]{0:T(128)S(1)} %fusion.6.place_ref, f32[3,6,64,256]{3,2,1,0:T(8,128)S(1)} %copy-done, bf16[18,256,256]{2,1,0:T(8,128)(2,1)S(1)} %get-tuple-element.62.refs_0_, ...), custom_call_target="tpu_custom_call" | custom-call | flops 600000000 | bytes 3000000 | tf_op jit(solution)/shard_map/pallas_call | solution.py:110
  92.7 6.3 %shard_map.109 = (f32[6,32,256]{2,1,0:T(8,128)S(1)}, f32[36,32,256]{2,1,0:T(8,128)S(1)}, f32[12,32,256]{2,1,0:T(8,128)S(1)}, f32[4,32,256]{2,1,0:T(8,128)S(1)}, f32[4,32,256]{2,1,0:T(8,128)S(1)}) custom-call(s32[48]{0:T(128)S(1)} %fusion.6.place_ref, f32[3,6,64,256]{3,2,1,0:T(8,128)S(1)} %copy-done, bf16[18,256,256]{2,1,0:T(8,128)(2,1)S(1)} %get-tuple-element.62.refs_0_, ...), custom_call_target="tpu_custom_call" | custom-call | flops 600000000 | bytes 3000000 | tf_op jit(solution)/shard_map/pallas_call | solution.py:110
  100.6 2.0 %collective-permute-start.46 = (f32[4,32,256]{2,1,0:T(8,128)S(1)}, f32[4,32,256]{2,1,0:T(8,128)S(1)}, u32[]{:S(2)}, u32[]{:S(2)}) collective-permute-start(f32[4,32,256]{2,1,0:T(8,128)S(1)} %get-tuple-element.101), channel_id=1, source_target_pairs={{0,6},{1,7},{2,4},{3,5},{4,2},{5,3},{6,0},{7,1},{8,14},{9,15},{10,... | collective-permute-start | bytes 393224 | tf_op jit(solution)/shard_map/ppermute | solution.py:336
  102.6 4.4 %collective-permute-done.45.refs_1_ = f32[4,32,256]{2,1,0:T(8,128)S(1)} collective-permute-done((f32[4,32,256]{2,1,0:T(8,128)S(1)}, f32[4,32,256]{2,1,0:T(8,128)S(1)}, u32[]{:S(2)}, u32[]{:S(2)}) %collective-permute-start.45) | collective-permute-done | bytes 131104 | tf_op jit(solution)/shard_map/ppermute | solution.py:336
  107.0 2.7 %collective-permute-done.46.refs_2_ = f32[4,32,256]{2,1,0:T(8,128)S(1)} collective-permute-done((f32[4,32,256]{2,1,0:T(8,128)S(1)}, f32[4,32,256]{2,1,0:T(8,128)S(1)}, u32[]{:S(2)}, u32[]{:S(2)}) %collective-permute-start.46) | collective-permute-done | bytes 131104 | tf_op jit(solution)/shard_map/ppermute | solution.py:336
  120.4 7.4 %collective-permute-done.48.refs_6_ = f32[6,32,256]{2,1,0:T(8,128)S(1)} collective-permute-done((f32[6,32,256]{2,1,0:T(8,128)S(1)}, f32[6,32,256]{2,1,0:T(8,128)S(1)}, u32[]{:S(2)}, u32[]{:S(2)}) %collective-permute-start.48) | collective-permute-done | bytes 196640 | tf_op jit(solution)/shard_map/ppermute | solution.py:336
  128.1 2.8 %shard_map.121 = (f32[6,32,256]{2,1,0:T(8,128)S(1)}, f32[36,32,256]{2,1,0:T(8,128)S(1)}, f32[12,32,256]{2,1,0:T(8,128)S(1)}, f32[4,32,256]{2,1,0:T(8,128)S(1)}, f32[4,32,256]{2,1,0:T(8,128)S(1)}) custom-call(s32[48]{0:T(128)S(1)} %fusion.6.place_ref, f32[6,32,256]{2,1,0:T(8,128)S(1)} %shard_map.116.refs_0_.refs_4_.panel_ref, ...), custom_call_target="tpu_custom_call" | custom-call | flops 600000000 | bytes 3000000 | tf_op jit(solution)/shard_map/pallas_call | solution.py:110
  132.5 3.3 %collective-permute-done.25.refs_6_ = f32[6,32,256]{2,1,0:T(8,128)S(1)} collective-permute-done((f32[6,32,256]{2,1,0:T(8,128)S(1)}, f32[6,32,256]{2,1,0:T(8,128)S(1)}, u32[]{:S(2)}, u32[]{:S(2)}) %collective-permute-start.25) | collective-permute-done | bytes 196640 | tf_op jit(solution)/shard_map/ppermute | solution.py:336
  135.8 2.8 %shard_map.112 = (f32[6,32,256]{2,1,0:T(8,128)S(1)}, f32[36,32,256]{2,1,0:T(8,128)S(1)}, f32[12,32,256]{2,1,0:T(8,128)S(1)}, f32[4,32,256]{2,1,0:T(8,128)S(1)}, f32[4,32,256]{2,1,0:T(8,128)S(1)}) custom-call(s32[48]{0:T(128)S(1)} %fusion.6.place_ref, f32[6,32,256]{2,1,0:T(8,128)S(1)} %shard_map.106.refs_0_.refs_4_.panel_ref, ...), custom_call_target="tpu_custom_call" | custom-call | flops 600000000 | bytes 3000000 | tf_op jit(solution)/shard_map/pallas_call | solution.py:110
  142.4 4.1 %collective-permute-done.51.refs_1_ = f32[4,32,256]{2,1,0:T(8,128)S(1)} collective-permute-done((f32[4,32,256]{2,1,0:T(8,128)S(1)}, f32[4,32,256]{2,1,0:T(8,128)S(1)}, u32[]{:S(2)}, u32[]{:S(2)}) %collective-permute-start.51) | collective-permute-done | bytes 131104 | tf_op jit(solution)/shard_map/ppermute | solution.py:336
  146.6 2.7 %collective-permute-done.52.refs_2_ = f32[4,32,256]{2,1,0:T(8,128)S(1)} collective-permute-done((f32[4,32,256]{2,1,0:T(8,128)S(1)}, f32[4,32,256]{2,1,0:T(8,128)S(1)}, u32[]{:S(2)}, u32[]{:S(2)}) %collective-permute-start.52) | collective-permute-done | bytes 131104 | tf_op jit(solution)/shard_map/ppermute | solution.py:336
  150.2 2.0 %collective-permute-done.28.refs_1_ = f32[4,32,256]{2,1,0:T(8,128)S(1)} collective-permute-done((f32[4,32,256]{2,1,0:T(8,128)S(1)}, f32[4,32,256]{2,1,0:T(8,128)S(1)}, u32[]{:S(2)}, u32[]{:S(2)}) %collective-permute-start.28) | collective-permute-done | bytes 131104 | tf_op jit(solution)/shard_map/ppermute | solution.py:336
  153.8 1.9 %collective-permute-done.27.refs_0_ = f32[12,32,256]{2,1,0:T(8,128)S(1)} collective-permute-done((f32[12,32,256]{2,1,0:T(8,128)S(1)}, f32[12,32,256]{2,1,0:T(8,128)S(1)}, u32[]{:S(2)}, u32[]{:S(2)}) %collective-permute-start.27) | collective-permute-done | bytes 393248 | tf_op jit(solution)/shard_map/ppermute | solution.py:336
  156.7 2.6 %collective-permute-start.55 = (f32[6,32,256]{2,1,0:T(8,128)S(1)}, f32[6,32,256]{2,1,0:T(8,128)S(1)}, u32[]{:S(2)}, u32[]{:S(2)}) collective-permute-start(f32[6,32,256]{2,1,0:T(8,128)S(1)} %get-tuple-element.113), channel_id=1, source_target_pairs={{0,4},{1,5},{2,6},{3,7},{4,0},{5,1},{6,2},{7,3},{8,12},{9,13},{10,... | collective-permute-start | bytes 589832 | tf_op jit(solution)/shard_map/ppermute | solution.py:336
  159.8 2.0 %collective-permute-start.32 = (f32[6,32,256]{2,1,0:T(8,128)S(1)}, f32[6,32,256]{2,1,0:T(8,128)S(1)}, u32[]{:S(2)}, u32[]{:S(2)}) collective-permute-start(f32[6,32,256]{2,1,0:T(8,128)S(1)} %get-tuple-element.92), channel_id=1, source_target_pairs={{0,4},{1,5},{2,6},{3,7},{4,0},{5,1},{6,2},{7,3},{8,12},{9,13},{10,... | collective-permute-start | bytes 589832 | tf_op jit(solution)/shard_map/ppermute | solution.py:336
  162.7 6.1 %collective-permute-done.54.refs_4_ = f32[6,32,256]{2,1,0:T(8,128)S(1)} collective-permute-done((f32[6,32,256]{2,1,0:T(8,128)S(1)}, f32[6,32,256]{2,1,0:T(8,128)S(1)}, u32[]{:S(2)}, u32[]{:S(2)}) %collective-permute-start.54) | collective-permute-done | bytes 196640 | tf_op jit(solution)/shard_map/ppermute | solution.py:336
  170.9 6.2 %collective-permute-done.31.refs_4_ = f32[6,32,256]{2,1,0:T(8,128)S(1)} collective-permute-done((f32[6,32,256]{2,1,0:T(8,128)S(1)}, f32[6,32,256]{2,1,0:T(8,128)S(1)}, u32[]{:S(2)}, u32[]{:S(2)}) %collective-permute-start.31) | collective-permute-done | bytes 196640 | tf_op jit(solution)/shard_map/ppermute | solution.py:336
  (164 shorter events, 58.4 us)
Async XLA Ops:
  1.9 15.0 %collective-permute-start.5 = (f32[6,32,256]{2,1,0:T(8,128)S(1)}, f32[6,32,256]{2,1,0:T(8,128)S(1)}, u32[]{:S(2)}, u32[]{:S(2)}) collective-permute-start(f32[6,32,256]{2,1,0:T(8,128)S(1)} %shard_map.103.refs_0_.refs_4_.panel_ref), channel_id=1, source_target_pairs={{0,8},{1,9},{2,10},{3,11},{4,12},{5,13},{6,14},{7,15},{8,0},{9,1},... | collective-permute-start | bytes 589832 | tf_op jit(solution)/shard_map/ppermute | solution.py:336
  6.0 10.9 %collective-permute-start.3 = (f32[6,32,256]{2,1,0:T(8,128)S(1)}, f32[6,32,256]{2,1,0:T(8,128)S(1)}, u32[]{:S(2)}, u32[]{:S(2)}) collective-permute-start(f32[6,32,256]{2,1,0:T(8,128)S(1)} %shard_map.103.refs_0_.refs_4_.panel_ref), channel_id=1, source_target_pairs={{0,4},{1,5},{2,6},{3,7},{4,0},{5,1},{6,2},{7,3},{8,12},{9,13},{10,... | collective-permute-start | bytes 589832 | tf_op jit(solution)/shard_map/ppermute | solution.py:336
  7.6 10.1 %collective-permute-start.2 = (f32[6,32,256]{2,1,0:T(8,128)S(1)}, f32[6,32,256]{2,1,0:T(8,128)S(1)}, u32[]{:S(2)}, u32[]{:S(2)}) collective-permute-start(f32[6,32,256]{2,1,0:T(8,128)S(1)} %shard_map.103.refs_0_.refs_4_.panel_ref), channel_id=1, source_target_pairs={{0,1},{1,0},{2,3},{3,2},{4,5},{5,4},{6,7},{7,6},{8,9},{9,8},{10,11... | collective-permute-start | bytes 589832 | tf_op jit(solution)/shard_map/ppermute | solution.py:336
  9.5 14.2 %collective-permute-start.8 = (f32[6,32,256]{2,1,0:T(8,128)S(1)}, f32[6,32,256]{2,1,0:T(8,128)S(1)}, u32[]{:S(2)}, u32[]{:S(2)}) collective-permute-start(f32[6,32,256]{2,1,0:T(8,128)S(1)} %shard_map.100.refs_0_.refs_4_.panel_ref), channel_id=1, source_target_pairs={{0,8},{1,9},{2,10},{3,11},{4,12},{5,13},{6,14},{7,15},{8,0},{9,1},... | collective-permute-start | bytes 589832 | tf_op jit(solution)/shard_map/ppermute | solution.py:336
  9.9 14.0 %collective-permute-start.1 = (f32[6,32,256]{2,1,0:T(8,128)S(1)}, f32[6,32,256]{2,1,0:T(8,128)S(1)}, u32[]{:S(2)}, u32[]{:S(2)}) collective-permute-start(f32[6,32,256]{2,1,0:T(8,128)S(1)} %shard_map.100.refs_0_.refs_4_.panel_ref), channel_id=1, source_target_pairs={{0,4},{1,5},{2,6},{3,7},{4,0},{5,1},{6,2},{7,3},{8,12},{9,13},{10,... | collective-permute-start | bytes 589832 | tf_op jit(solution)/shard_map/ppermute | solution.py:336
  17.7 10.2 %collective-permute-start = (f32[6,32,256]{2,1,0:T(8,128)S(1)}, f32[6,32,256]{2,1,0:T(8,128)S(1)}, u32[]{:S(2)}, u32[]{:S(2)}) collective-permute-start(f32[6,32,256]{2,1,0:T(8,128)S(1)} %shard_map.100.refs_0_.refs_4_.panel_ref), channel_id=1, source_target_pairs={{0,1},{1,0},{2,3},{3,2},{4,5},{5,4},{6,7},{7,6},{8,9},{9,8},{10,11... | collective-permute-start | bytes 589832 | tf_op jit(solution)/shard_map/ppermute | solution.py:336
  24.8 17.6 %collective-permute-start.33 = (f32[12,32,256]{2,1,0:T(8,128)S(1)}, f32[12,32,256]{2,1,0:T(8,128)S(1)}, u32[]{:S(2)}, u32[]{:S(2)}) collective-permute-start(f32[12,32,256]{2,1,0:T(8,128)S(1)} %get-tuple-element.66), channel_id=1, source_target_pairs={{0,2},{1,3},{2,0},{3,1},{4,6},{5,7},{6,4},{7,5},{8,10},{9,11},{10,... | collective-permute-start | bytes 1179656 | tf_op jit(solution)/shard_map/ppermute | solution.py:336
  27.9 13.1 %collective-permute-start.35 = (f32[4,32,256]{2,1,0:T(8,128)S(1)}, f32[4,32,256]{2,1,0:T(8,128)S(1)}, u32[]{:S(2)}, u32[]{:S(2)}) collective-permute-start(f32[4,32,256]{2,1,0:T(8,128)S(1)} %get-tuple-element.94), channel_id=1, source_target_pairs={{0,6},{1,7},{2,4},{3,5},{4,2},{5,3},{6,0},{7,1},{8,14},{9,15},{10,... | collective-permute-start | bytes 393224 | tf_op jit(solution)/shard_map/ppermute | solution.py:336
  28.9 21.0 %collective-permute-start.10 = (f32[12,32,256]{2,1,0:T(8,128)S(1)}, f32[12,32,256]{2,1,0:T(8,128)S(1)}, u32[]{:S(2)}, u32[]{:S(2)}) collective-permute-start(f32[12,32,256]{2,1,0:T(8,128)S(1)} %get-tuple-element.69), channel_id=1, source_target_pairs={{0,2},{1,3},{2,0},{3,1},{4,6},{5,7},{6,4},{7,5},{8,10},{9,11},{10,... | collective-permute-start | bytes 1179656 | tf_op jit(solution)/shard_map/ppermute | solution.py:336
  30.6 19.2 %collective-permute-start.11 = (f32[4,32,256]{2,1,0:T(8,128)S(1)}, f32[4,32,256]{2,1,0:T(8,128)S(1)}, u32[]{:S(2)}, u32[]{:S(2)}) collective-permute-start(f32[4,32,256]{2,1,0:T(8,128)S(1)} %get-tuple-element.70), channel_id=1, source_target_pairs={{0,4},{1,5},{2,6},{3,7},{4,0},{5,1},{6,2},{7,3},{8,12},{9,13},{10,... | collective-permute-start | bytes 393224 | tf_op jit(solution)/shard_map/ppermute | solution.py:336
  32.8 17.0 %collective-permute-start.12 = (f32[4,32,256]{2,1,0:T(8,128)S(1)}, f32[4,32,256]{2,1,0:T(8,128)S(1)}, u32[]{:S(2)}, u32[]{:S(2)}) collective-permute-start(f32[4,32,256]{2,1,0:T(8,128)S(1)} %get-tuple-element.71), channel_id=1, source_target_pairs={{0,6},{1,7},{2,4},{3,5},{4,2},{5,3},{6,0},{7,1},{8,14},{9,15},{10,... | collective-permute-start | bytes 393224 | tf_op jit(solution)/shard_map/ppermute | solution.py:336
  45.9 11.4 %collective-permute-start.39 = (f32[6,32,256]{2,1,0:T(8,128)S(1)}, f32[6,32,256]{2,1,0:T(8,128)S(1)}, u32[]{:S(2)}, u32[]{:S(2)}) collective-permute-start(f32[6,32,256]{2,1,0:T(8,128)S(1)} %shard_map.116.refs_0_.refs_4_.panel_ref), channel_id=1, source_target_pairs={{0,8},{1,9},{2,10},{3,11},{4,12},{5,13},{6,14},{7,15},{8,0},{9,1},... | collective-permute-start | bytes 589832 | tf_op jit(solution)/shard_map/ppermute | solution.py:336
  53.4 12.1 %collective-permute-start.16 = (f32[6,32,256]{2,1,0:T(8,128)S(1)}, f32[6,32,256]{2,1,0:T(8,128)S(1)}, u32[]{:S(2)}, u32[]{:S(2)}) collective-permute-start(f32[6,32,256]{2,1,0:T(8,128)S(1)} %shard_map.106.refs_0_.refs_4_.panel_ref), channel_id=1, source_target_pairs={{0,8},{1,9},{2,10},{3,11},{4,12},{5,13},{6,14},{7,15},{8,0},{9,1},... | collective-permute-start | bytes 589832 | tf_op jit(solution)/shard_map/ppermute | solution.py:336
  54.9 10.7 %collective-permute-start.14 = (f32[6,32,256]{2,1,0:T(8,128)S(1)}, f32[6,32,256]{2,1,0:T(8,128)S(1)}, u32[]{:S(2)}, u32[]{:S(2)}) collective-permute-start(f32[6,32,256]{2,1,0:T(8,128)S(1)} %shard_map.106.refs_0_.refs_4_.panel_ref), channel_id=1, source_target_pairs={{0,4},{1,5},{2,6},{3,7},{4,0},{5,1},{6,2},{7,3},{8,12},{9,13},{10,... | collective-permute-start | bytes 589832 | tf_op jit(solution)/shard_map/ppermute | solution.py:336
  57.8 10.4 %collective-permute-start.13 = (f32[6,32,256]{2,1,0:T(8,128)S(1)}, f32[6,32,256]{2,1,0:T(8,128)S(1)}, u32[]{:S(2)}, u32[]{:S(2)}) collective-permute-start(f32[6,32,256]{2,1,0:T(8,128)S(1)} %shard_map.106.refs_0_.refs_4_.panel_ref), channel_id=1, source_target_pairs={{0,1},{1,0},{2,3},{3,2},{4,5},{5,4},{6,7},{7,6},{8,9},{9,8},{10,11... | collective-permute-start | bytes 589832 | tf_op jit(solution)/shard_map/ppermute | solution.py:336
  66.7 17.7 %collective-permute-start.41 = (f32[12,32,256]{2,1,0:T(8,128)S(1)}, f32[12,32,256]{2,1,0:T(8,128)S(1)}, u32[]{:S(2)}, u32[]{:S(2)}) collective-permute-start(f32[12,32,256]{2,1,0:T(8,128)S(1)} %get-tuple-element.95), channel_id=1, source_target_pairs={{0,2},{1,3},{2,0},{3,1},{4,6},{5,7},{6,4},{7,5},{8,10},{9,11},{10,... | collective-permute-start | bytes 1179656 | tf_op jit(solution)/shard_map/ppermute | solution.py:336
  68.8 23.9 %collective-permute-start.18 = (f32[12,32,256]{2,1,0:T(8,128)S(1)}, f32[12,32,256]{2,1,0:T(8,128)S(1)}, u32[]{:S(2)}, u32[]{:S(2)}) collective-permute-start(f32[12,32,256]{2,1,0:T(8,128)S(1)} %get-tuple-element.74), channel_id=1, source_target_pairs={{0,2},{1,3},{2,0},{3,1},{4,6},{5,7},{6,4},{7,5},{8,10},{9,11},{10,... | collective-permute-start | bytes 1179656 | tf_op jit(solution)/shard_map/ppermute | solution.py:336
  69.4 11.2 %collective-permute-start.43 = (f32[4,32,256]{2,1,0:T(8,128)S(1)}, f32[4,32,256]{2,1,0:T(8,128)S(1)}, u32[]{:S(2)}, u32[]{:S(2)}) collective-permute-start(f32[4,32,256]{2,1,0:T(8,128)S(1)} %get-tuple-element.97), channel_id=1, source_target_pairs={{0,6},{1,7},{2,4},{3,5},{4,2},{5,3},{6,0},{7,1},{8,14},{9,15},{10,... | collective-permute-start | bytes 393224 | tf_op jit(solution)/shard_map/ppermute | solution.py:336
  72.4 19.8 %collective-permute-start.19 = (f32[4,32,256]{2,1,0:T(8,128)S(1)}, f32[4,32,256]{2,1,0:T(8,128)S(1)}, u32[]{:S(2)}, u32[]{:S(2)}) collective-permute-start(f32[4,32,256]{2,1,0:T(8,128)S(1)} %get-tuple-element.75), channel_id=1, source_target_pairs={{0,4},{1,5},{2,6},{3,7},{4,0},{5,1},{6,2},{7,3},{8,12},{9,13},{10,... | collective-permute-start | bytes 393224 | tf_op jit(solution)/shard_map/ppermute | solution.py:336
  75.8 16.3 %collective-permute-start.20 = (f32[4,32,256]{2,1,0:T(8,128)S(1)}, f32[4,32,256]{2,1,0:T(8,128)S(1)}, u32[]{:S(2)}, u32[]{:S(2)}) collective-permute-start(f32[4,32,256]{2,1,0:T(8,128)S(1)} %get-tuple-element.76), channel_id=1, source_target_pairs={{0,6},{1,7},{2,4},{3,5},{4,2},{5,3},{6,0},{7,1},{8,14},{9,15},{10,... | collective-permute-start | bytes 393224 | tf_op jit(solution)/shard_map/ppermute | solution.py:336
  90.6 19.2 %collective-permute-start.44 = (f32[12,32,256]{2,1,0:T(8,128)S(1)}, f32[12,32,256]{2,1,0:T(8,128)S(1)}, u32[]{:S(2)}, u32[]{:S(2)}) collective-permute-start(f32[12,32,256]{2,1,0:T(8,128)S(1)} %get-tuple-element.99), channel_id=1, source_target_pairs={{0,2},{1,3},{2,0},{3,1},{4,6},{5,7},{6,4},{7,5},{8,10},{9,11},{10,... | collective-permute-start | bytes 1179656 | tf_op jit(solution)/shard_map/ppermute | solution.py:336
  99.0 15.3 %collective-permute-start.21 = (f32[12,32,256]{2,1,0:T(8,128)S(1)}, f32[12,32,256]{2,1,0:T(8,128)S(1)}, u32[]{:S(2)}, u32[]{:S(2)}) collective-permute-start(f32[12,32,256]{2,1,0:T(8,128)S(1)} %get-tuple-element.78), channel_id=1, source_target_pairs={{0,2},{1,3},{2,0},{3,1},{4,6},{5,7},{6,4},{7,5},{8,10},{9,11},{10,... | collective-permute-start | bytes 1179656 | tf_op jit(solution)/shard_map/ppermute | solution.py:336
  115.3 12.6 %collective-permute-start.48 = (f32[6,32,256]{2,1,0:T(8,128)S(1)}, f32[6,32,256]{2,1,0:T(8,128)S(1)}, u32[]{:S(2)}, u32[]{:S(2)}) collective-permute-start(f32[6,32,256]{2,1,0:T(8,128)S(1)} %get-tuple-element.104), channel_id=1, source_target_pairs={{0,8},{1,9},{2,10},{3,11},{4,12},{5,13},{6,14},{7,15},{8,0},{9,1},... | collective-permute-start | bytes 589832 | tf_op jit(solution)/shard_map/ppermute | solution.py:336
  116.1 12.0 %collective-permute-start.49 = (f32[6,32,256]{2,1,0:T(8,128)S(1)}, f32[6,32,256]{2,1,0:T(8,128)S(1)}, u32[]{:S(2)}, u32[]{:S(2)}) collective-permute-start(f32[6,32,256]{2,1,0:T(8,128)S(1)} %get-tuple-element.105), channel_id=1, source_target_pairs={{0,4},{1,5},{2,6},{3,7},{4,0},{5,1},{6,2},{7,3},{8,12},{9,13},{10,... | collective-permute-start | bytes 589832 | tf_op jit(solution)/shard_map/ppermute | solution.py:336
  117.7 18.1 %collective-permute-start.25 = (f32[6,32,256]{2,1,0:T(8,128)S(1)}, f32[6,32,256]{2,1,0:T(8,128)S(1)}, u32[]{:S(2)}, u32[]{:S(2)}) collective-permute-start(f32[6,32,256]{2,1,0:T(8,128)S(1)} %get-tuple-element.83), channel_id=1, source_target_pairs={{0,8},{1,9},{2,10},{3,11},{4,12},{5,13},{6,14},{7,15},{8,0},{9,1},... | collective-permute-start | bytes 589832 | tf_op jit(solution)/shard_map/ppermute | solution.py:336
  118.5 17.3 %collective-permute-start.26 = (f32[6,32,256]{2,1,0:T(8,128)S(1)}, f32[6,32,256]{2,1,0:T(8,128)S(1)}, u32[]{:S(2)}, u32[]{:S(2)}) collective-permute-start(f32[6,32,256]{2,1,0:T(8,128)S(1)} %get-tuple-element.84), channel_id=1, source_target_pairs={{0,4},{1,5},{2,6},{3,7},{4,0},{5,1},{6,2},{7,3},{8,12},{9,13},{10,... | collective-permute-start | bytes 589832 | tf_op jit(solution)/shard_map/ppermute | solution.py:336
  130.9 18.4 %collective-permute-start.50 = (f32[12,32,256]{2,1,0:T(8,128)S(1)}, f32[12,32,256]{2,1,0:T(8,128)S(1)}, u32[]{:S(2)}, u32[]{:S(2)}) collective-permute-start(f32[12,32,256]{2,1,0:T(8,128)S(1)} %get-tuple-element.107), channel_id=1, source_target_pairs={{0,2},{1,3},{2,0},{3,1},{4,6},{5,7},{6,4},{7,5},{8,10},{9,11},{10,... | collective-permute-start | bytes 1179656 | tf_op jit(solution)/shard_map/ppermute | solution.py:336
  138.6 17.1 %collective-permute-start.27 = (f32[12,32,256]{2,1,0:T(8,128)S(1)}, f32[12,32,256]{2,1,0:T(8,128)S(1)}, u32[]{:S(2)}, u32[]{:S(2)}) collective-permute-start(f32[12,32,256]{2,1,0:T(8,128)S(1)} %get-tuple-element.86), channel_id=1, source_target_pairs={{0,2},{1,3},{2,0},{3,1},{4,6},{5,7},{6,4},{7,5},{8,10},{9,11},{10,... | collective-permute-start | bytes 1179656 | tf_op jit(solution)/shard_map/ppermute | solution.py:336
  156.6 12.2 %collective-permute-start.54 = (f32[6,32,256]{2,1,0:T(8,128)S(1)}, f32[6,32,256]{2,1,0:T(8,128)S(1)}, u32[]{:S(2)}, u32[]{:S(2)}) collective-permute-start(f32[6,32,256]{2,1,0:T(8,128)S(1)} %get-tuple-element.112), channel_id=1, source_target_pairs={{0,8},{1,9},{2,10},{3,11},{4,12},{5,13},{6,14},{7,15},{8,0},{9,1},... | collective-permute-start | bytes 589832 | tf_op jit(solution)/shard_map/ppermute | solution.py:336
  156.7 12.6 %collective-permute-start.55 = (f32[6,32,256]{2,1,0:T(8,128)S(1)}, f32[6,32,256]{2,1,0:T(8,128)S(1)}, u32[]{:S(2)}, u32[]{:S(2)}) collective-permute-start(f32[6,32,256]{2,1,0:T(8,128)S(1)} %get-tuple-element.113), channel_id=1, source_target_pairs={{0,4},{1,5},{2,6},{3,7},{4,0},{5,1},{6,2},{7,3},{8,12},{9,13},{10,... | collective-permute-start | bytes 589832 | tf_op jit(solution)/shard_map/ppermute | solution.py:336
  159.4 17.7 %collective-permute-start.31 = (f32[6,32,256]{2,1,0:T(8,128)S(1)}, f32[6,32,256]{2,1,0:T(8,128)S(1)}, u32[]{:S(2)}, u32[]{:S(2)}) collective-permute-start(f32[6,32,256]{2,1,0:T(8,128)S(1)} %get-tuple-element.91), channel_id=1, source_target_pairs={{0,8},{1,9},{2,10},{3,11},{4,12},{5,13},{6,14},{7,15},{8,0},{9,1},... | collective-permute-start | bytes 589832 | tf_op jit(solution)/shard_map/ppermute | solution.py:336
  159.8 17.5 %collective-permute-start.32 = (f32[6,32,256]{2,1,0:T(8,128)S(1)}, f32[6,32,256]{2,1,0:T(8,128)S(1)}, u32[]{:S(2)}, u32[]{:S(2)}) collective-permute-start(f32[6,32,256]{2,1,0:T(8,128)S(1)} %get-tuple-element.92), channel_id=1, source_target_pairs={{0,4},{1,5},{2,6},{3,7},{4,0},{5,1},{6,2},{7,3},{8,12},{9,13},{10,... | collective-permute-start | bytes 589832 | tf_op jit(solution)/shard_map/ppermute | solution.py:336
  (29 other events, 198.4 us)
